TPU v7x, 32 devices: a whole 2x2x4 slice. The times are simulated.
32 devices in a mesh: pp: 2 (over x), ep: 16 (over z, y, core).
Axes of the slice: x: 2, y: 2, z: 4, core: 2. Of those that a mesh axis runs over, the one named last changes fastest.
Arguments:
- fwd_act: bfloat16 [2, 1024, 3584], P('pp', 'ep'), may hold values from -6 to 6
- fwd_route: int32 [2, 1024, 1], P('pp', 'ep'), may hold values from 0 to 1, as said below
- fwd_gate: float32 [2, 1024, 1], P('pp', 'ep'), may hold values from 0.25 to 2
- bwd_act: bfloat16 [2, 1024, 3584], P('pp', 'ep'), may hold values from -6 to 6
- bwd_grad: bfloat16 [2, 1024, 3584], P('pp', 'ep'), may hold values from -6 to 6
- bwd_route: int32 [2, 1024, 1], P('pp', 'ep'), may hold values from 0 to 1, as said below
- bwd_gate: float32 [2, 1024, 1], P('pp', 'ep'), may hold values from 0.25 to 2
- norm_gain: float32 [2, 3584], P('pp'), may hold values from 0.25 to 1.75
- w_gate: bfloat16 [2, 16, 1792, 256], P('pp', 'ep'), may hold values from -0.09375 to 0.09375
- w_up: bfloat16 [2, 16, 1792, 256], P('pp', 'ep'), may hold values from -0.09375 to 0.09375
- w_down: bfloat16 [2, 16, 256, 1792], P('pp', 'ep'), may hold values from -0.1875 to 0.1875
Outputs:
- fwd_next: bfloat16 [2, 1024, 3584], P('pp', 'ep')
- bwd_next: bfloat16 [2, 1024, 3584], P('pp', 'ep')
Inputs may be any that keep to these rules, and one draw needn't show every extreme that they name: `fwd_route`: among the 64 rows of one device, no expert is named more than 40 times; at each section one expert is named exactly 40 times in every device's rows. `bwd_route`: as fwd_route, drawn independently.
All inputs are finite; a program needn't handle non-finite values.
Results may differ from a plain program's by a relative error of at most 0.011.
Values may be sent and summed in bfloat16 or wider, within the bound.
No kernel may reach another device: no remote copies, remote signals or barrier semaphores. Data moves between devices by JAX's collectives and lax.ppermute only.
A program may use at most 128 MiB of HBM per device.

v0:
```python
import jax
import jax.numpy as jnp
from jax import lax
from jax.sharding import PartitionSpec as P

SLICES = 8


def from_partner(value, axis, stride):
    return lax.ppermute(value, axis, [(i, i ^ 1 << stride) for i in range(lax.axis_size(axis))])


def from_behind(value, axis, steps):
    count = lax.axis_size(axis)
    pairs = [(source, (source + steps) % count) for source in range(count)]
    return lax.ppermute(value, axis, pairs)


def normalize(values, norm_scale):
    widened = values.astype(jnp.float32)
    inverse = lax.rsqrt(jnp.mean(widened * widened, axis=-1, keepdims=True) + 1e-06)
    return ((widened * inverse * norm_scale).astype(jnp.bfloat16), inverse)


def slot_plan(route_ids, experts, capacity):
    chosen = route_ids[:, 0]
    onehot = (chosen[:, None] == jnp.arange(experts, dtype=jnp.int32)[None, :]).astype(jnp.int32)
    running = jnp.cumsum(onehot, axis=0) - 1
    position = jnp.sum(running * onehot, axis=1)
    target = chosen * capacity + position
    chooser = (jnp.arange(experts * capacity, dtype=jnp.int32)[:, None] == target[None, :]).astype(
        jnp.bfloat16
    )
    return (target, chooser)


def lay_out(chooser, members, experts, capacity):
    half_width = members[0].shape[1] // 2
    pieces = []
    for half in range(2):
        for member in members:
            columns = member[:, half * half_width : (half + 1) * half_width]
            placed = jnp.dot(chooser, columns, preferred_element_type=jnp.float32).astype(
                jnp.bfloat16
            )
            pieces.append(placed.reshape(experts, capacity * half_width))
    stacked = jnp.stack(pieces, axis=1)
    return stacked.reshape(experts, 2, len(members) * capacity * half_width)


def send_rows(placed, count, capacity, half_width):
    experts = placed.shape[0]
    blocks = SLICES // 2
    length = placed.shape[2]
    half_slots = capacity // 2
    shaped = placed.reshape(experts, 2, count, capacity, half_width)
    pieces = [
        shaped[
            :, :, :, hidden_block % 2 * half_slots : (hidden_block % 2 + 1) * half_slots
        ].reshape(experts, 2, length // 2)
        for hidden_block in range(blocks)
    ]
    outgoing = jnp.stack(pieces, axis=1).reshape(-1, length // 2)
    arrived = lax.all_to_all(outgoing, "ep", split_axis=0, concat_axis=0, tiled=True)
    partner = from_partner(arrived, "ep", 1)
    odd_block = lax.axis_index("ep") // 2 % 2 == 1
    lower_part = jnp.where(odd_block, partner, arrived).reshape(-1, count, half_slots, half_width)
    upper_part = jnp.where(odd_block, arrived, partner).reshape(-1, count, half_slots, half_width)
    return jnp.concatenate([lower_part, upper_part], axis=2).reshape(-1, length)


def member_rows(arrived, member, count, half_width):
    senders = arrived.shape[0]
    return arrived.reshape(senders, count, -1)[:, member].reshape(-1, half_width)


def pair_sum(stacked):
    return stacked + from_partner(stacked.astype(jnp.bfloat16), "ep", 0).astype(stacked.dtype)


def return_rows(results):
    return lax.all_to_all(results, "ep", split_axis=0, concat_axis=0, tiled=True)


def gather_back(returned, target, experts, capacity, half_width):
    summed = (
        returned.reshape(experts, SLICES // 2, 2, capacity * half_width)
        .astype(jnp.float32)
        .sum(axis=1)
    )
    halves = [
        jnp.take(summed[:, half].reshape(experts * capacity, half_width), target, axis=0)
        for half in range(2)
    ]
    return jnp.concatenate(halves, axis=1)


def body(
    fwd_act,
    fwd_route,
    fwd_gate,
    bwd_act,
    bwd_grad,
    bwd_route,
    bwd_gate,
    norm_gain,
    w_gate,
    w_up,
    w_down,
):
    senders = lax.axis_size("ep")
    experts = senders // SLICES
    tokens_here = fwd_act.shape[1]
    capacity = 2 * ((5 * tokens_here + 8 * experts - 1) // (8 * experts))
    norm_scale = norm_gain[0]
    gate_weight = w_gate[0, 0]
    up_weight = w_up[0, 0]
    down_weight = w_down[0, 0]
    half_width = gate_weight.shape[0]
    contract = (((1,), (1,)), ((), ()))
    fwd_rows = fwd_act[0]
    fwd_normed, fwd_inverse = normalize(fwd_rows, norm_scale)
    fwd_target, fwd_chooser = slot_plan(fwd_route[0], experts, capacity)
    fwd_arrived = send_rows(
        lay_out(fwd_chooser, (fwd_normed,), experts, capacity), 1, capacity, half_width
    )
    fwd_inputs = member_rows(fwd_arrived, 0, 1, half_width)
    fwd_pre = pair_sum(
        jnp.stack(
            [
                jnp.dot(fwd_inputs, gate_weight, preferred_element_type=jnp.float32),
                jnp.dot(fwd_inputs, up_weight, preferred_element_type=jnp.float32),
            ]
        )
    )
    hidden = (jax.nn.silu(fwd_pre[0]) * fwd_pre[1]).astype(jnp.bfloat16)
    fwd_partial = jnp.dot(hidden, down_weight, preferred_element_type=jnp.float32).astype(
        jnp.bfloat16
    )
    fwd_returned = return_rows(fwd_partial.reshape(senders, capacity * half_width))
    fwd_mixed = gather_back(fwd_returned, fwd_target, experts, capacity, half_width)
    fwd_result = (fwd_rows.astype(jnp.float32) + fwd_gate[0] * fwd_mixed).astype(jnp.bfloat16)
    fwd_next = from_behind(fwd_result, "pp", 1)
    bwd_rows = bwd_act[0]
    bwd_normed, bwd_inverse = normalize(bwd_rows, norm_scale)
    weighted = (bwd_gate[0] * bwd_grad[0].astype(jnp.float32)).astype(jnp.bfloat16)
    bwd_target, bwd_chooser = slot_plan(bwd_route[0], experts, capacity)
    bwd_arrived = send_rows(
        lay_out(bwd_chooser, (bwd_normed, weighted), experts, capacity), 2, capacity, half_width
    )
    bwd_inputs = member_rows(bwd_arrived, 0, 2, half_width)
    grad_inputs = member_rows(bwd_arrived, 1, 2, half_width)
    bwd_pre = pair_sum(
        jnp.stack(
            [
                jnp.dot(bwd_inputs, gate_weight, preferred_element_type=jnp.float32),
                jnp.dot(bwd_inputs, up_weight, preferred_element_type=jnp.float32),
                lax.dot_general(
                    grad_inputs, down_weight, contract, preferred_element_type=jnp.float32
                ),
            ]
        )
    )
    logistic = jax.nn.sigmoid(bwd_pre[0])
    d_gate = (bwd_pre[2] * bwd_pre[1] * logistic * (1.0 + bwd_pre[0] * (1.0 - logistic))).astype(
        jnp.bfloat16
    )
    d_up = (bwd_pre[2] * bwd_pre[0] * logistic).astype(jnp.bfloat16)
    d_partial = (
        lax.dot_general(d_gate, gate_weight, contract, preferred_element_type=jnp.float32)
        + lax.dot_general(d_up, up_weight, contract, preferred_element_type=jnp.float32)
    ).astype(jnp.bfloat16)
    bwd_returned = return_rows(d_partial.reshape(senders, capacity * half_width))
    d_normed = gather_back(bwd_returned, bwd_target, experts, capacity, half_width)
    scaled = norm_scale * d_normed
    widened = bwd_rows.astype(jnp.float32)
    cubed = bwd_inverse * bwd_inverse * bwd_inverse
    d_rows = (
        bwd_grad[0].astype(jnp.float32)
        + scaled * bwd_inverse
        - widened * cubed * jnp.mean(scaled * widened, axis=-1, keepdims=True)
    )
    bwd_next = from_behind(d_rows.astype(jnp.bfloat16), "pp", -1)
    return (fwd_next[None], bwd_next[None])


def solution(mesh):
    in_specs = (
        P("pp", "ep", None),
        P("pp", "ep", None),
        P("pp", "ep", None),
        P("pp", "ep", None),
        P("pp", "ep", None),
        P("pp", "ep", None),
        P("pp", "ep", None),
        P("pp", None),
        P("pp", "ep", None, None),
        P("pp", "ep", None, None),
        P("pp", "ep", None, None),
    )
    out_specs = (P("pp", "ep", None), P("pp", "ep", None))
    return jax.shard_map(body, mesh=mesh, in_specs=in_specs, out_specs=out_specs, check_vma=False)
```

profile of v0, /device:TPU:0, one launch (start us, length us, event | category | flops | bytes accessed | tf_op | source)
XLA Modules:
  0.0 708.4 jit_solution(2498123310328379021)
XLA Ops:
  22.6 27.6 %reduce.17 = bf16[16,71680]{1,0:T(8,128)(2,1)S(1)} reduce(bf16[16,1,71680]{2,1,0:T(2,128)(2,1)} %all_to_all.40, bf16[]{:T(256)} %broadcast.119), dimensions={1}, to_apply=%all_to_all.40.reduce_sub_computation | reduce | bytes 4587522 | tf_op jit(solution)/shard_map/all_to_all | solution.py:64
  53.1 60.7 %all_to_all.46 = bf16[16,2,35840]{2,1,0:T(2,128)(2,1)S(1)} all-to-all(bf16[16,2,35840]{2,1,0:T(2,128)(2,1)} %reshape.173), channel_id=1, replica_groups=mesh['pp'=2,'ep'=16] {'ep'}, dimensions={0} | all-to-all | bytes 4587520 | tf_op jit(solution)/shard_map/all_to_all | solution.py:64
  113.8 6.7 reshape.174
  125.0 51.7 %collective-permute-done.3 = bf16[16,71680]{1,0:T(8,128)(2,1)} collective-permute-done((bf16[16,71680]{1,0:T(8,128)(2,1)S(1)}, bf16[16,71680]{1,0:T(8,128)(2,1)}, u32[]{:S(2)}, u32[]{:S(2)}) %collective-permute-start.3) | collective-permute-done | bytes 2293792 | tf_op jit(solution)/shard_map/ppermute | solution.py:10
  176.7 5.8 broadcast_select_fusion.1
  189.3 6.0 pad_maximum_fusion
  195.3 10.6 %reshape_reshape.8 = bf16[16,2,71680]{2,1,0:T(2,128)(2,1)} reshape(bf16[16,2,40,1792]{3,2,1,0:T(8,128)(2,1)} %pad_maximum_fusion) | data formatting | bytes 9175040 | tf_op jit(solution)/shard_map/reshape;reshape | solution.py:74
  205.9 44.8 %slice_reduce_fusion.1 = (bf16[16,71680]{1,0:T(8,128)(2,1)S(1)}, bf16[16,71680]{1,0:T(8,128)(2,1)}) fusion(bf16[16,2,71680]{2,1,0:T(2,128)(2,1)} %reshape_reshape.8), kind=kLoop, calls=%fused_computation.5 | loop fusion | bytes 9175040 | tf_op jit(solution)/shard_map/slice | solution.py:74
  266.3 6.3 all_to_all.41
  272.5 27.6 %reduce.18 = bf16[16,71680]{1,0:T(8,128)(2,1)S(1)} reduce(bf16[16,1,71680]{2,1,0:T(2,128)(2,1)} %all_to_all.41, bf16[]{:T(256)} %broadcast.119), dimensions={1}, to_apply=%all_to_all.41.reduce_sub_computation | reduce | bytes 4587522 | tf_op jit(solution)/shard_map/all_to_all | solution.py:82
  307.3 44.1 %all-to-all-done.3 = bf16[16,2,35840]{2,1,0:T(2,128)(2,1)S(1)} async-done(((bf16[16,2,35840]{2,1,0:T(2,128)(2,1)}), bf16[16,2,35840]{2,1,0:T(2,128)(2,1)S(1)}, u32[]{:S(2)}, u32[]{:S(2)}) %all-to-all-start.3) | async-done | bytes 2293792 | tf_op jit(solution)/shard_map/all_to_all | solution.py:82
  351.4 6.8 reshape.176
  358.2 50.5 %convert_reduce_fusion = f32[16,71680]{1,0:T(8,128)} fusion(bf16[16,1,71680]{2,1,0:T(2,128)(2,1)} %reshape.176), kind=kLoop, calls=%fused_computation.7 | loop fusion | flops 1146880 | bytes 6881280 | tf_op jit(solution)/shard_map/convert_element_type | solution.py:88
  408.7 6.0 reshape.113
  436.6 8.6 %reduce.19 = bf16[16,35840]{1,0:T(8,128)(2,1)} reduce(bf16[16,1,35840]{2,1,0:T(2,128)(2,1)S(1)} %all_to_all.38, bf16[]{:T(256)} %broadcast.119), dimensions={1}, to_apply=%all_to_all.38.reduce_sub_computation | reduce | bytes 2293762 | tf_op jit(solution)/shard_map/all_to_all | solution.py:64
  447.2 41.1 %all_to_all.47 = bf16[16,2,17920]{2,1,0:T(2,128)(2,1)} all-to-all(bf16[16,2,17920]{2,1,0:T(2,128)(2,1)S(1)} %reshape.169), channel_id=1, replica_groups=mesh['pp'=2,'ep'=16] {'ep'}, dimensions={0} | all-to-all | bytes 2293760 | tf_op jit(solution)/shard_map/all_to_all | solution.py:64
  493.7 26.6 %collective-permute-done = bf16[16,35840]{1,0:T(8,128)(2,1)S(1)} collective-permute-done((bf16[16,35840]{1,0:T(8,128)(2,1)S(1)}, bf16[16,35840]{1,0:T(8,128)(2,1)S(1)}, u32[]{:S(2)}, u32[]{:S(2)}) %collective-permute-start) | collective-permute-done | bytes 1146912 | tf_op jit(solution)/shard_map/ppermute | solution.py:10
  532.7 6.3 all_to_all.39
  538.9 27.6 %reduce.20 = bf16[16,71680]{1,0:T(8,128)(2,1)S(1)} reduce(bf16[16,1,71680]{2,1,0:T(2,128)(2,1)} %all_to_all.39, bf16[]{:T(256)} %broadcast.119), dimensions={1}, to_apply=%all_to_all.39.reduce_sub_computation | reduce | bytes 4587522 | tf_op jit(solution)/shard_map/all_to_all | solution.py:82
  575.0 42.8 %all-to-all-done.1 = bf16[16,2,35840]{2,1,0:T(2,128)(2,1)S(1)} async-done(((bf16[16,2,35840]{2,1,0:T(2,128)(2,1)}), bf16[16,2,35840]{2,1,0:T(2,128)(2,1)S(1)}, u32[]{:S(2)}, u32[]{:S(2)}) %all-to-all-start.1) | async-done | bytes 2293792 | tf_op jit(solution)/shard_map/all_to_all | solution.py:82
  617.8 6.8 reshape.172
  624.6 50.5 %convert_reduce_fusion.1 = f32[16,71680]{1,0:T(8,128)} fusion(bf16[16,1,71680]{2,1,0:T(2,128)(2,1)} %reshape.172), kind=kLoop, calls=%fused_computation.8 | loop fusion | flops 1146880 | bytes 6881280 | tf_op jit(solution)/shard_map/convert_element_type | solution.py:88
  675.1 6.1 reshape.110
  693.8 11.7 %collective-permute-done.2 = bf16[64,3584]{1,0:T(8,128)(2,1)S(1)} collective-permute-done((bf16[64,3584]{1,0:T(8,128)(2,1)S(1)}, bf16[64,3584]{1,0:T(8,128)(2,1)S(1)}, u32[]{:S(2)}, u32[]{:S(2)}) %collective-permute-start.2) | collective-permute-done | bytes 458784 | tf_op jit(solution)/shard_map/ppermute | solution.py:16
  (135 shorter events, 123.6 us)
Async XLA Ops:
  0.6 255.5 %copy-start = (bf16[1,1,1792,256]{3,2,1,0:T(8,128)(2,1)S(1)}, bf16[1,1,1792,256]{3,2,1,0:T(8,128)(2,1)}, u32[]{:S(2)}) copy-start(bf16[1,1,1792,256]{3,2,1,0:T(8,128)(2,1)} %param.22) | copy-start | bytes 2752516
  0.6 7.3 %copy-start.12 = (f32[1,64,1]{1,2,0:T(1,128)S(1)}, f32[1,64,1]{1,2,0:T(1,128)}, u32[]{:S(2)}) copy-start(f32[1,64,1]{1,2,0:T(1,128)} %param.19) | copy-start | bytes 772
  0.7 7.3 %copy-start.7 = (bf16[1,64,3584]{2,1,0:T(8,128)(2,1)S(1)}, bf16[1,64,3584]{2,1,0:T(8,128)(2,1)}, u32[]{:S(2)}) copy-start(bf16[1,64,3584]{2,1,0:T(8,128)(2,1)} %param.17) | copy-start | bytes 1376260
  124.1 52.6 %collective-permute-start.3 = (bf16[16,71680]{1,0:T(8,128)(2,1)S(1)}, bf16[16,71680]{1,0:T(8,128)(2,1)}, u32[]{:S(2)}, u32[]{:S(2)}) collective-permute-start(bf16[16,71680]{1,0:T(8,128)(2,1)S(1)} %bitcast.95), channel_id=1, source_target_pairs={{0,2},{1,3},{2,0},{3,1},{4,6},{5,7},{6,4},{7,5},{8,10},{9,11},{10,... | collective-permute-start | bytes 6881288 | tf_op jit(solution)/shard_map/ppermute | solution.py:10
  256.2 2.6 copy-start.6
  256.2 2.6 copy-start.9
  258.8 1.6 copy-start.5
  258.8 1.9 copy-start.14
  261.6 2.6 collective-permute-start.4
  303.1 3.9 copy-start.11
  303.1 48.3 %all-to-all-start.3 = ((bf16[16,2,35840]{2,1,0:T(2,128)(2,1)}), bf16[16,2,35840]{2,1,0:T(2,128)(2,1)S(1)}, u32[]{:S(2)}, u32[]{:S(2)}) async-start(bf16[16,2,35840]{2,1,0:T(2,128)(2,1)} %reshape.175), calls=%async_computation.3 | async-start | bytes 4587520 | tf_op jit(solution)/shard_map/all_to_all | solution.py:82
  424.6 1.0 copy-start.1
  425.3 1.1 copy-start.3
  425.3 1.2 copy-start.8
  493.0 27.4 %collective-permute-start = (bf16[16,35840]{1,0:T(8,128)(2,1)S(1)}, bf16[16,35840]{1,0:T(8,128)(2,1)S(1)}, u32[]{:S(2)}, u32[]{:S(2)}) collective-permute-start(bf16[16,35840]{1,0:T(8,128)(2,1)S(1)} %bitcast.98), channel_id=1, source_target_pairs={{0,2},{1,3},{2,0},{3,1},{4,6},{5,7},{6,4},{7,5},{8,10},{9,11},{10,... | collective-permute-start | bytes 3440648 | tf_op jit(solution)/shard_map/ppermute | solution.py:10
  522.1 1.9 copy-start.2
  527.5 1.2 copy-start.10
  529.4 2.4 copy-start.15
  529.5 2.2 collective-permute-start.1
  569.5 48.4 %all-to-all-start.1 = ((bf16[16,2,35840]{2,1,0:T(2,128)(2,1)}), bf16[16,2,35840]{2,1,0:T(2,128)(2,1)S(1)}, u32[]{:S(2)}, u32[]{:S(2)}) async-start(bf16[16,2,35840]{2,1,0:T(2,128)(2,1)} %reshape.171), calls=%async_computation.1 | async-start | bytes 4587520 | tf_op jit(solution)/shard_map/all_to_all | solution.py:82
  573.4 120.4 %collective-permute-start.5 = (bf16[64,3584]{1,0:T(8,128)(2,1)}, bf16[64,3584]{1,0:T(8,128)(2,1)}, u32[]{:S(2)}, u32[]{:S(2)}) collective-permute-start(bf16[64,3584]{1,0:T(8,128)(2,1)} %get-tuple-element.21), channel_id=1, source_target_pairs={{0,16},{16,0},{1,17},{17,1},{2,18},{18,2},{3,19},{19,3},{4,20},{20... | collective-permute-start | bytes 1376264 | tf_op jit(solution)/shard_map/ppermute | solution.py:16
  691.0 1.0 copy-start.4
  691.0 1.0 copy-start.13
  692.2 13.3 %collective-permute-start.2 = (bf16[64,3584]{1,0:T(8,128)(2,1)S(1)}, bf16[64,3584]{1,0:T(8,128)(2,1)S(1)}, u32[]{:S(2)}, u32[]{:S(2)}) collective-permute-start(bf16[64,3584]{1,0:T(8,128)(2,1)S(1)} %fusion.8), channel_id=1, source_target_pairs={{0,16},{16,0},{1,17},{17,1},{2,18},{18,2},{3,19},{19,3},{4,20},{20... | collective-permute-start | bytes 1376264 | tf_op jit(solution)/shard_map/ppermute | solution.py:16
where the time goes:
time: 723 us; the launch traced here: 708 us
  other arithmetic  234 us (32%)
  waiting for transfers between devices  182 us (25%)
  local copies, waits for them, and re-layouts  167 us (23%)
  blocking collectives  102 us (14%)
  starting transfers between devices  12.7 us (2%)
  matrix products  9.63 us (1%)
    all_to_all x2, blocking collectives, send_rows(): lax.all_to_all(outgoing, 'ep', split_axis=0, concat_axis=0, tiled=True)  102 us
    convert_element_type x2, other arithmetic, gather_back(): summed = returned.reshape(experts, SLICES // 2, 2, capacity * half_width)...  101 us
    all_to_all x2, waiting for transfers between devices, return_rows(): lax.all_to_all(results, 'ep', split_axis=0, concat_axis=0, tiled=True)  86.9 us
    ppermute x4, waiting for transfers between devices, from_partner(): lax.ppermute(value, axis, [(i, i ^ 1 << stride) for i in range(lax.axis_s...  83 us
    all_to_all x2, other arithmetic, return_rows(): lax.all_to_all(results, 'ep', split_axis=0, concat_axis=0, tiled=True)  55.1 us
    slice x1, local copies, waits for them, and re-layouts, member_rows(): arrived.reshape(senders, count, -1)[:, member].reshape(-1, half_width)  44.8 us
    unnamed x46, local copies, waits for them, and re-layouts  44.4 us
    all_to_all x2, other arithmetic, send_rows(): lax.all_to_all(outgoing, 'ep', split_axis=0, concat_axis=0, tiled=True)  36.2 us
  transfers between devices with their start and end apart: 8, of which 7 were waited for; matrix products, arithmetic and copies ran while one was open for 11% of the time, Pallas kernels for 0%

commit v1 on v0

v1 whole, which is shorter than its diff:
```python
import jax
import jax.numpy as jnp
from jax import lax
from jax.sharding import PartitionSpec as P

SLICES = 8
NEAR, SIDE, FAR = 1, 2, 4


def swap(value, bit):
    return lax.ppermute(value, "ep", [(i, i ^ bit) for i in range(lax.axis_size("ep"))])


def to_expert(value, shift):
    count = lax.axis_size("ep")
    return lax.ppermute(value, "ep", [(i, (i + SLICES * shift) % count) for i in range(count)])


def to_section(value, step, place=lambda i: i):
    sections, count = lax.axis_size("pp"), lax.axis_size("ep")
    pairs = [
        (p * count + i, (p + step) % sections * count + place(i) % count)
        for p in range(sections)
        for i in range(count)
    ]
    return lax.ppermute(value, ("pp", "ep"), pairs)


def dot(a, b):
    return jnp.dot(a, b, preferred_element_type=jnp.float32)


def dot_t(a, b):
    return lax.dot_general(a, b, (((1,), (1,)), ((), ())), preferred_element_type=jnp.float32)


def inverse_rms(widened):
    return lax.rsqrt(jnp.mean(widened * widened, axis=-1, keepdims=True) + 1e-06)


def own_half_first(rows):
    half = rows.shape[1] // 2
    turned = jnp.concatenate([rows[:, half:], rows[:, :half]], axis=1)
    return jnp.where(lax.axis_index("ep") % 2 == 0, rows, turned)


def slot_plan(route_ids, experts, capacity):
    chosen = route_ids[:, 0]
    onehot = (chosen[:, None] == jnp.arange(experts, dtype=jnp.int32)[None, :]).astype(jnp.int32)
    position = jnp.sum((jnp.cumsum(onehot, axis=0) - 1) * onehot, axis=1)
    relative = (chosen - lax.axis_index("ep") // SLICES) % experts
    target = relative * capacity + position
    return target[:, None] == jnp.arange(experts * capacity, dtype=jnp.int32)[None, :]


def place(plan, shift, capacity, values):
    chooser = plan[:, shift * capacity : (shift + 1) * capacity].astype(jnp.bfloat16)
    return lax.dot_general(
        chooser, values, (((0,), (0,)), ((), ())), preferred_element_type=jnp.float32
    ).astype(jnp.bfloat16)


def spread(groups):
    mine = [groups[0]] + [to_expert(groups[r], r) for r in range(1, len(groups))]
    theirs = [swap(part, FAR) for part in mine]
    return mine + theirs


def send_back(partial, experts, capacity, step):
    rows = [partial[i * capacity : (i + 1) * capacity] for i in range(2 * experts)]
    near = [part.astype(jnp.bfloat16) for part in rows[experts:]]
    received = swap(jnp.concatenate(near[1:], axis=0), FAR).astype(jnp.float32)
    back = [
        to_section(rows[0].astype(jnp.bfloat16), step),
        to_section(near[0], step, lambda i: i ^ FAR),
    ]
    for r in range(1, experts):
        summed = rows[r] + received[(r - 1) * capacity : r * capacity]
        back.append(
            to_section(summed.astype(jnp.bfloat16), step, lambda i, r=r: i - SLICES * r)
        )
    return back


def collect(chooser, back, experts, capacity):
    chooser = chooser.astype(jnp.bfloat16)
    total = dot(chooser[:, :capacity], back[0]) + dot(chooser[:, :capacity], back[1])
    for r in range(1, experts):
        total = total + dot(chooser[:, r * capacity : (r + 1) * capacity], back[r + 1])
    return own_half_first(total)


def body(
    fwd_act,
    fwd_route,
    fwd_gate,
    bwd_act,
    bwd_grad,
    bwd_route,
    bwd_gate,
    norm_gain,
    w_gate,
    w_up,
    w_down,
):
    experts = lax.axis_size("ep") // SLICES
    tokens = fwd_act.shape[1]
    capacity = 2 * ((5 * tokens + 8 * experts - 1) // (8 * experts))
    half = w_gate.shape[2]
    gain = norm_gain[0][None, :]

    blocks = []
    for weight in (w_gate[0, 0], w_up[0, 0], w_down[0, 0]):
        beside = swap(weight, SIDE)
        blocks.append([[weight, swap(weight, NEAR)], [beside, swap(beside, NEAR)]])
    gates, ups, downs = blocks

    fwd_wide = fwd_act[0].astype(jnp.float32)
    fwd_normed = own_half_first((fwd_wide * inverse_rms(fwd_wide) * gain).astype(jnp.bfloat16))
    fwd_plan = slot_plan(fwd_route[0], experts, capacity)
    fwd_groups = [place(fwd_plan, r, capacity, fwd_normed) for r in range(experts)]
    fwd_x = jnp.concatenate(spread(fwd_groups), axis=0)

    bwd_wide = bwd_act[0].astype(jnp.float32)
    bwd_normed = own_half_first((bwd_wide * inverse_rms(bwd_wide) * gain).astype(jnp.bfloat16))
    weighted = own_half_first((bwd_gate[0] * bwd_grad[0].astype(jnp.float32)).astype(jnp.bfloat16))
    bwd_plan = slot_plan(bwd_route[0], experts, capacity)
    bwd_groups = [
        jnp.concatenate(
            [place(bwd_plan, r, capacity, bwd_normed), place(bwd_plan, r, capacity, weighted)], axis=0
        )
        for r in range(experts)
    ]
    bwd_arrived = spread(bwd_groups)
    bwd_x = jnp.concatenate([part[:capacity] for part in bwd_arrived], axis=0)
    bwd_g = jnp.concatenate([part[capacity:] for part in bwd_arrived], axis=0)

    fwd_base = to_section(fwd_act[0], 1)
    fwd_mix = to_section(fwd_plan.astype(jnp.float32) * fwd_gate[0], 1)
    bwd_base = to_section(bwd_act[0], -1)
    bwd_seed = to_section(bwd_grad[0], -1)
    bwd_mix = to_section(bwd_plan.astype(jnp.bfloat16), -1)

    def project(rows, pair):
        return dot(rows[:, :half], pair[0]) + dot(rows[:, half:], pair[1])

    hidden = []
    for j in range(2):
        pre = project(fwd_x, gates[j])
        hidden.append((jax.nn.silu(pre) * project(fwd_x, ups[j])).astype(jnp.bfloat16))
    fwd_out = jnp.concatenate(
        [dot(hidden[0], downs[0][k]) + dot(hidden[1], downs[1][k]) for k in range(2)], axis=1
    )
    fwd_back = send_back(fwd_out, experts, capacity, 1)

    d_gates, d_ups = [], []
    for j in range(2):
        pre = project(bwd_x, gates[j])
        up = project(bwd_x, ups[j])
        d_hidden = dot_t(bwd_g[:, :half], downs[j][0]) + dot_t(bwd_g[:, half:], downs[j][1])
        logistic = jax.nn.sigmoid(pre)
        d_gates.append(
            (d_hidden * up * logistic * (1.0 + pre * (1.0 - logistic))).astype(jnp.bfloat16)
        )
        d_ups.append((d_hidden * pre * logistic).astype(jnp.bfloat16))
    d_out = jnp.concatenate(
        [
            dot_t(d_gates[0], gates[0][k])
            + dot_t(d_ups[0], ups[0][k])
            + dot_t(d_gates[1], gates[1][k])
            + dot_t(d_ups[1], ups[1][k])
            for k in range(2)
        ],
        axis=1,
    )
    bwd_back = send_back(own_half_first(gain) * d_out, experts, capacity, -1)

    fwd_weight = jnp.sum(fwd_mix, axis=1, keepdims=True)
    fwd_mixed = collect(fwd_mix > 0, fwd_back, experts, capacity)
    fwd_next = (fwd_base.astype(jnp.float32) + fwd_weight * fwd_mixed).astype(jnp.bfloat16)

    scaled = collect(bwd_mix, bwd_back, experts, capacity)
    widened = bwd_base.astype(jnp.float32)
    inverse = inverse_rms(widened)
    bwd_next = (
        bwd_seed.astype(jnp.float32)
        + scaled * inverse
        - widened * (inverse * inverse * inverse) * jnp.mean(scaled * widened, axis=-1, keepdims=True)
    ).astype(jnp.bfloat16)
    return (fwd_next[None], bwd_next[None])


def solution(mesh):
    rows = P("pp", "ep", None)
    weights = P("pp", "ep", None, None)
    in_specs = (rows,) * 7 + (P("pp", None),) + (weights,) * 3
    return jax.shard_map(
        body, mesh=mesh, in_specs=in_specs, out_specs=(rows, rows), check_vma=False
    )
```

time: 723 us -> 187 us (0.26); the launches traced: 708 us -> 186 us
  other arithmetic: 234 us -> 15.3 us
  local copies, waits for them, and re-layouts: 167 us -> 4.59 us
  blocking collectives: 102 us -> 0 us
  waiting for transfers between devices: 182 us -> 118 us
  starting transfers between devices: 12.7 us -> 30 us
  matrix products: 9.63 us -> 17.3 us
    convert_element_type x7 -> x4, other arithmetic: 104 us -> 1.1 us  [the longest x1 0.68 us: body(): bwd_mix = to_section(bwd_plan.astype(jnp.bfloat16), -1)]
    all_to_all x2 -> x0, blocking collectives: 102 us -> none  [send_rows(): lax.all_to_all(outgoing, 'ep', split_axis=0, concat_axis=0, tiled=True)]
    all_to_all x4 -> x0, other arithmetic: 91.3 us -> none  [the longest x2 55.1 us: return_rows(): lax.all_to_all(results, 'ep', split_axis=0, concat_axis=0, tiled=True)]
    all_to_all x2 -> x0, waiting for transfers between devices: 86.9 us -> none  [return_rows(): lax.all_to_all(results, 'ep', split_axis=0, concat_axis=0, tiled=True)]
    slice x4 -> x11, local copies, waits for them, and re-layouts: 52.2 us -> 1.5 us  [the longest x3 1.16 us: body(): bwd_x = jnp.concatenate([part[:capacity] for part in bwd_arrived], axis=0)]
    unnamed x46 -> x38, local copies, waits for them, and re-layouts: 44.4 us -> 3.09 us
    ppermute x6 -> x28, starting transfers between devices: 4.88 us -> 30 us  [the longest x11 14 us: to_section(): return lax.ppermute(value, ('pp', 'ep'), pairs)]
    another operation x18 -> x0, local copies, waits for them, and re-layouts: 23 us -> none  [the longest x3 16.1 us: member_rows(): arrived.reshape(senders, count, -1)[:, member].reshape(-1, half_width)]
  transfers between devices with their start and end apart: 8 -> 28, of which waited for: 7 -> 12; matrix products, arithmetic and copies ran while one was open for 11% -> 18% of each run, Pallas kernels for 0% -> 0%
where the time goes in v1:
time: 187 us; the launch traced here: 186 us
  waiting for transfers between devices  118 us (63%)
  starting transfers between devices  30 us (16%)
  matrix products  17.3 us (9%)
  other arithmetic  15.3 us (8%)
  local copies, waits for them, and re-layouts  4.59 us (2%)
    ppermute x15, waiting for transfers between devices, swap(): lax.ppermute(value, 'ep', [(i, i ^ bit) for i in range(lax.axis_size('ep'...  61.4 us
    ppermute x11, waiting for transfers between devices, to_section(): return lax.ppermute(value, ('pp', 'ep'), pairs)  32.2 us
    ppermute x2, waiting for transfers between devices, to_expert(): lax.ppermute(value, 'ep', [(i, (i + SLICES * shift) % count) for i in ran...  24 us
    ppermute x11, starting transfers between devices, to_section(): return lax.ppermute(value, ('pp', 'ep'), pairs)  14 us
    ppermute x15, starting transfers between devices, swap(): lax.ppermute(value, 'ep', [(i, i ^ bit) for i in range(lax.axis_size('ep'...  12.5 us
    dot_general x26, matrix products, dot(): return jnp.dot(a, b, preferred_element_type=jnp.float32)  8.26 us
    dot_general x12, matrix products, dot_t(): lax.dot_general(a, b, (((1,), (1,)), ((), ())), preferred_element_type=jn...  5.67 us
  transfers between devices with their start and end apart: 28, of which 12 were waited for; matrix products, arithmetic and copies ran while one was open for 18% of the time, Pallas kernels for 0%

profile of v1, /device:TPU:0, one launch (start us, length us, event | category | flops | bytes accessed | tf_op | source)
XLA Modules:
  0.0 186.2 jit_solution(4241018478006136861)
XLA Ops:
  1.2 2.6 %collective-permute-start.9 = (bf16[1792,256]{1,0:T(8,128)(2,1)}, bf16[1792,256]{1,0:T(8,128)(2,1)S(1)}, u32[]{:S(2)}, u32[]{:S(2)}) collective-permute-start(bf16[1792,256]{1,0:T(8,128)(2,1)} %bitcast.90), channel_id=1, source_target_pairs={{0,2},{1,3},{2,0},{3,1},{4,6},{5,7},{6,4},{7,5},{8,10},{9,11},{10,... | collective-permute-start | bytes 2752520 | tf_op jit(solution)/shard_map/ppermute | solution.py:11
  7.5 1.5 collective-permute-start.1
  13.8 2.6 %collective-permute-start.2 = (bf16[40,3584]{1,0:T(8,128)(2,1)}, bf16[40,3584]{1,0:T(8,128)(2,1)}, u32[]{:S(2)}, u32[]{:S(2)}) collective-permute-start(bf16[40,3584]{1,0:T(8,128)(2,1)} %convolution_convert_fusion.4), channel_id=1, source_target_pairs={{0,8},{1,9},{2,10},{3,11},{4,12},{5,13},{6,14},{7,15},{8,0},{9,1},... | collective-permute-start | bytes 860168 | tf_op jit(solution)/shard_map/ppermute | solution.py:16
  20.6 1.6 collective-permute-start.21
  25.4 16.1 %collective-permute-done.21 = bf16[80,3584]{1,0:T(8,128)(2,1)} collective-permute-done((bf16[80,3584]{1,0:T(8,128)(2,1)}, bf16[80,3584]{1,0:T(8,128)(2,1)}, u32[]{:S(2)}, u32[]{:S(2)}) %collective-permute-start.21) | collective-permute-done | bytes 573472 | tf_op jit(solution)/shard_map/ppermute | solution.py:11
  43.5 24.0 %collective-permute-done.20 = bf16[80,3584]{1,0:T(8,128)(2,1)S(1)} collective-permute-done((bf16[80,3584]{1,0:T(8,128)(2,1)}, bf16[80,3584]{1,0:T(8,128)(2,1)S(1)}, u32[]{:S(2)}, u32[]{:S(2)}) %collective-permute-start.20) | collective-permute-done | bytes 573472 | tf_op jit(solution)/shard_map/ppermute | solution.py:16
  68.1 8.2 %collective-permute-done.4 = bf16[40,3584]{1,0:T(8,128)(2,1)S(1)} collective-permute-done((bf16[40,3584]{1,0:T(8,128)(2,1)}, bf16[40,3584]{1,0:T(8,128)(2,1)S(1)}, u32[]{:S(2)}, u32[]{:S(2)}) %collective-permute-start.4) | collective-permute-done | bytes 286752 | tf_op jit(solution)/shard_map/ppermute | solution.py:11
  81.6 1.5 collective-permute-start.27
  83.5 7.3 %collective-permute-done.7 = bf16[1792,256]{1,0:T(8,128)(2,1)S(1)} collective-permute-done((bf16[1792,256]{1,0:T(8,128)(2,1)S(1)}, bf16[1792,256]{1,0:T(8,128)(2,1)S(1)}, u32[]{:S(2)}, u32[]{:S(2)}) %collective-permute-start.7) | collective-permute-done | bytes 917536 | tf_op jit(solution)/shard_map/ppermute | solution.py:11
  90.8 2.1 %collective-permute-start.22 = (bf16[80,3584]{1,0:T(8,128)(2,1)S(1)}, bf16[80,3584]{1,0:T(8,128)(2,1)S(1)}, u32[]{:S(2)}, u32[]{:S(2)}) collective-permute-start(bf16[80,3584]{1,0:T(8,128)(2,1)S(1)} %collective-permute-done.20), channel_id=1, source_target_pairs={{0,4},{1,5},{2,6},{3,7},{4,0},{5,1},{6,2},{7,3},{8,12},{9,13},{10,... | collective-permute-start | bytes 1720328 | tf_op jit(solution)/shard_map/ppermute | solution.py:11
  93.9 15.4 %collective-permute-done.11 = bf16[256,1792]{1,0:T(8,128)(2,1)S(1)} collective-permute-done((bf16[256,1792]{1,0:T(8,128)(2,1)S(1)}, bf16[256,1792]{1,0:T(8,128)(2,1)S(1)}, u32[]{:S(2)}, u32[]{:S(2)}) %collective-permute-start.11) | collective-permute-done | bytes 917536 | tf_op jit(solution)/shard_map/ppermute | solution.py:11
  120.0 1.8 collective-permute-start.25
  124.6 5.2 %collective-permute-done.25 = bf16[40,3584]{1,0:T(8,128)(2,1)S(1)} collective-permute-done((bf16[40,3584]{1,0:T(8,128)(2,1)S(1)}, bf16[40,3584]{1,0:T(8,128)(2,1)S(1)}, u32[]{:S(2)}, u32[]{:S(2)}) %collective-permute-start.25) | collective-permute-done | bytes 286752 | tf_op jit(solution)/shard_map/ppermute | solution.py:11
  129.8 1.7 collective-permute-start.16
  131.6 9.2 %collective-permute-done.16 = bf16[40,3584]{1,0:T(8,128)(2,1)S(1)} collective-permute-done((bf16[40,3584]{1,0:T(8,128)(2,1)S(1)}, bf16[40,3584]{1,0:T(8,128)(2,1)S(1)}, u32[]{:S(2)}, u32[]{:S(2)}) %collective-permute-start.16) | collective-permute-done | bytes 286752 | tf_op jit(solution)/shard_map/ppermute | solution.py:11
  140.8 2.7 %collective-permute-start.15 = (bf16[40,3584]{1,0:T(8,128)(2,1)S(1)}, bf16[40,3584]{1,0:T(8,128)(2,1)S(1)}, u32[]{:S(2)}, u32[]{:S(2)}) collective-permute-start(bf16[40,3584]{1,0:T(8,128)(2,1)S(1)} %get-tuple-element.13), channel_id=1, source_target_pairs={{0,20},{1,21},{2,22},{3,23},{4,16},{5,17},{6,18},{7,19},{8,28},{9,... | collective-permute-start | bytes 860168 | tf_op jit(solution)/shard_map/ppermute | solution.py:26
  144.2 1.4 collective-permute-start.17
  145.9 7.5 %collective-permute-done.15 = bf16[40,3584]{1,0:T(8,128)(2,1)S(1)} collective-permute-done((bf16[40,3584]{1,0:T(8,128)(2,1)S(1)}, bf16[40,3584]{1,0:T(8,128)(2,1)S(1)}, u32[]{:S(2)}, u32[]{:S(2)}) %collective-permute-start.15) | collective-permute-done | bytes 286752 | tf_op jit(solution)/shard_map/ppermute | solution.py:26
  154.7 12.9 %collective-permute-done.17 = bf16[40,3584]{1,0:T(8,128)(2,1)S(1)} collective-permute-done((bf16[40,3584]{1,0:T(8,128)(2,1)S(1)}, bf16[40,3584]{1,0:T(8,128)(2,1)S(1)}, u32[]{:S(2)}, u32[]{:S(2)}) %collective-permute-start.17) | collective-permute-done | bytes 286752 | tf_op jit(solution)/shard_map/ppermute | solution.py:26
  167.5 1.5 collective-permute-start.23
  169.4 2.2 %collective-permute-done.26 = bf16[40,3584]{1,0:T(8,128)(2,1)S(1)} collective-permute-done((bf16[40,3584]{1,0:T(8,128)(2,1)S(1)}, bf16[40,3584]{1,0:T(8,128)(2,1)S(1)}, u32[]{:S(2)}, u32[]{:S(2)}) %collective-permute-start.26) | collective-permute-done | bytes 286752 | tf_op jit(solution)/shard_map/ppermute | solution.py:26
  171.6 1.5 collective-permute-start.14
  173.4 4.4 %collective-permute-done.23 = bf16[40,3584]{1,0:T(8,128)(2,1)S(1)} collective-permute-done((bf16[40,3584]{1,0:T(8,128)(2,1)S(1)}, bf16[40,3584]{1,0:T(8,128)(2,1)S(1)}, u32[]{:S(2)}, u32[]{:S(2)}) %collective-permute-start.23) | collective-permute-done | bytes 286752 | tf_op jit(solution)/shard_map/ppermute | solution.py:26
  178.4 5.3 %collective-permute-done.14 = bf16[40,3584]{1,0:T(8,128)(2,1)S(1)} collective-permute-done((bf16[40,3584]{1,0:T(8,128)(2,1)S(1)}, bf16[40,3584]{1,0:T(8,128)(2,1)S(1)}, u32[]{:S(2)}, u32[]{:S(2)}) %collective-permute-start.14) | collective-permute-done | bytes 286752 | tf_op jit(solution)/shard_map/ppermute | solution.py:26
  (159 shorter events, 44.6 us)
Async XLA Ops:
  0.7 77.3 %collective-permute-start.6 = (bf16[1792,256]{1,0:T(8,128)(2,1)}, bf16[1792,256]{1,0:T(8,128)(2,1)S(1)}, u32[]{:S(2)}, u32[]{:S(2)}) collective-permute-start(bf16[1792,256]{1,0:T(8,128)(2,1)} %bitcast.89), channel_id=1, source_target_pairs={{0,1},{1,0},{2,3},{3,2},{4,5},{5,4},{6,7},{7,6},{8,9},{9,8},{10,11... | collective-permute-start | bytes 2752520 | tf_op jit(solution)/shard_map/ppermute | solution.py:11
  1.2 79.8 %collective-permute-start.9 = (bf16[1792,256]{1,0:T(8,128)(2,1)}, bf16[1792,256]{1,0:T(8,128)(2,1)S(1)}, u32[]{:S(2)}, u32[]{:S(2)}) collective-permute-start(bf16[1792,256]{1,0:T(8,128)(2,1)} %bitcast.90), channel_id=1, source_target_pairs={{0,2},{1,3},{2,0},{3,1},{4,6},{5,7},{6,4},{7,5},{8,10},{9,11},{10,... | collective-permute-start | bytes 2752520 | tf_op jit(solution)/shard_map/ppermute | solution.py:11
  7.5 17.3 %collective-permute-start.1 = (f32[64,80]{1,0:T(8,128)}, f32[64,80]{1,0:T(8,128)S(1)}, u32[]{:S(2)}, u32[]{:S(2)}) collective-permute-start(f32[64,80]{1,0:T(8,128)} %broadcast_select_fusion.1), channel_id=1, source_target_pairs={{0,16},{1,17},{2,18},{3,19},{4,20},{5,21},{6,22},{7,23},{8,24},{9,... | collective-permute-start | bytes 61448 | tf_op jit(solution)/shard_map/ppermute | solution.py:26
  13.8 29.5 %collective-permute-start.2 = (bf16[40,3584]{1,0:T(8,128)(2,1)}, bf16[40,3584]{1,0:T(8,128)(2,1)}, u32[]{:S(2)}, u32[]{:S(2)}) collective-permute-start(bf16[40,3584]{1,0:T(8,128)(2,1)} %convolution_convert_fusion.4), channel_id=1, source_target_pairs={{0,8},{1,9},{2,10},{3,11},{4,12},{5,13},{6,14},{7,15},{8,0},{9,1},... | collective-permute-start | bytes 860168 | tf_op jit(solution)/shard_map/ppermute | solution.py:16
  20.6 20.9 %collective-permute-start.21 = (bf16[80,3584]{1,0:T(8,128)(2,1)}, bf16[80,3584]{1,0:T(8,128)(2,1)}, u32[]{:S(2)}, u32[]{:S(2)}) collective-permute-start(bf16[80,3584]{1,0:T(8,128)(2,1)} %pad_maximum_fusion.5), channel_id=1, source_target_pairs={{0,4},{1,5},{2,6},{3,7},{4,0},{5,1},{6,2},{7,3},{8,12},{9,13},{10,... | collective-permute-start | bytes 1720328 | tf_op jit(solution)/shard_map/ppermute | solution.py:11
  24.8 42.7 %collective-permute-start.3 = (bf16[40,3584]{1,0:T(8,128)(2,1)}, bf16[40,3584]{1,0:T(8,128)(2,1)S(1)}, u32[]{:S(2)}, u32[]{:S(2)}) collective-permute-start(bf16[40,3584]{1,0:T(8,128)(2,1)} %convolution_convert_fusion.5), channel_id=1, source_target_pairs={{0,4},{1,5},{2,6},{3,7},{4,0},{5,1},{6,2},{7,3},{8,12},{9,13},{10,... | collective-permute-start | bytes 860168 | tf_op jit(solution)/shard_map/ppermute | solution.py:11
  41.5 26.0 %collective-permute-start.20 = (bf16[80,3584]{1,0:T(8,128)(2,1)}, bf16[80,3584]{1,0:T(8,128)(2,1)S(1)}, u32[]{:S(2)}, u32[]{:S(2)}) collective-permute-start(bf16[80,3584]{1,0:T(8,128)(2,1)} %pad_maximum_fusion.4), channel_id=1, source_target_pairs={{0,8},{1,9},{2,10},{3,11},{4,12},{5,13},{6,14},{7,15},{8,0},{9,1},... | collective-permute-start | bytes 1720328 | tf_op jit(solution)/shard_map/ppermute | solution.py:16
  43.4 35.0 %collective-permute-start.5 = (bf16[1792,256]{1,0:T(8,128)(2,1)S(1)}, bf16[1792,256]{1,0:T(8,128)(2,1)S(1)}, u32[]{:S(2)}, u32[]{:S(2)}) collective-permute-start(bf16[1792,256]{1,0:T(8,128)(2,1)S(1)} %bitcast.83), channel_id=1, source_target_pairs={{0,1},{1,0},{2,3},{3,2},{4,5},{5,4},{6,7},{7,6},{8,9},{9,8},{10,11... | collective-permute-start | bytes 2752520 | tf_op jit(solution)/shard_map/ppermute | solution.py:11
  67.5 23.3 %collective-permute-start.7 = (bf16[1792,256]{1,0:T(8,128)(2,1)S(1)}, bf16[1792,256]{1,0:T(8,128)(2,1)S(1)}, u32[]{:S(2)}, u32[]{:S(2)}) collective-permute-start(bf16[1792,256]{1,0:T(8,128)(2,1)S(1)} %bitcast.84), channel_id=1, source_target_pairs={{0,2},{1,3},{2,0},{3,1},{4,6},{5,7},{6,4},{7,5},{8,10},{9,11},{10,... | collective-permute-start | bytes 2752520 | tf_op jit(solution)/shard_map/ppermute | solution.py:11
  76.3 33.1 %collective-permute-start.11 = (bf16[256,1792]{1,0:T(8,128)(2,1)S(1)}, bf16[256,1792]{1,0:T(8,128)(2,1)S(1)}, u32[]{:S(2)}, u32[]{:S(2)}) collective-permute-start(bf16[256,1792]{1,0:T(8,128)(2,1)S(1)} %bitcast.87), channel_id=1, source_target_pairs={{0,2},{1,3},{2,0},{3,1},{4,6},{5,7},{6,4},{7,5},{8,10},{9,11},{10,... | collective-permute-start | bytes 2752520 | tf_op jit(solution)/shard_map/ppermute | solution.py:11
  77.9 15.6 %collective-permute-start.12 = (bf16[256,1792]{1,0:T(8,128)(2,1)S(1)}, bf16[256,1792]{1,0:T(8,128)(2,1)S(1)}, u32[]{:S(2)}, u32[]{:S(2)}) collective-permute-start(bf16[256,1792]{1,0:T(8,128)(2,1)S(1)} %bitcast.88), channel_id=1, source_target_pairs={{0,1},{1,0},{2,3},{3,2},{4,5},{5,4},{6,7},{7,6},{8,9},{9,8},{10,11... | collective-permute-start | bytes 2752520 | tf_op jit(solution)/shard_map/ppermute | solution.py:11
  78.6 64.9 %collective-permute-start.19 = (bf16[64,80]{1,0:T(8,128)(2,1)S(1)}, bf16[64,80]{1,0:T(8,128)(2,1)S(1)}, u32[]{:S(2)}, u32[]{:S(2)}) collective-permute-start(bf16[64,80]{1,0:T(8,128)(2,1)S(1)} %copy-done.16), channel_id=1, source_target_pairs={{0,16},{1,17},{2,18},{3,19},{4,20},{5,21},{6,22},{7,23},{8,24},{9,... | collective-permute-start | bytes 30728 | tf_op jit(solution)/shard_map/ppermute | solution.py:26
  81.6 96.5 %collective-permute-start.27 = (bf16[64,3584]{1,0:T(8,128)(2,1)S(1)}, bf16[64,3584]{1,0:T(8,128)(2,1)S(1)}, u32[]{:S(2)}, u32[]{:S(2)}) collective-permute-start(bf16[64,3584]{1,0:T(8,128)(2,1)S(1)} %bitcast.85), channel_id=1, source_target_pairs={{0,16},{1,17},{2,18},{3,19},{4,20},{5,21},{6,22},{7,23},{8,24},{9,... | collective-permute-start | bytes 1376264 | tf_op jit(solution)/shard_map/ppermute | solution.py:26
  90.8 18.6 %collective-permute-start.22 = (bf16[80,3584]{1,0:T(8,128)(2,1)S(1)}, bf16[80,3584]{1,0:T(8,128)(2,1)S(1)}, u32[]{:S(2)}, u32[]{:S(2)}) collective-permute-start(bf16[80,3584]{1,0:T(8,128)(2,1)S(1)} %collective-permute-done.20), channel_id=1, source_target_pairs={{0,4},{1,5},{2,6},{3,7},{4,0},{5,1},{6,2},{7,3},{8,12},{9,13},{10,... | collective-permute-start | bytes 1720328 | tf_op jit(solution)/shard_map/ppermute | solution.py:11
  93.5 24.2 %collective-permute-start.10 = (bf16[1792,256]{1,0:T(8,128)(2,1)S(1)}, bf16[1792,256]{1,0:T(8,128)(2,1)S(1)}, u32[]{:S(2)}, u32[]{:S(2)}) collective-permute-start(bf16[1792,256]{1,0:T(8,128)(2,1)S(1)} %collective-permute-done.9), channel_id=1, source_target_pairs={{0,1},{1,0},{2,3},{3,2},{4,5},{5,4},{6,7},{7,6},{8,9},{9,8},{10,11... | collective-permute-start | bytes 2752520 | tf_op jit(solution)/shard_map/ppermute | solution.py:11
  116.0 69.2 %collective-permute-start = (bf16[64,3584]{1,0:T(8,128)(2,1)S(1)}, bf16[64,3584]{1,0:T(8,128)(2,1)S(1)}, u32[]{:S(2)}, u32[]{:S(2)}) collective-permute-start(bf16[64,3584]{1,0:T(8,128)(2,1)S(1)} %bitcast.86), channel_id=1, source_target_pairs={{0,16},{1,17},{2,18},{3,19},{4,20},{5,21},{6,22},{7,23},{8,24},{9,... | collective-permute-start | bytes 1376264 | tf_op jit(solution)/shard_map/ppermute | solution.py:26
  121.8 22.4 %collective-permute-start.24 = (bf16[40,3584]{1,0:T(8,128)(2,1)S(1)}, bf16[40,3584]{1,0:T(8,128)(2,1)S(1)}, u32[]{:S(2)}, u32[]{:S(2)}) collective-permute-start(bf16[40,3584]{1,0:T(8,128)(2,1)S(1)} %get-tuple-element.10), channel_id=1, source_target_pairs={{0,20},{1,21},{2,22},{3,23},{4,16},{5,17},{6,18},{7,19},{8,28},{9,... | collective-permute-start | bytes 860168 | tf_op jit(solution)/shard_map/ppermute | solution.py:26
  129.8 11.0 %collective-permute-start.16 = (bf16[40,3584]{1,0:T(8,128)(2,1)S(1)}, bf16[40,3584]{1,0:T(8,128)(2,1)S(1)}, u32[]{:S(2)}, u32[]{:S(2)}) collective-permute-start(bf16[40,3584]{1,0:T(8,128)(2,1)S(1)} %get-tuple-element.12), channel_id=1, source_target_pairs={{0,4},{1,5},{2,6},{3,7},{4,0},{5,1},{6,2},{7,3},{8,12},{9,13},{10,... | collective-permute-start | bytes 860168 | tf_op jit(solution)/shard_map/ppermute | solution.py:11
  140.8 12.6 %collective-permute-start.15 = (bf16[40,3584]{1,0:T(8,128)(2,1)S(1)}, bf16[40,3584]{1,0:T(8,128)(2,1)S(1)}, u32[]{:S(2)}, u32[]{:S(2)}) collective-permute-start(bf16[40,3584]{1,0:T(8,128)(2,1)S(1)} %get-tuple-element.13), channel_id=1, source_target_pairs={{0,20},{1,21},{2,22},{3,23},{4,16},{5,17},{6,18},{7,19},{8,28},{9,... | collective-permute-start | bytes 860168 | tf_op jit(solution)/shard_map/ppermute | solution.py:26
  143.6 40.4 %collective-permute-start.18 = (bf16[64,3584]{1,0:T(8,128)(2,1)S(1)}, bf16[64,3584]{1,0:T(8,128)(2,1)S(1)}, u32[]{:S(2)}, u32[]{:S(2)}) collective-permute-start(bf16[64,3584]{1,0:T(8,128)(2,1)S(1)} %bitcast.91), channel_id=1, source_target_pairs={{0,16},{1,17},{2,18},{3,19},{4,20},{5,21},{6,22},{7,23},{8,24},{9,... | collective-permute-start | bytes 1376264 | tf_op jit(solution)/shard_map/ppermute | solution.py:26
  144.2 23.4 %collective-permute-start.17 = (bf16[40,3584]{1,0:T(8,128)(2,1)S(1)}, bf16[40,3584]{1,0:T(8,128)(2,1)S(1)}, u32[]{:S(2)}, u32[]{:S(2)}) collective-permute-start(bf16[40,3584]{1,0:T(8,128)(2,1)S(1)} %fusion.31), channel_id=1, source_target_pairs={{0,24},{1,25},{2,26},{3,27},{4,28},{5,29},{6,30},{7,31},{8,16},{9,... | collective-permute-start | bytes 860168 | tf_op jit(solution)/shard_map/ppermute | solution.py:26
  153.4 18.2 %collective-permute-start.26 = (bf16[40,3584]{1,0:T(8,128)(2,1)S(1)}, bf16[40,3584]{1,0:T(8,128)(2,1)S(1)}, u32[]{:S(2)}, u32[]{:S(2)}) collective-permute-start(bf16[40,3584]{1,0:T(8,128)(2,1)S(1)} %fusion.32), channel_id=1, source_target_pairs={{0,24},{1,25},{2,26},{3,27},{4,28},{5,29},{6,30},{7,31},{8,16},{9,... | collective-permute-start | bytes 860168 | tf_op jit(solution)/shard_map/ppermute | solution.py:26
  167.5 10.2 %collective-permute-start.23 = (bf16[40,3584]{1,0:T(8,128)(2,1)S(1)}, bf16[40,3584]{1,0:T(8,128)(2,1)S(1)}, u32[]{:S(2)}, u32[]{:S(2)}) collective-permute-start(bf16[40,3584]{1,0:T(8,128)(2,1)S(1)} %get-tuple-element.8), channel_id=1, source_target_pairs={{0,16},{1,17},{2,18},{3,19},{4,20},{5,21},{6,22},{7,23},{8,24},{9,... | collective-permute-start | bytes 860168 | tf_op jit(solution)/shard_map/ppermute | solution.py:26
  171.6 12.2 %collective-permute-start.14 = (bf16[40,3584]{1,0:T(8,128)(2,1)S(1)}, bf16[40,3584]{1,0:T(8,128)(2,1)S(1)}, u32[]{:S(2)}, u32[]{:S(2)}) collective-permute-start(bf16[40,3584]{1,0:T(8,128)(2,1)S(1)} %get-tuple-element.11), channel_id=1, source_target_pairs={{0,16},{1,17},{2,18},{3,19},{4,20},{5,21},{6,22},{7,23},{8,24},{9,... | collective-permute-start | bytes 860168 | tf_op jit(solution)/shard_map/ppermute | solution.py:26
  (23 other events, 181.4 us)

commit v2 on v1

v2 whole, which is shorter than its diff:
```python
import functools

import jax
import jax.numpy as jnp
from jax import lax
from jax.experimental import pallas as pl
from jax.experimental.pallas import tpu as pltpu
from jax.sharding import PartitionSpec as P

SLICES = 8
NEAR, SIDE, FAR = 1, 2, 4
SHORT, LONG = 10**9, 2 * 10**11


def swap(value, bit):
    return lax.ppermute(value, "ep", [(i, i ^ bit) for i in range(lax.axis_size("ep"))])


def to_expert(value, shift):
    count = lax.axis_size("ep")
    return lax.ppermute(value, "ep", [(i, (i + SLICES * shift) % count) for i in range(count)])


def to_section(value, step, place=lambda i: i):
    sections, count = lax.axis_size("pp"), lax.axis_size("ep")
    pairs = [
        (p * count + i, (p + step) % sections * count + place(i) % count)
        for p in range(sections)
        for i in range(count)
    ]
    return lax.ppermute(value, ("pp", "ep"), pairs)


def after(value, *done):
    return lax.optimization_barrier((value, done))[0]


def dot(a, b):
    return jnp.dot(a, b, preferred_element_type=jnp.float32)


def dot_t(a, b):
    return lax.dot_general(a, b, (((1,), (1,)), ((), ())), preferred_element_type=jnp.float32)


def dot_first(a, b):
    return lax.dot_general(a, b, (((0,), (0,)), ((), ())), preferred_element_type=jnp.float32)


def call(kernel, name, outs, cost, args):
    def whole(shape):
        return pl.BlockSpec(shape, lambda i: (0, 0))

    return pl.pallas_call(
        kernel,
        name=name,
        grid=(1,),
        out_shape=[jax.ShapeDtypeStruct(shape, jnp.bfloat16) for shape in outs],
        in_specs=[whole(arg.shape) for arg in args],
        out_specs=[whole(shape) for shape in outs],
        cost_estimate=pl.CostEstimate(flops=cost, bytes_accessed=0, transcendentals=0),
        compiler_params=pltpu.CompilerParams(vmem_limit_bytes=24 * 2**20),
    )(*args)


def my_place():
    me = lax.axis_index("ep")
    return me // SLICES, me % 2


def slot_rows(route_ref, mine, experts, capacity):
    chosen = route_ref[...]
    tokens = chosen.shape[1]
    onehot = lax.broadcasted_iota(jnp.int32, (experts, tokens), 0) == chosen
    before = lax.broadcasted_iota(jnp.int32, (tokens, tokens), 0) <= lax.broadcasted_iota(
        jnp.int32, (tokens, tokens), 1
    )
    running = dot(onehot.astype(jnp.bfloat16), before.astype(jnp.bfloat16))
    position = jnp.sum(jnp.where(onehot, running, 0.0), axis=0, keepdims=True) - 1.0
    relative = chosen - mine
    relative = jnp.where(relative < 0, relative + experts, relative)
    return relative * capacity + position.astype(jnp.int32)


def choose(target, first, count):
    slots = lax.broadcasted_iota(jnp.int32, (count, target.shape[1]), 0)
    return slots == target - first


def to_column(row):
    size = row.shape[1]
    same = lax.broadcasted_iota(jnp.int32, (size, size), 0) == lax.broadcasted_iota(
        jnp.int32, (size, size), 1
    )
    return jnp.sum(jnp.where(same, row, 0.0), axis=1, keepdims=True)


def inverse_rms(widened):
    return lax.rsqrt(jnp.mean(widened * widened, axis=-1, keepdims=True) + 1e-06)


def put_halves(out_ref, first, core, chooser, rows):
    half = rows.shape[1] // 2
    for k in range(2):
        placed = dot(chooser, rows[:, k * half : (k + 1) * half]).astype(jnp.bfloat16)
        start = first + half * (core if k == 0 else 1 - core)
        out_ref[:, pl.ds(pl.multiple_of(start, 128), half)] = placed


def token_slots(target, count, lanes):
    column = to_column(target.astype(jnp.float32)).astype(jnp.int32)
    return lax.broadcasted_iota(jnp.int32, (target.shape[1], lanes), 1) == column


def prepare_kernel(experts, capacity, route_ref, gate_ref, act_ref, gain_ref, pack_ref, *outs):
    mine, core = my_place()
    width = act_ref.shape[1]
    target = slot_rows(route_ref, mine, experts, capacity)
    widened = act_ref[...].astype(jnp.float32)
    normed = (widened * inverse_rms(widened) * gain_ref[...]).astype(jnp.bfloat16)
    for r in range(experts):
        chooser = choose(target, r * capacity, capacity).astype(jnp.bfloat16)
        put_halves(outs[r], 0, core, chooser, normed)
    pack_ref[:, :width] = act_ref[...]
    lanes = pack_ref.shape[1] - width
    slots = experts * capacity
    packed = token_slots(target, slots, lanes).astype(jnp.float32)
    rest = to_column(gate_ref[...])
    lane = lax.broadcasted_iota(jnp.int32, packed.shape, 1)
    for part in range(3):
        piece = rest.astype(jnp.bfloat16).astype(jnp.float32)
        packed = jnp.where(lane == slots + part, piece, packed)
        rest = rest - piece
    pack_ref[:, width:] = packed.astype(jnp.bfloat16)


def prepare_back_kernel(
    experts, capacity, route_ref, gate_ref, act_ref, grad_ref, gain_ref, pack_ref, *outs
):
    mine, core = my_place()
    width = act_ref.shape[1]
    target = slot_rows(route_ref, mine, experts, capacity)
    widened = act_ref[...].astype(jnp.float32)
    normed = (widened * inverse_rms(widened) * gain_ref[...]).astype(jnp.bfloat16)
    weighted = (to_column(gate_ref[...]) * grad_ref[...].astype(jnp.float32)).astype(jnp.bfloat16)
    for r in range(experts):
        chooser = choose(target, r * capacity, capacity).astype(jnp.bfloat16)
        if r == 0:
            put_halves(outs[0], 0, core, chooser, normed)
            put_halves(outs[1], 0, core, chooser, weighted)
        else:
            put_halves(outs[r + 1], 0, core, chooser, normed)
            put_halves(outs[r + 1], width, core, chooser, weighted)
    pack_ref[:, :width] = act_ref[...]
    pack_ref[:, width : 2 * width] = grad_ref[...]
    lanes = pack_ref.shape[1] - 2 * width
    packed = token_slots(target, experts * capacity, lanes)
    pack_ref[:, 2 * width :] = packed.astype(jnp.float32).astype(jnp.bfloat16)


def join_kernel(*refs):
    *parts, out_ref = refs
    width = parts[0].shape[1]
    for i, part in enumerate(parts):
        out_ref[:, i * width : (i + 1) * width] = part[...]


def collected(chooser, core, back, capacity, k):
    half = back[0].shape[1] // 2
    start = pl.multiple_of(half * (core if k == 0 else 1 - core), 128)
    columns = pl.ds(start, half)
    first = chooser[:, :capacity]
    total = dot(first, back[0][:, columns]) + dot(first, back[1][:, columns])
    for r, part in enumerate(back[2:], 1):
        total = total + dot(chooser[:, r * capacity : (r + 1) * capacity], part[:, columns])
    return total


def finish_kernel(experts, capacity, pack_ref, *rest):
    *back, out_ref = rest
    core = my_place()[1]
    width = out_ref.shape[1]
    half = width // 2
    slots = experts * capacity
    packed = pack_ref[:, width:]
    parts = packed[:, slots : slots + 3].astype(jnp.float32)
    weight = parts[:, 0:1] + parts[:, 1:2] + parts[:, 2:3]
    for k in range(2):
        columns = slice(k * half, (k + 1) * half)
        mixed = collected(packed, core, back, capacity, k)
        out_ref[:, columns] = (
            pack_ref[:, columns].astype(jnp.float32) + weight * mixed
        ).astype(jnp.bfloat16)


def finish_back_kernel(experts, capacity, pack_ref, *rest):
    *back, out_ref = rest
    core = my_place()[1]
    width = out_ref.shape[1]
    half = width // 2
    packed = pack_ref[:, 2 * width :]
    scaled = [collected(packed, core, back, capacity, k) for k in range(2)]
    widened = [pack_ref[:, k * half : (k + 1) * half].astype(jnp.float32) for k in range(2)]
    squares = sum(jnp.sum(w * w, axis=-1, keepdims=True) for w in widened)
    inverse = lax.rsqrt(squares / width + 1e-06)
    inner = sum(jnp.sum(s * w, axis=-1, keepdims=True) for s, w in zip(scaled, widened))
    factor = inverse * inverse * inverse * (inner / width)
    for k in range(2):
        seed = pack_ref[:, width + k * half : width + (k + 1) * half].astype(jnp.float32)
        out_ref[:, k * half : (k + 1) * half] = (
            seed + scaled[k] * inverse - widened[k] * factor
        ).astype(jnp.bfloat16)


def send_back(partial, experts, capacity):
    near = partial[experts * capacity :].astype(jnp.bfloat16)
    return swap(near[capacity:], FAR), near[:capacity], partial[:capacity].astype(jnp.bfloat16)


def send_sums(partial, received, experts, capacity, step):
    sums = []
    for r in range(1, experts):
        part = received[(r - 1) * capacity : r * capacity].astype(jnp.float32)
        summed = (partial[r * capacity : (r + 1) * capacity] + part).astype(jnp.bfloat16)
        sums.append(to_section(summed, step, lambda i, r=r: i - SLICES * r))
    return sums


def body(
    fwd_act,
    fwd_route,
    fwd_gate,
    bwd_act,
    bwd_grad,
    bwd_route,
    bwd_gate,
    norm_gain,
    w_gate,
    w_up,
    w_down,
):
    experts = lax.axis_size("ep") // SLICES
    tokens, width = fwd_act.shape[1:]
    capacity = 2 * ((5 * tokens + 8 * experts - 1) // (8 * experts))
    half = w_gate.shape[2]
    shifts = range(1, experts)
    me = lax.axis_index("ep")
    gate, up, down = w_gate[0, 0], w_up[0, 0], w_down[0, 0]
    row = (1, tokens)
    lanes = -(-(experts * capacity + 3) // 128) * 128
    slots = (capacity, width)
    two_slots = (capacity, 2 * width)

    side_down = swap(down, SIDE)
    near_gate = swap(gate, NEAR)
    fwd_pack, *fwd_groups = call(
        functools.partial(prepare_kernel, experts, capacity),
        "prepare",
        [(tokens, width + lanes)] + [slots] * experts,
        LONG,
        (fwd_route.reshape(row), fwd_gate.reshape(row), fwd_act[0], norm_gain),
    )
    fwd_far = [to_expert(fwd_groups[r], r) for r in shifts]
    own_pairs = [swap(fwd_groups[0], FAR)]
    fwd_pack = to_section(fwd_pack, 1)
    bwd_pack, bwd_first, grad_first, *bwd_groups = call(
        functools.partial(prepare_back_kernel, experts, capacity),
        "prepare_back",
        [(tokens, 2 * width + lanes), slots, slots] + [two_slots] * (experts - 1),
        SHORT,
        (bwd_route.reshape(row), bwd_gate.reshape(row), bwd_act[0], bwd_grad[0], norm_gain),
    )

    first = (side_down, near_gate, fwd_pack, own_pairs[0], *fwd_far)
    near_up = swap(after(up, *first), NEAR)
    bwd_pack = to_section(after(bwd_pack, *first), -1)
    (mixed,) = call(
        join_kernel,
        "join",
        [(capacity, experts * width)],
        LONG,
        (after(bwd_first, *first), *fwd_far),
    )
    mixed_pair = swap(mixed, FAR)
    own_pairs.append(mixed_pair[:, :width])
    fwd_far_pair = [mixed_pair[:, r * width : (r + 1) * width] for r in shifts]
    side_gate = swap(after(gate, *first), SIDE)
    bwd_far = [to_expert(after(bwd_groups[r - 1], *first), r) for r in shifts]

    second = (side_gate, near_up, bwd_pack, mixed_pair, *bwd_far)
    side_near_down = swap(after(side_down, *second), NEAR)
    near_down = swap(after(down, *second), NEAR)
    side_near_gate = swap(after(side_gate, side_near_down), NEAR)
    own_pairs.append(swap(after(grad_first, *second), FAR))
    bwd_far_pair = [swap(after(part, *second), FAR) for part in bwd_far]
    side_up = swap(after(up, *second), SIDE)
    third = (side_up, near_down, side_near_gate, own_pairs[2], *bwd_far_pair)
    side_near_up = swap(after(side_up, *third), NEAR)

    gates = [[gate, near_gate], [side_gate, side_near_gate]]
    ups = [[up, near_up], [side_up, side_near_up]]
    downs = [[down, near_down], [side_down, side_near_down]]

    def joined(own, mine, own_pair, theirs, at):
        def part(value):
            return value[:, at * width : (at + 1) * width]

        return jnp.concatenate([own, *map(part, mine), own_pair, *map(part, theirs)], axis=0)

    fwd_x = joined(fwd_groups[0], fwd_far, own_pairs[0], fwd_far_pair, 0)
    bwd_x = joined(bwd_first, bwd_far, own_pairs[1], bwd_far_pair, 0)
    bwd_g = joined(grad_first, bwd_far, own_pairs[2], bwd_far_pair, 1)

    def project(rows, pair):
        return dot(rows[:, :half], pair[0]) + dot(rows[:, half:], pair[1])

    hidden = []
    for j in range(2):
        pre = project(fwd_x, gates[j])
        hidden.append((jax.nn.silu(pre) * project(fwd_x, ups[j])).astype(jnp.bfloat16))
    fwd_out = jnp.concatenate(
        [dot(hidden[0], downs[0][k]) + dot(hidden[1], downs[1][k]) for k in range(2)], axis=1
    )
    fwd_received, fwd_near, fwd_own = send_back(fwd_out, experts, capacity)
    fwd_near_sums = to_section(fwd_own, 1)

    d_gates, d_ups = [], []
    for j in range(2):
        pre = project(bwd_x, gates[j])
        upper = project(bwd_x, ups[j])
        d_hidden = dot_t(bwd_g[:, :half], downs[j][0]) + dot_t(bwd_g[:, half:], downs[j][1])
        logistic = jax.nn.sigmoid(pre)
        d_gates.append(
            (d_hidden * upper * logistic * (1.0 + pre * (1.0 - logistic))).astype(jnp.bfloat16)
        )
        d_ups.append((d_hidden * pre * logistic).astype(jnp.bfloat16))
    d_out = jnp.concatenate(
        [
            dot_t(d_gates[0], gates[0][k])
            + dot_t(d_ups[0], ups[0][k])
            + dot_t(d_gates[1], gates[1][k])
            + dot_t(d_ups[1], ups[1][k])
            for k in range(2)
        ],
        axis=1,
    )
    turned = jnp.concatenate([norm_gain[:, half:], norm_gain[:, :half]], axis=1)
    gain = jnp.where(me % 2 == 0, norm_gain, turned)
    d_out = gain * d_out
    bwd_received, bwd_near, bwd_own = send_back(d_out, experts, capacity)
    bwd_near_sums = to_section(bwd_own, -1)
    fwd_sums = send_sums(fwd_out, fwd_received, experts, capacity, 1)
    bwd_sums = send_sums(d_out, bwd_received, experts, capacity, -1)
    both = (fwd_received, bwd_received)
    fwd_second = to_section(after(fwd_near, *both), 1, lambda i: i ^ FAR)
    bwd_second = to_section(after(bwd_near, *both), -1, lambda i: i ^ FAR)
    fwd_back = (fwd_near_sums, fwd_second, *fwd_sums)
    bwd_back = (bwd_near_sums, bwd_second, *bwd_sums)

    (fwd_next,) = call(
        functools.partial(finish_kernel, experts, capacity),
        "finish",
        [(tokens, width)],
        SHORT,
        (fwd_pack, *fwd_back),
    )
    (bwd_next,) = call(
        functools.partial(finish_back_kernel, experts, capacity),
        "finish_back",
        [(tokens, width)],
        SHORT,
        (bwd_pack, *bwd_back),
    )
    return (fwd_next[None], bwd_next[None])


def solution(mesh):
    rows = P("pp", "ep", None)
    weights = P("pp", "ep", None, None)
    in_specs = (rows,) * 7 + (P("pp", None),) + (weights,) * 3
    return jax.shard_map(
        body, mesh=mesh, in_specs=in_specs, out_specs=(rows, rows), check_vma=False
    )
```

time: 187 us -> 140 us (0.75)
  waiting for transfers between devices: 118 us -> 81.6 us
  other arithmetic: 15.3 us -> 0.86 us
  Pallas kernels: 0 us -> 4.14 us
  starting transfers between devices: 30 us -> 27.4 us
    ppermute x15, waiting for transfers between devices: 61.4 us -> 45.6 us  [swap(): lax.ppermute(value, 'ep', [(i, i ^ bit) for i in range(lax.axis_size('ep'...]
    ppermute x11 -> x8, waiting for transfers between devices: 32.2 us -> 21.2 us  [to_section(): return lax.ppermute(value, ('pp', 'ep'), pairs)]
    ppermute x2, waiting for transfers between devices: 24 us -> 14.8 us  [to_expert(): lax.ppermute(value, 'ep', [(i, (i + SLICES * shift) % count) for i in ran...]
    ppermute x11 -> x8, starting transfers between devices: 14 us -> 9.38 us  [to_section(): return lax.ppermute(value, ('pp', 'ep'), pairs)]
    pallas_call x0 -> x5, Pallas kernels: none -> 4.14 us  [call(): pl.pallas_call(kernel, name=name, grid=(1,), out_shape=[jax.ShapeDtypeStr...]
    reduce_sum x6 -> x0, other arithmetic: 3.91 us -> none  [the longest x3 2.79 us: inverse_rms(): jnp.mean(widened * widened, axis=-1, keepdims=True) + 1e-06]
    dot_general x6 -> x0, matrix products: 3.36 us -> none  [place(): lax.dot_general(chooser, values, (((0,), (0,)), ((), ())), preferred_elem...]
    concatenate x5 -> x3, other arithmetic: 3.07 us -> 0.26 us  [joined(): jnp.concatenate([own, *map(part, mine), own_pair, *map(part, theirs)], ax...]
  transfers between devices with their start and end apart: 28 -> 25, of which waited for: 12 -> 12; matrix products, arithmetic and copies ran while one was open for 18% -> 12% of each run, Pallas kernels for 0% -> 2%
where the time goes in v2:
time: 140 us; the launch traced here: 139 us
  waiting for transfers between devices  81.6 us (58%)
  starting transfers between devices  27.4 us (20%)
  matrix products  18.1 us (13%)
  local copies, waits for them, and re-layouts  5.94 us (4%)
  Pallas kernels  4.14 us (3%)
    ppermute x15, waiting for transfers between devices, swap(): lax.ppermute(value, 'ep', [(i, i ^ bit) for i in range(lax.axis_size('ep'...  45.6 us
    ppermute x8, waiting for transfers between devices, to_section(): return lax.ppermute(value, ('pp', 'ep'), pairs)  21.2 us
    ppermute x2, waiting for transfers between devices, to_expert(): lax.ppermute(value, 'ep', [(i, (i + SLICES * shift) % count) for i in ran...  14.8 us
    ppermute x15, starting transfers between devices, swap(): lax.ppermute(value, 'ep', [(i, i ^ bit) for i in range(lax.axis_size('ep'...  12.8 us
    dot_general x20, matrix products, dot(): return jnp.dot(a, b, preferred_element_type=jnp.float32)  10.1 us
    ppermute x8, starting transfers between devices, to_section(): return lax.ppermute(value, ('pp', 'ep'), pairs)  9.38 us
    dot_general x12, matrix products, dot_t(): lax.dot_general(a, b, (((1,), (1,)), ((), ())), preferred_element_type=jn...  8.01 us
    ppermute x2, starting transfers between devices, to_expert(): lax.ppermute(value, 'ep', [(i, (i + SLICES * shift) % count) for i in ran...  5.17 us
  transfers between devices with their start and end apart: 25, of which 12 were waited for; matrix products, arithmetic and copies ran while one was open for 12% of the time, Pallas kernels for 2%

profile of v2, /device:TPU:0, one launch (start us, length us, event | category | flops | bytes accessed | tf_op | source)
XLA Modules:
  0.0 139.2 jit_solution(6906129402989881070)
XLA Ops:
  1.1 2.6 %collective-permute-start.3 = (bf16[256,1792]{1,0:T(8,128)(2,1)}, bf16[256,1792]{1,0:T(8,128)(2,1)}, u32[]{:S(2)}, u32[]{:S(2)}) collective-permute-start(bf16[256,1792]{1,0:T(8,128)(2,1)} %bitcast.77), channel_id=1, source_target_pairs={{0,2},{1,3},{2,0},{3,1},{4,6},{5,7},{6,4},{7,5},{8,10},{9,11},{10,... | collective-permute-start | bytes 2752520 | tf_op jit(solution)/shard_map/ppermute | solution.py:16
  7.4 1.6 %collective-permute-start = (bf16[64,3712]{1,0:T(8,128)(2,1)S(1)}, bf16[64,3712]{1,0:T(8,128)(2,1)S(1)}, u32[]{:S(2)}, u32[]{:S(2)}) collective-permute-start(bf16[64,3712]{1,0:T(8,128)(2,1)S(1)} %get-tuple-element.23), channel_id=1, source_target_pairs={{0,16},{1,17},{2,18},{3,19},{4,20},{5,21},{6,22},{7,23},{8,24},{9,... | collective-permute-start | bytes 1425416 | tf_op jit(solution)/shard_map/ppermute | solution.py:31
  9.0 2.6 %collective-permute-start.1 = (bf16[40,3584]{1,0:T(8,128)(2,1)S(1)}, bf16[40,3584]{1,0:T(8,128)(2,1)S(1)}, u32[]{:S(2)}, u32[]{:S(2)}) collective-permute-start(bf16[40,3584]{1,0:T(8,128)(2,1)S(1)} %get-tuple-element.25), channel_id=1, source_target_pairs={{0,8},{1,9},{2,10},{3,11},{4,12},{5,13},{6,14},{7,15},{8,0},{9,1},... | collective-permute-start | bytes 860168 | tf_op jit(solution)/shard_map/ppermute | solution.py:21
  11.5 1.6 %collective-permute-start.2 = (bf16[40,3584]{1,0:T(8,128)(2,1)S(1)}, bf16[40,3584]{1,0:T(8,128)(2,1)S(1)}, u32[]{:S(2)}, u32[]{:S(2)}) collective-permute-start(bf16[40,3584]{1,0:T(8,128)(2,1)S(1)} %get-tuple-element.24), channel_id=1, source_target_pairs={{0,4},{1,5},{2,6},{3,7},{4,0},{5,1},{6,2},{7,3},{8,12},{9,13},{10,... | collective-permute-start | bytes 860168 | tf_op jit(solution)/shard_map/ppermute | solution.py:16
  13.9 10.8 %collective-permute-done.1.refs_1_ = bf16[40,3584]{1,0:T(8,128)(2,1)S(1)} collective-permute-done((bf16[40,3584]{1,0:T(8,128)(2,1)S(1)}, bf16[40,3584]{1,0:T(8,128)(2,1)S(1)}, u32[]{:S(2)}, u32[]{:S(2)}) %collective-permute-start.1) | collective-permute-done | bytes 286752 | tf_op jit(solution)/shard_map/ppermute | solution.py:21
  28.7 2.6 %collective-permute-start.9 = (bf16[40,7168]{1,0:T(8,128)(2,1)S(1)}, bf16[40,7168]{1,0:T(8,128)(2,1)S(1)}, u32[]{:S(2)}, u32[]{:S(2)}) collective-permute-start(bf16[40,7168]{1,0:T(8,128)(2,1)S(1)} %get-tuple-element.33), channel_id=1, source_target_pairs={{0,8},{1,9},{2,10},{3,11},{4,12},{5,13},{6,14},{7,15},{8,0},{9,1},... | collective-permute-start | bytes 1720328 | tf_op jit(solution)/shard_map/ppermute | solution.py:21
  32.8 17.0 %collective-permute-done.5 = bf16[40,7168]{1,0:T(8,128)(2,1)} collective-permute-done((bf16[40,7168]{1,0:T(8,128)(2,1)S(1)}, bf16[40,7168]{1,0:T(8,128)(2,1)}, u32[]{:S(2)}, u32[]{:S(2)}) %collective-permute-start.5) | collective-permute-done | bytes 573472 | tf_op jit(solution)/shard_map/ppermute | solution.py:16
  51.0 1.6 %fusion.40 = f32[160,256]{1,0:T(8,128)S(1)} fusion(bf16[1792,256]{1,0:T(8,128)(2,1)} %collective-permute-done.4, bf16[160,3584]{1,0:T(8,128)(2,1)S(1)} %pad_maximum_fusion.1), kind=kOutput, calls=%fused_computation.63 | convolution fusion | flops 146800640 | bytes 1654784 | tf_op jit(solution)/shard_map/dot_general | solution.py:39
  53.0 4.0 %collective-permute-done.9 = bf16[40,7168]{1,0:T(8,128)(2,1)S(1)} collective-permute-done((bf16[40,7168]{1,0:T(8,128)(2,1)S(1)}, bf16[40,7168]{1,0:T(8,128)(2,1)S(1)}, u32[]{:S(2)}, u32[]{:S(2)}) %collective-permute-start.9) | collective-permute-done | bytes 573472 | tf_op jit(solution)/shard_map/ppermute | solution.py:21
  59.0 2.1 %collective-permute-start.14 = (bf16[40,3584]{1,0:T(8,128)(2,1)S(1)}, bf16[40,3584]{1,0:T(8,128)(2,1)S(1)}, u32[]{:S(2)}, u32[]{:S(2)}) collective-permute-start(bf16[40,3584]{1,0:T(8,128)(2,1)S(1)} %get-tuple-element.39), channel_id=1, source_target_pairs={{0,4},{1,5},{2,6},{3,7},{4,0},{5,1},{6,2},{7,3},{8,12},{9,13},{10,... | collective-permute-start | bytes 860168 | tf_op jit(solution)/shard_map/ppermute | solution.py:16
  62.0 11.0 %collective-permute-done.15 = bf16[40,7168]{1,0:T(8,128)(2,1)S(1)} collective-permute-done((bf16[40,7168]{1,0:T(8,128)(2,1)S(1)}, bf16[40,7168]{1,0:T(8,128)(2,1)S(1)}, u32[]{:S(2)}, u32[]{:S(2)}) %collective-permute-start.15) | collective-permute-done | bytes 573472 | tf_op jit(solution)/shard_map/ppermute | solution.py:16
  73.2 1.5 %fusion.26 = f32[160,256]{1,0:T(8,128)S(1)} fusion(bf16[1792,256]{1,0:T(8,128)(2,1)} %collective-permute-done.4, bf16[160,3584]{1,0:T(8,128)(2,1)S(1)} %pad_maximum_fusion.3), kind=kOutput, calls=%fused_computation.49 | convolution fusion | flops 146800640 | bytes 1654784 | tf_op jit(solution)/shard_map/dot_general | solution.py:39
  75.3 2.2 %collective-permute-done.14 = bf16[40,3584]{1,0:T(8,128)(2,1)S(1)} collective-permute-done((bf16[40,3584]{1,0:T(8,128)(2,1)S(1)}, bf16[40,3584]{1,0:T(8,128)(2,1)S(1)}, u32[]{:S(2)}, u32[]{:S(2)}) %collective-permute-start.14) | collective-permute-done | bytes 286752 | tf_op jit(solution)/shard_map/ppermute | solution.py:16
  80.8 3.0 %collective-permute-done.12 = bf16[1792,256]{1,0:T(8,128)(2,1)S(1)} collective-permute-done((bf16[1792,256]{1,0:T(8,128)(2,1)S(1)}, bf16[1792,256]{1,0:T(8,128)(2,1)S(1)}, u32[]{:S(2)}, u32[]{:S(2)}) %collective-permute-start.12) | collective-permute-done | bytes 917536 | tf_op jit(solution)/shard_map/ppermute | solution.py:16
  85.1 1.7 %multiply_convert_fusion = (bf16[160,256]{1,0:T(8,128)(2,1)S(1)}, f32[160,256]{1,0:T(8,128)S(1)}) fusion(f32[160,256]{1,0:T(8,128)S(1)} %convolution_add_fusion.5, f32[160,256]{1,0:T(8,128)S(1)} %fusion.16, bf16[256,1792]{1,0:T(8,128)(2,1)} %collective-permute-done.3, bf16[160,3584]{1,0:T(8,128)(2,1)S(1)} %pad_maximum_fusion.2), kind=kOutput, calls=%fused_computation.69 | convolution fusion | flops 147087360 | bytes 2064384 | tf_op jit(solution)/shard_map/dot_general | solution.py:43
  89.4 1.7 %fusion.2 = f32[160,1792]{1,0:T(8,128)S(1)} fusion(f32[160,1792]{1,0:T(8,128)S(1)} %fusion.72, f32[160,1792]{1,0:T(8,128)S(1)} %fusion.71, f32[160,1792]{1,0:T(8,128)S(1)} %fusion.70, bf16[160,256]{1,0:T(8,128)(2,1)S(1)} %fusion.10, bf16[1792,256]{1,0:T(8,128)(2,1)} %collective-permute-done.4), kind=kOutput, calls=%fused_computation.10 | convolution fusion | flops 147660800 | bytes 5586944 | tf_op jit(solution)/shard_map/dot_general | solution.py:43
  91.4 1.6 %collective-permute-start.22 = (bf16[40,3584]{1,0:T(8,128)(2,1)S(1)}, bf16[40,3584]{1,0:T(8,128)(2,1)S(1)}, u32[]{:S(2)}, u32[]{:S(2)}) collective-permute-start(bf16[40,3584]{1,0:T(8,128)(2,1)S(1)} %get-tuple-element.47), channel_id=1, source_target_pairs={{0,16},{1,17},{2,18},{3,19},{4,20},{5,21},{6,22},{7,23},{8,24},{9,... | collective-permute-start | bytes 860168 | tf_op jit(solution)/shard_map/ppermute | solution.py:31
  94.4 1.5 %convolution_add_fusion.4 = f32[160,1792]{1,0:T(8,128)S(1)} fusion(f32[160,1792]{1,0:T(8,128)S(1)} %fusion.59, bf16[160,256]{1,0:T(8,128)(2,1)S(1)} %multiply_convert_fusion.2, bf16[256,1792]{1,0:T(8,128)(2,1)} %collective-permute-done.3), kind=kOutput, calls=%fused_computation.9 | convolution fusion | flops 147087360 | bytes 3293184 | tf_op jit(solution)/shard_map/dot_general | solution.py:39
  96.1 2.0 %collective-permute-start.18 = (bf16[40,3584]{1,0:T(8,128)(2,1)S(1)}, bf16[40,3584]{1,0:T(8,128)(2,1)S(1)}, u32[]{:S(2)}, u32[]{:S(2)}) collective-permute-start(bf16[40,3584]{1,0:T(8,128)(2,1)S(1)} %get-tuple-element.49), channel_id=1, source_target_pairs={{0,4},{1,5},{2,6},{3,7},{4,0},{5,1},{6,2},{7,3},{8,12},{9,13},{10,... | collective-permute-start | bytes 860168 | tf_op jit(solution)/shard_map/ppermute | solution.py:16
  98.6 4.0 %collective-permute-done.19 = bf16[40,3584]{1,0:T(8,128)(2,1)S(1)} collective-permute-done((bf16[40,3584]{1,0:T(8,128)(2,1)S(1)}, bf16[40,3584]{1,0:T(8,128)(2,1)S(1)}, u32[]{:S(2)}, u32[]{:S(2)}) %collective-permute-start.19) | collective-permute-done | bytes 286752 | tf_op jit(solution)/shard_map/ppermute | solution.py:16
  103.9 8.2 %collective-permute-done.18 = bf16[40,3584]{1,0:T(8,128)(2,1)S(1)} collective-permute-done((bf16[40,3584]{1,0:T(8,128)(2,1)S(1)}, bf16[40,3584]{1,0:T(8,128)(2,1)S(1)}, u32[]{:S(2)}, u32[]{:S(2)}) %collective-permute-start.18) | collective-permute-done | bytes 286752 | tf_op jit(solution)/shard_map/ppermute | solution.py:16
  112.1 2.9 %collective-permute-start.23 = (bf16[40,3584]{1,0:T(8,128)(2,1)S(1)}, bf16[40,3584]{1,0:T(8,128)(2,1)S(1)}, u32[]{:S(2)}, u32[]{:S(2)}) collective-permute-start(bf16[40,3584]{1,0:T(8,128)(2,1)S(1)} %get-tuple-element.43), channel_id=1, source_target_pairs={{0,20},{1,21},{2,22},{3,23},{4,16},{5,17},{6,18},{7,19},{8,28},{9,... | collective-permute-start | bytes 860168 | tf_op jit(solution)/shard_map/ppermute | solution.py:31
  115.2 3.1 %collective-permute-done.24.rest_2_ = bf16[40,3584]{1,0:T(8,128)(2,1)S(1)} collective-permute-done((bf16[40,3584]{1,0:T(8,128)(2,1)S(1)}, bf16[40,3584]{1,0:T(8,128)(2,1)S(1)}, u32[]{:S(2)}, u32[]{:S(2)}) %collective-permute-start.24) | collective-permute-done | bytes 286752 | tf_op jit(solution)/shard_map/ppermute | solution.py:31
  118.3 18.1 %collective-permute-done.23.rest_1_ = bf16[40,3584]{1,0:T(8,128)(2,1)S(1)} collective-permute-done((bf16[40,3584]{1,0:T(8,128)(2,1)S(1)}, bf16[40,3584]{1,0:T(8,128)(2,1)S(1)}, u32[]{:S(2)}, u32[]{:S(2)}) %collective-permute-start.23) | collective-permute-done | bytes 286752 | tf_op jit(solution)/shard_map/ppermute | solution.py:31
  (115 shorter events, 29.4 us)
Async XLA Ops:
  0.6 24.3 %collective-permute-start.4 = (bf16[1792,256]{1,0:T(8,128)(2,1)}, bf16[1792,256]{1,0:T(8,128)(2,1)}, u32[]{:S(2)}, u32[]{:S(2)}) collective-permute-start(bf16[1792,256]{1,0:T(8,128)(2,1)} %bitcast.75), channel_id=1, source_target_pairs={{0,1},{1,0},{2,3},{3,2},{4,5},{5,4},{6,7},{7,6},{8,9},{9,8},{10,11... | collective-permute-start | bytes 2752520 | tf_op jit(solution)/shard_map/ppermute | solution.py:16
  1.1 23.9 %collective-permute-start.3 = (bf16[256,1792]{1,0:T(8,128)(2,1)}, bf16[256,1792]{1,0:T(8,128)(2,1)}, u32[]{:S(2)}, u32[]{:S(2)}) collective-permute-start(bf16[256,1792]{1,0:T(8,128)(2,1)} %bitcast.77), channel_id=1, source_target_pairs={{0,2},{1,3},{2,0},{3,1},{4,6},{5,7},{6,4},{7,5},{8,10},{9,11},{10,... | collective-permute-start | bytes 2752520 | tf_op jit(solution)/shard_map/ppermute | solution.py:16
  7.4 17.5 %collective-permute-start = (bf16[64,3712]{1,0:T(8,128)(2,1)S(1)}, bf16[64,3712]{1,0:T(8,128)(2,1)S(1)}, u32[]{:S(2)}, u32[]{:S(2)}) collective-permute-start(bf16[64,3712]{1,0:T(8,128)(2,1)S(1)} %get-tuple-element.23), channel_id=1, source_target_pairs={{0,16},{1,17},{2,18},{3,19},{4,20},{5,21},{6,22},{7,23},{8,24},{9,... | collective-permute-start | bytes 1425416 | tf_op jit(solution)/shard_map/ppermute | solution.py:31
  9.0 15.8 %collective-permute-start.1 = (bf16[40,3584]{1,0:T(8,128)(2,1)S(1)}, bf16[40,3584]{1,0:T(8,128)(2,1)S(1)}, u32[]{:S(2)}, u32[]{:S(2)}) collective-permute-start(bf16[40,3584]{1,0:T(8,128)(2,1)S(1)} %get-tuple-element.25), channel_id=1, source_target_pairs={{0,8},{1,9},{2,10},{3,11},{4,12},{5,13},{6,14},{7,15},{8,0},{9,1},... | collective-permute-start | bytes 860168 | tf_op jit(solution)/shard_map/ppermute | solution.py:21
  11.5 13.4 %collective-permute-start.2 = (bf16[40,3584]{1,0:T(8,128)(2,1)S(1)}, bf16[40,3584]{1,0:T(8,128)(2,1)S(1)}, u32[]{:S(2)}, u32[]{:S(2)}) collective-permute-start(bf16[40,3584]{1,0:T(8,128)(2,1)S(1)} %get-tuple-element.24), channel_id=1, source_target_pairs={{0,4},{1,5},{2,6},{3,7},{4,0},{5,1},{6,2},{7,3},{8,12},{9,13},{10,... | collective-permute-start | bytes 860168 | tf_op jit(solution)/shard_map/ppermute | solution.py:16
  25.8 24.0 %collective-permute-start.5 = (bf16[40,7168]{1,0:T(8,128)(2,1)S(1)}, bf16[40,7168]{1,0:T(8,128)(2,1)}, u32[]{:S(2)}, u32[]{:S(2)}) collective-permute-start(bf16[40,7168]{1,0:T(8,128)(2,1)S(1)} %join.1), channel_id=1, source_target_pairs={{0,4},{1,5},{2,6},{3,7},{4,0},{5,1},{6,2},{7,3},{8,12},{9,13},{10,... | collective-permute-start | bytes 1720328 | tf_op jit(solution)/shard_map/ppermute | solution.py:16
  27.3 29.7 %collective-permute-start.6 = (bf16[1792,256]{1,0:T(8,128)(2,1)}, bf16[1792,256]{1,0:T(8,128)(2,1)S(1)}, u32[]{:S(2)}, u32[]{:S(2)}) collective-permute-start(bf16[1792,256]{1,0:T(8,128)(2,1)} %bitcast.79), channel_id=1, source_target_pairs={{0,1},{1,0},{2,3},{3,2},{4,5},{5,4},{6,7},{7,6},{8,9},{9,8},{10,11... | collective-permute-start | bytes 2752520 | tf_op jit(solution)/shard_map/ppermute | solution.py:16
  27.4 29.7 %collective-permute-start.7 = (bf16[1792,256]{1,0:T(8,128)(2,1)}, bf16[1792,256]{1,0:T(8,128)(2,1)S(1)}, u32[]{:S(2)}, u32[]{:S(2)}) collective-permute-start(bf16[1792,256]{1,0:T(8,128)(2,1)} %bitcast.76), channel_id=1, source_target_pairs={{0,2},{1,3},{2,0},{3,1},{4,6},{5,7},{6,4},{7,5},{8,10},{9,11},{10,... | collective-permute-start | bytes 2752520 | tf_op jit(solution)/shard_map/ppermute | solution.py:16
  28.7 28.3 %collective-permute-start.9 = (bf16[40,7168]{1,0:T(8,128)(2,1)S(1)}, bf16[40,7168]{1,0:T(8,128)(2,1)S(1)}, u32[]{:S(2)}, u32[]{:S(2)}) collective-permute-start(bf16[40,7168]{1,0:T(8,128)(2,1)S(1)} %get-tuple-element.33), channel_id=1, source_target_pairs={{0,8},{1,9},{2,10},{3,11},{4,12},{5,13},{6,14},{7,15},{8,0},{9,1},... | collective-permute-start | bytes 1720328 | tf_op jit(solution)/shard_map/ppermute | solution.py:21
  31.3 25.8 %collective-permute-start.8 = (bf16[64,7296]{1,0:T(8,128)(2,1)S(1)}, bf16[64,7296]{1,0:T(8,128)(2,1)S(1)}, u32[]{:S(2)}, u32[]{:S(2)}) collective-permute-start(bf16[64,7296]{1,0:T(8,128)(2,1)S(1)} %get-tuple-element.31), channel_id=1, source_target_pairs={{0,16},{1,17},{2,18},{3,19},{4,20},{5,21},{6,22},{7,23},{8,24},{9,... | collective-permute-start | bytes 2801672 | tf_op jit(solution)/shard_map/ppermute | solution.py:31
  57.0 16.0 %collective-permute-start.15 = (bf16[40,7168]{1,0:T(8,128)(2,1)S(1)}, bf16[40,7168]{1,0:T(8,128)(2,1)S(1)}, u32[]{:S(2)}, u32[]{:S(2)}) collective-permute-start(bf16[40,7168]{1,0:T(8,128)(2,1)S(1)} %collective-permute-done.9), channel_id=1, source_target_pairs={{0,4},{1,5},{2,6},{3,7},{4,0},{5,1},{6,2},{7,3},{8,12},{9,13},{10,... | collective-permute-start | bytes 1720328 | tf_op jit(solution)/shard_map/ppermute | solution.py:16
  59.0 18.5 %collective-permute-start.14 = (bf16[40,3584]{1,0:T(8,128)(2,1)S(1)}, bf16[40,3584]{1,0:T(8,128)(2,1)S(1)}, u32[]{:S(2)}, u32[]{:S(2)}) collective-permute-start(bf16[40,3584]{1,0:T(8,128)(2,1)S(1)} %get-tuple-element.39), channel_id=1, source_target_pairs={{0,4},{1,5},{2,6},{3,7},{4,0},{5,1},{6,2},{7,3},{8,12},{9,13},{10,... | collective-permute-start | bytes 860168 | tf_op jit(solution)/shard_map/ppermute | solution.py:16
  61.0 16.5 %collective-permute-start.10 = (bf16[256,1792]{1,0:T(8,128)(2,1)}, bf16[256,1792]{1,0:T(8,128)(2,1)S(1)}, u32[]{:S(2)}, u32[]{:S(2)}) collective-permute-start(bf16[256,1792]{1,0:T(8,128)(2,1)} %collective-permute-done.3), channel_id=1, source_target_pairs={{0,1},{1,0},{2,3},{3,2},{4,5},{5,4},{6,7},{7,6},{8,9},{9,8},{10,11... | collective-permute-start | bytes 2752520 | tf_op jit(solution)/shard_map/ppermute | solution.py:16
  61.0 22.8 %collective-permute-start.12 = (bf16[1792,256]{1,0:T(8,128)(2,1)S(1)}, bf16[1792,256]{1,0:T(8,128)(2,1)S(1)}, u32[]{:S(2)}, u32[]{:S(2)}) collective-permute-start(bf16[1792,256]{1,0:T(8,128)(2,1)S(1)} %bitcast.80), channel_id=1, source_target_pairs={{0,2},{1,3},{2,0},{3,1},{4,6},{5,7},{6,4},{7,5},{8,10},{9,11},{10,... | collective-permute-start | bytes 2752520 | tf_op jit(solution)/shard_map/ppermute | solution.py:16
  61.8 15.9 %collective-permute-start.13 = (bf16[256,1792]{1,0:T(8,128)(2,1)S(1)}, bf16[256,1792]{1,0:T(8,128)(2,1)S(1)}, u32[]{:S(2)}, u32[]{:S(2)}) collective-permute-start(bf16[256,1792]{1,0:T(8,128)(2,1)S(1)} %bitcast.78), channel_id=1, source_target_pairs={{0,1},{1,0},{2,3},{3,2},{4,5},{5,4},{6,7},{7,6},{8,9},{9,8},{10,11... | collective-permute-start | bytes 2752520 | tf_op jit(solution)/shard_map/ppermute | solution.py:16
  77.6 6.2 %collective-permute-start.11 = (bf16[1792,256]{1,0:T(8,128)(2,1)S(1)}, bf16[1792,256]{1,0:T(8,128)(2,1)S(1)}, u32[]{:S(2)}, u32[]{:S(2)}) collective-permute-start(bf16[1792,256]{1,0:T(8,128)(2,1)S(1)} %collective-permute-done.7), channel_id=1, source_target_pairs={{0,1},{1,0},{2,3},{3,2},{4,5},{5,4},{6,7},{7,6},{8,9},{9,8},{10,11... | collective-permute-start | bytes 2752520 | tf_op jit(solution)/shard_map/ppermute | solution.py:16
  91.4 23.7 %collective-permute-start.22 = (bf16[40,3584]{1,0:T(8,128)(2,1)S(1)}, bf16[40,3584]{1,0:T(8,128)(2,1)S(1)}, u32[]{:S(2)}, u32[]{:S(2)}) collective-permute-start(bf16[40,3584]{1,0:T(8,128)(2,1)S(1)} %get-tuple-element.47), channel_id=1, source_target_pairs={{0,16},{1,17},{2,18},{3,19},{4,20},{5,21},{6,22},{7,23},{8,24},{9,... | collective-permute-start | bytes 860168 | tf_op jit(solution)/shard_map/ppermute | solution.py:31
  93.0 9.7 %collective-permute-start.19 = (bf16[40,3584]{1,0:T(8,128)(2,1)S(1)}, bf16[40,3584]{1,0:T(8,128)(2,1)S(1)}, u32[]{:S(2)}, u32[]{:S(2)}) collective-permute-start(bf16[40,3584]{1,0:T(8,128)(2,1)S(1)} %get-tuple-element.48), channel_id=1, source_target_pairs={{0,4},{1,5},{2,6},{3,7},{4,0},{5,1},{6,2},{7,3},{8,12},{9,13},{10,... | collective-permute-start | bytes 860168 | tf_op jit(solution)/shard_map/ppermute | solution.py:16
  96.1 16.0 %collective-permute-start.18 = (bf16[40,3584]{1,0:T(8,128)(2,1)S(1)}, bf16[40,3584]{1,0:T(8,128)(2,1)S(1)}, u32[]{:S(2)}, u32[]{:S(2)}) collective-permute-start(bf16[40,3584]{1,0:T(8,128)(2,1)S(1)} %get-tuple-element.49), channel_id=1, source_target_pairs={{0,4},{1,5},{2,6},{3,7},{4,0},{5,1},{6,2},{7,3},{8,12},{9,13},{10,... | collective-permute-start | bytes 860168 | tf_op jit(solution)/shard_map/ppermute | solution.py:16
  98.1 39.8 %collective-permute-start.17 = (bf16[40,3584]{1,0:T(8,128)(2,1)S(1)}, bf16[40,3584]{1,0:T(8,128)(2,1)S(1)}, u32[]{:S(2)}, u32[]{:S(2)}) collective-permute-start(bf16[40,3584]{1,0:T(8,128)(2,1)S(1)} %get-tuple-element.51), channel_id=1, source_target_pairs={{0,16},{1,17},{2,18},{3,19},{4,20},{5,21},{6,22},{7,23},{8,24},{9,... | collective-permute-start | bytes 860168 | tf_op jit(solution)/shard_map/ppermute | solution.py:31
  102.7 15.6 %collective-permute-start.24 = (bf16[40,3584]{1,0:T(8,128)(2,1)S(1)}, bf16[40,3584]{1,0:T(8,128)(2,1)S(1)}, u32[]{:S(2)}, u32[]{:S(2)}) collective-permute-start(bf16[40,3584]{1,0:T(8,128)(2,1)S(1)} %fusion.15), channel_id=1, source_target_pairs={{0,24},{1,25},{2,26},{3,27},{4,28},{5,29},{6,30},{7,31},{8,16},{9,... | collective-permute-start | bytes 860168 | tf_op jit(solution)/shard_map/ppermute | solution.py:31
  112.1 25.7 %collective-permute-start.20 = (bf16[40,3584]{1,0:T(8,128)(2,1)S(1)}, bf16[40,3584]{1,0:T(8,128)(2,1)S(1)}, u32[]{:S(2)}, u32[]{:S(2)}) collective-permute-start(bf16[40,3584]{1,0:T(8,128)(2,1)S(1)} %get-tuple-element.42), channel_id=1, source_target_pairs={{0,20},{1,21},{2,22},{3,23},{4,16},{5,17},{6,18},{7,19},{8,28},{9,... | collective-permute-start | bytes 860168 | tf_op jit(solution)/shard_map/ppermute | solution.py:31
  112.1 24.2 %collective-permute-start.23 = (bf16[40,3584]{1,0:T(8,128)(2,1)S(1)}, bf16[40,3584]{1,0:T(8,128)(2,1)S(1)}, u32[]{:S(2)}, u32[]{:S(2)}) collective-permute-start(bf16[40,3584]{1,0:T(8,128)(2,1)S(1)} %get-tuple-element.43), channel_id=1, source_target_pairs={{0,20},{1,21},{2,22},{3,23},{4,16},{5,17},{6,18},{7,19},{8,28},{9,... | collective-permute-start | bytes 860168 | tf_op jit(solution)/shard_map/ppermute | solution.py:31
  115.1 22.7 %collective-permute-start.21 = (bf16[40,3584]{1,0:T(8,128)(2,1)S(1)}, bf16[40,3584]{1,0:T(8,128)(2,1)S(1)}, u32[]{:S(2)}, u32[]{:S(2)}) collective-permute-start(bf16[40,3584]{1,0:T(8,128)(2,1)S(1)} %fusion.14), channel_id=1, source_target_pairs={{0,24},{1,25},{2,26},{3,27},{4,28},{5,29},{6,30},{7,31},{8,16},{9,... | collective-permute-start | bytes 860168 | tf_op jit(solution)/shard_map/ppermute | solution.py:31
  (20 other events, 127.3 us)

commit v3 on v2

--- a/solution.py
+++ b/solution.py
@@ -9,7 +9,8 @@
 
 SLICES = 8
 NEAR, SIDE, FAR = 1, 2, 4
-SHORT, LONG = 10**9, 2 * 10**11
+SHORT, LONG = 10**6, 2 * 10**11
+FULL = 58 * 2**20
 
 
 def swap(value, bit):
@@ -47,25 +48,84 @@
     return lax.dot_general(a, b, (((0,), (0,)), ((), ())), preferred_element_type=jnp.float32)
 
 
-def call(kernel, name, outs, cost, args):
-    def whole(shape):
-        return pl.BlockSpec(shape, lambda i: (0, 0))
-
+def call(kernel, name, outs, cost, args, held=4, scratch=()):
+    space = pl.BlockSpec(memory_space=pltpu.VMEM)
     return pl.pallas_call(
         kernel,
         name=name,
-        grid=(1,),
-        out_shape=[jax.ShapeDtypeStruct(shape, jnp.bfloat16) for shape in outs],
-        in_specs=[whole(arg.shape) for arg in args],
-        out_specs=[whole(shape) for shape in outs],
+        out_shape=[jax.ShapeDtypeStruct(shape, kind) for shape, kind in outs],
+        in_specs=[space] * len(args),
+        out_specs=[space] * len(outs),
+        scratch_shapes=list(scratch),
         cost_estimate=pl.CostEstimate(flops=cost, bytes_accessed=0, transcendentals=0),
-        compiler_params=pltpu.CompilerParams(vmem_limit_bytes=24 * 2**20),
+        compiler_params=pltpu.CompilerParams(vmem_limit_bytes=held * 2**20),
+    )(*args)
+
+
+def call_fetching(kernel, name, outs, cost, args):
+    count = len(args)
+
+    def fetching(*refs):
+        sources, rest = refs[:count], refs[count : count + len(outs)]
+        held, sems = refs[count + len(outs) : -1], refs[-1]
+        copies = [
+            pltpu.make_async_copy(source, target, sems.at[i])
+            for i, (source, target) in enumerate(zip(sources, held))
+        ]
+        for copy in copies:
+            copy.start()
+        for copy in copies:
+            copy.wait()
+        kernel(*held, *rest)
+
+    return pl.pallas_call(
+        fetching,
+        name=name,
+        out_shape=[jax.ShapeDtypeStruct(shape, kind) for shape, kind in outs],
+        in_specs=[pl.BlockSpec(memory_space=pltpu.HBM)] * count,
+        out_specs=[pl.BlockSpec(memory_space=pltpu.VMEM)] * len(outs),
+        scratch_shapes=[pltpu.VMEM(arg.shape, arg.dtype) for arg in args]
+        + [pltpu.SemaphoreType.DMA((count,))],
+        cost_estimate=pl.CostEstimate(flops=cost, bytes_accessed=0, transcendentals=0),
+        compiler_params=pltpu.CompilerParams(vmem_limit_bytes=FULL),
     )(*args)
 
 
 def my_place():
     me = lax.axis_index("ep")
     return me // SLICES, me % 2
+
+
+def split_kernel(gate_ref, up_ref, large_ref, small_ref, sems):
+    half, cut = gate_ref.shape[0], up_ref.shape[0] - small_ref.shape[0]
+    copies = [
+        pltpu.make_async_copy(gate_ref, large_ref.at[pl.ds(0, half)], sems.at[0]),
+        pltpu.make_async_copy(up_ref.at[pl.ds(0, cut)], large_ref.at[pl.ds(half, cut)], sems.at[1]),
+        pltpu.make_async_copy(up_ref.at[pl.ds(cut, half - cut)], small_ref, sems.at[2]),
+    ]
+    for copy in copies:
+        copy.start()
+    for copy in copies:
+        copy.wait()
+
+
+def split_weights(gate, up):
+    half, units = up.shape
+    cut = -(-half // 512) * 128
+    anywhere = pl.BlockSpec(memory_space=pl.ANY)
+    return pl.pallas_call(
+        split_kernel,
+        name="split_weights",
+        out_shape=[
+            jax.ShapeDtypeStruct((half + cut, units), up.dtype),
+            jax.ShapeDtypeStruct((half - cut, units), up.dtype),
+        ],
+        in_specs=[anywhere] * 2,
+        out_specs=[anywhere] * 2,
+        scratch_shapes=[pltpu.SemaphoreType.DMA((3,))],
+        cost_estimate=pl.CostEstimate(flops=SHORT, bytes_accessed=0, transcendentals=0),
+        compiler_params=pltpu.CompilerParams(vmem_limit_bytes=2 * 2**20),
+    )(gate, up)
 
 
 def slot_rows(route_ref, mine, experts, capacity):
@@ -160,9 +220,10 @@
 
 def join_kernel(*refs):
     *parts, out_ref = refs
-    width = parts[0].shape[1]
-    for i, part in enumerate(parts):
-        out_ref[:, i * width : (i + 1) * width] = part[...]
+    start = 0
+    for part in parts:
+        out_ref[:, start : start + part.shape[1]] = part[...]
+        start += part.shape[1]
 
 
 def collected(chooser, core, back, capacity, k):
@@ -212,16 +273,108 @@
         ).astype(jnp.bfloat16)
 
 
-def send_back(partial, experts, capacity):
-    near = partial[experts * capacity :].astype(jnp.bfloat16)
-    return swap(near[capacity:], FAR), near[:capacity], partial[:capacity].astype(jnp.bfloat16)
-
-
-def send_sums(partial, received, experts, capacity, step):
+def up_rows(block, half, begin, end):
+    large, small, _ = block
+    cut = large.shape[0] - half
+    return large[half + begin : half + end] if begin < cut else small[begin - cut : end - cut]
+
+
+def row_ranges(blocks, half):
+    cut = max(block[0].shape[0] - half for block in blocks)
+    return ((0, cut), (cut, half)) if cut else ((0, half),)
+
+
+def activations(x_ref, blocks):
+    half = x_ref.shape[1] // 2
+    pre, upper = 0.0, 0.0
+    for k, block in enumerate(blocks):
+        first = k * half
+        pre = pre + dot(x_ref[:, first : first + half], block[0][:half])
+        for begin, end in row_ranges(blocks, half):
+            columns = slice(first + begin, first + end)
+            upper = upper + dot(x_ref[:, columns], up_rows(block, half, begin, end))
+    return pre, upper
+
+
+def stack_rows(out_ref, pieces):
+    width = out_ref.shape[1]
+    step = width // 4
+    for first in range(0, width, step):
+        parts = [ref[:, at + first : at + first + step].astype(jnp.float32) for ref, at in pieces]
+        out_ref[:, first : first + step] = jnp.concatenate(parts, axis=0).astype(jnp.bfloat16)
+
+
+def forward_near_kernel(experts, *refs):
+    *near, pair_ref = refs[: experts + 2]
+    blocks = refs[experts + 2 : experts + 5], refs[experts + 5 : experts + 8]
+    x_ref, part_ref = refs[experts + 8 :]
+    pieces = [(ref, 0) for ref in near]
+    stack_rows(x_ref, pieces + [(pair_ref, r * x_ref.shape[1]) for r in range(experts - 1)])
+    pre, upper = activations(x_ref, blocks)
+    hidden = (jax.nn.silu(pre) * upper).astype(jnp.bfloat16)
+    half = x_ref.shape[1] // 2
+    for k in range(2):
+        part_ref[:, k * half : (k + 1) * half] = dot(hidden, blocks[k][2][...])
+
+
+def put_rows(capacity, total, first, own_ref, near_ref, cross_ref, far_ref):
+    columns = slice(first, first + total.shape[1])
+    count = total.shape[0] // 2
+    own_ref[:, columns] = total[:capacity].astype(jnp.bfloat16)
+    far_ref[:, columns] = total[capacity:count]
+    near_ref[:, columns] = total[count : count + capacity].astype(jnp.bfloat16)
+    cross_ref[:, columns] = total[count + capacity :].astype(jnp.bfloat16)
+
+
+def forward_side_kernel(capacity, x_ref, part_ref, *refs):
+    blocks, outs = (refs[:3], refs[3:6]), refs[6:]
+    pre, upper = activations(x_ref, blocks)
+    hidden = (jax.nn.silu(pre) * upper).astype(jnp.bfloat16)
+    half = x_ref.shape[1] // 2
+    for k in range(2):
+        total = part_ref[:, k * half : (k + 1) * half] + dot(hidden, blocks[k][2][...])
+        put_rows(capacity, total, k * half, *outs)
+
+
+def backward_kernel(experts, capacity, *refs):
+    core = my_place()[1]
+    first_ref, grad_ref, *far_refs = refs[: experts + 1]
+    pair_ref, rest_ref, gain_ref = refs[experts + 1 : experts + 4]
+    blocks = refs[experts + 4 : experts + 16]
+    *outs, x_ref, g_ref = refs[experts + 16 :]
+    sets = [(blocks[i : i + 3], blocks[i + 3 : i + 6]) for i in (0, 6)]
+    width = first_ref.shape[1]
+    half = width // 2
+    ahead = [(ref, 0) for ref in (first_ref, *far_refs)] + [(pair_ref, pair_ref.shape[1] - width)]
+    stack_rows(x_ref, ahead + [(rest_ref, (2 * r - 1) * width) for r in range(1, experts)])
+    behind = [(grad_ref, 0)] + [(ref, width) for ref in far_refs] + [(rest_ref, 0)]
+    stack_rows(g_ref, behind + [(rest_ref, 2 * r * width) for r in range(1, experts)])
+    steps = []
+    for blocks in sets:
+        pre, upper = activations(x_ref, blocks)
+        d_hidden = sum(
+            dot_t(g_ref[:, k * half : (k + 1) * half], blocks[k][2][...]) for k in range(2)
+        )
+        logistic = jax.nn.sigmoid(pre)
+        d_gate = d_hidden * upper * logistic * (1.0 + pre * (1.0 - logistic))
+        d_up = d_hidden * pre * logistic
+        steps.append((d_gate.astype(jnp.bfloat16), d_up.astype(jnp.bfloat16)))
+    for k in range(2):
+        for begin, end in row_ranges(sets[1], half):
+            total = 0.0
+            for (d_gate, d_up), blocks in zip(steps, sets):
+                upper = up_rows(blocks[k], half, begin, end)
+                total = total + dot_t(d_gate, blocks[k][0][begin:end]) + dot_t(d_up, upper)
+            start = half * (core if k == 0 else 1 - core) + begin
+            gain = gain_ref[:, pl.ds(pl.multiple_of(start, 128), end - begin)]
+            put_rows(capacity, gain * total, k * half + begin, *outs)
+
+
+def send_sums(far, received, experts, capacity, step):
     sums = []
     for r in range(1, experts):
-        part = received[(r - 1) * capacity : r * capacity].astype(jnp.float32)
-        summed = (partial[r * capacity : (r + 1) * capacity] + part).astype(jnp.bfloat16)
+        rows = slice((r - 1) * capacity, r * capacity)
+        summed = (far[rows] + received[rows].astype(jnp.float32)).astype(jnp.bfloat16)
         sums.append(to_section(summed, step, lambda i, r=r: i - SLICES * r))
     return sums
 
@@ -242,117 +395,108 @@
     experts = lax.axis_size("ep") // SLICES
     tokens, width = fwd_act.shape[1:]
     capacity = 2 * ((5 * tokens + 8 * experts - 1) // (8 * experts))
-    half = w_gate.shape[2]
     shifts = range(1, experts)
-    me = lax.axis_index("ep")
     gate, up, down = w_gate[0, 0], w_up[0, 0], w_down[0, 0]
     row = (1, tokens)
     lanes = -(-(experts * capacity + 3) // 128) * 128
-    slots = (capacity, width)
-    two_slots = (capacity, 2 * width)
-
+    slots = ((capacity, width), jnp.bfloat16)
+    two_slots = ((capacity, 2 * width), jnp.bfloat16)
+
+    large, small = split_weights(gate, up)
     side_down = swap(down, SIDE)
+    near_down = swap(down, NEAR)
     near_gate = swap(gate, NEAR)
-    fwd_pack, *fwd_groups = call(
+    fwd_pack, *fwd_groups = call_fetching(
         functools.partial(prepare_kernel, experts, capacity),
         "prepare",
-        [(tokens, width + lanes)] + [slots] * experts,
+        [((tokens, width + lanes), jnp.bfloat16)] + [slots] * experts,
         LONG,
         (fwd_route.reshape(row), fwd_gate.reshape(row), fwd_act[0], norm_gain),
     )
     fwd_far = [to_expert(fwd_groups[r], r) for r in shifts]
-    own_pairs = [swap(fwd_groups[0], FAR)]
-    fwd_pack = to_section(fwd_pack, 1)
+    first_pair = swap(fwd_groups[0], FAR)
     bwd_pack, bwd_first, grad_first, *bwd_groups = call(
         functools.partial(prepare_back_kernel, experts, capacity),
         "prepare_back",
-        [(tokens, 2 * width + lanes), slots, slots] + [two_slots] * (experts - 1),
+        [((tokens, 2 * width + lanes), jnp.bfloat16), slots, slots] + [two_slots] * (experts - 1),
         SHORT,
         (bwd_route.reshape(row), bwd_gate.reshape(row), bwd_act[0], bwd_grad[0], norm_gain),
-    )
-
-    first = (side_down, near_gate, fwd_pack, own_pairs[0], *fwd_far)
+        held=8,
+    )
+
+    first = (side_down, near_down, near_gate, first_pair, bwd_first, large, *fwd_far)
+    fwd_pack = to_section(after(fwd_pack, *first), 1)
     near_up = swap(after(up, *first), NEAR)
-    bwd_pack = to_section(after(bwd_pack, *first), -1)
     (mixed,) = call(
         join_kernel,
         "join",
-        [(capacity, experts * width)],
+        [((capacity, experts * width), jnp.bfloat16)],
+        SHORT,
+        (*after(tuple(fwd_far), *first), bwd_first),
+    )
+    own_pair = swap(mixed, FAR)
+    side_large = swap(after(large, *first), SIDE)
+    bwd_far = [to_expert(after(bwd_groups[r - 1], *first), r) for r in shifts]
+
+    (rest,) = call(
+        join_kernel,
+        "join_back",
+        [((capacity, (2 * experts - 1) * width), jnp.bfloat16)],
         LONG,
-        (after(bwd_first, *first), *fwd_far),
-    )
-    mixed_pair = swap(mixed, FAR)
-    own_pairs.append(mixed_pair[:, :width])
-    fwd_far_pair = [mixed_pair[:, r * width : (r + 1) * width] for r in shifts]
-    side_gate = swap(after(gate, *first), SIDE)
-    bwd_far = [to_expert(after(bwd_groups[r - 1], *first), r) for r in shifts]
-
-    second = (side_gate, near_up, bwd_pack, mixed_pair, *bwd_far)
+        (after(grad_first, side_large), *bwd_far),
+    )
+    second = (rest, fwd_pack, near_up, own_pair)
+    rest_pair = swap(rest, FAR)
+    bwd_pack = to_section(after(bwd_pack, *second), -1)
+    side_small = swap(after(small, *second), SIDE)
+    side_near_large = swap(after(side_large, *second), NEAR)
     side_near_down = swap(after(side_down, *second), NEAR)
-    near_down = swap(after(down, *second), NEAR)
-    side_near_gate = swap(after(side_gate, side_near_down), NEAR)
-    own_pairs.append(swap(after(grad_first, *second), FAR))
-    bwd_far_pair = [swap(after(part, *second), FAR) for part in bwd_far]
-    side_up = swap(after(up, *second), SIDE)
-    third = (side_up, near_down, side_near_gate, own_pairs[2], *bwd_far_pair)
-    side_near_up = swap(after(side_up, *third), NEAR)
-
-    gates = [[gate, near_gate], [side_gate, side_near_gate]]
-    ups = [[up, near_up], [side_up, side_near_up]]
-    downs = [[down, near_down], [side_down, side_near_down]]
-
-    def joined(own, mine, own_pair, theirs, at):
-        def part(value):
-            return value[:, at * width : (at + 1) * width]
-
-        return jnp.concatenate([own, *map(part, mine), own_pair, *map(part, theirs)], axis=0)
-
-    fwd_x = joined(fwd_groups[0], fwd_far, own_pairs[0], fwd_far_pair, 0)
-    bwd_x = joined(bwd_first, bwd_far, own_pairs[1], bwd_far_pair, 0)
-    bwd_g = joined(grad_first, bwd_far, own_pairs[2], bwd_far_pair, 1)
-
-    def project(rows, pair):
-        return dot(rows[:, :half], pair[0]) + dot(rows[:, half:], pair[1])
-
-    hidden = []
-    for j in range(2):
-        pre = project(fwd_x, gates[j])
-        hidden.append((jax.nn.silu(pre) * project(fwd_x, ups[j])).astype(jnp.bfloat16))
-    fwd_out = jnp.concatenate(
-        [dot(hidden[0], downs[0][k]) + dot(hidden[1], downs[1][k]) for k in range(2)], axis=1
-    )
-    fwd_received, fwd_near, fwd_own = send_back(fwd_out, experts, capacity)
+    mine = ((gate, up, down), (near_gate, near_up, near_down))
+
+    rows = (2 * experts * capacity, width)
+    far = ((experts - 1) * capacity, width)
+    outs = [slots, slots, (far, jnp.bfloat16), (far, jnp.float32)]
+    pieces = after((fwd_groups[0], *fwd_far, first_pair, own_pair), rest, side_near_down)
+    fwd_x, part = call(
+        functools.partial(forward_near_kernel, experts),
+        "forward_near",
+        [(rows, jnp.bfloat16), (rows, jnp.float32)],
+        SHORT,
+        (*pieces, *mine[0], *mine[1]),
+        held=6,
+    )
+    side_near_small = swap(after(side_small, part, side_near_large), NEAR)
+    beside = ((side_large, side_small, side_down), (side_near_large, side_near_small, side_near_down))
+    fwd_own, fwd_near, fwd_cross, fwd_sum = call(
+        functools.partial(forward_side_kernel, capacity),
+        "forward_side",
+        outs,
+        SHORT,
+        (fwd_x, part, *beside[0], *beside[1]),
+        held=6,
+    )
+    fwd_own, fwd_near, fwd_cross, fwd_sum, rest_pair, bwd_pack = lax.optimization_barrier(
+        (fwd_own, fwd_near, fwd_cross, fwd_sum, rest_pair, bwd_pack)
+    )
+    fwd_received = swap(fwd_cross, FAR)
     fwd_near_sums = to_section(fwd_own, 1)
-
-    d_gates, d_ups = [], []
-    for j in range(2):
-        pre = project(bwd_x, gates[j])
-        upper = project(bwd_x, ups[j])
-        d_hidden = dot_t(bwd_g[:, :half], downs[j][0]) + dot_t(bwd_g[:, half:], downs[j][1])
-        logistic = jax.nn.sigmoid(pre)
-        d_gates.append(
-            (d_hidden * upper * logistic * (1.0 + pre * (1.0 - logistic))).astype(jnp.bfloat16)
-        )
-        d_ups.append((d_hidden * pre * logistic).astype(jnp.bfloat16))
-    d_out = jnp.concatenate(
-        [
-            dot_t(d_gates[0], gates[0][k])
-            + dot_t(d_ups[0], ups[0][k])
-            + dot_t(d_gates[1], gates[1][k])
-            + dot_t(d_ups[1], ups[1][k])
-            for k in range(2)
-        ],
-        axis=1,
-    )
-    turned = jnp.concatenate([norm_gain[:, half:], norm_gain[:, :half]], axis=1)
-    gain = jnp.where(me % 2 == 0, norm_gain, turned)
-    d_out = gain * d_out
-    bwd_received, bwd_near, bwd_own = send_back(d_out, experts, capacity)
-    bwd_near_sums = to_section(bwd_own, -1)
-    fwd_sums = send_sums(fwd_out, fwd_received, experts, capacity, 1)
-    bwd_sums = send_sums(d_out, bwd_received, experts, capacity, -1)
+    fwd_second = to_section(fwd_near, 1, lambda i: i ^ FAR)
+
+    bwd_own, bwd_near, bwd_cross, bwd_sum = call(
+        functools.partial(backward_kernel, experts, capacity),
+        "backward",
+        outs,
+        SHORT,
+        (bwd_first, grad_first, *bwd_far, own_pair, rest_pair, norm_gain)
+        + (*mine[0], *mine[1], *beside[0], *beside[1]),
+        held=10,
+        scratch=(pltpu.VMEM(rows, jnp.bfloat16),) * 2,
+    )
+    bwd_received = swap(bwd_cross, FAR)
+    fwd_sums = send_sums(fwd_sum, fwd_received, experts, capacity, 1)
+    bwd_near_sums = to_section(after(bwd_own, fwd_received), -1)
+    bwd_sums = send_sums(bwd_sum, bwd_received, experts, capacity, -1)
     both = (fwd_received, bwd_received)
-    fwd_second = to_section(after(fwd_near, *both), 1, lambda i: i ^ FAR)
     bwd_second = to_section(after(bwd_near, *both), -1, lambda i: i ^ FAR)
     fwd_back = (fwd_near_sums, fwd_second, *fwd_sums)
     bwd_back = (bwd_near_sums, bwd_second, *bwd_sums)
@@ -360,16 +504,18 @@
     (fwd_next,) = call(
         functools.partial(finish_kernel, experts, capacity),
         "finish",
-        [(tokens, width)],
+        [((tokens, width), jnp.bfloat16)],
         SHORT,
         (fwd_pack, *fwd_back),
+        held=8,
     )
     (bwd_next,) = call(
         functools.partial(finish_back_kernel, experts, capacity),
         "finish_back",
-        [(tokens, width)],
+        [((tokens, width), jnp.bfloat16)],
         SHORT,
         (bwd_pack, *bwd_back),
+        held=8,
     )
     return (fwd_next[None], bwd_next[None])
 

time: 140 us -> 123 us (0.88)
  Pallas kernels: 4.14 us -> 23.1 us
  matrix products: 18.1 us -> 0 us
  waiting for transfers between devices: 81.6 us -> 68.7 us
  local copies, waits for them, and re-layouts: 5.94 us -> 1.98 us
    pallas_call x5 -> x10, Pallas kernels: 4.14 us -> 23.1 us  [the longest x8 19.1 us: call(): pl.pallas_call(kernel, name=name, out_shape=[jax.ShapeDtypeStruct(shape,...]
    dot_general x32 -> x0, matrix products: 18.1 us -> none  [the longest x20 10.1 us: dot(): return jnp.dot(a, b, preferred_element_type=jnp.float32)]
    ppermute x8, waiting for transfers between devices: 21.2 us -> 10.5 us  [to_section(): return lax.ppermute(value, ('pp', 'ep'), pairs)]
    ppermute x8, starting transfers between devices: 9.38 us -> 13.4 us  [to_section(): return lax.ppermute(value, ('pp', 'ep'), pairs)]
    ppermute x15 -> x14, starting transfers between devices: 12.8 us -> 9.36 us  [swap(): lax.ppermute(value, 'ep', [(i, i ^ bit) for i in range(lax.axis_size('ep'...]
    ppermute x2, waiting for transfers between devices: 14.8 us -> 11.5 us  [to_expert(): lax.ppermute(value, 'ep', [(i, (i + SLICES * shift) % count) for i in ran...]
    unnamed x38 -> x30, local copies, waits for them, and re-layouts: 4.66 us -> 1.98 us
    ppermute x15 -> x14, waiting for transfers between devices: 45.6 us -> 46.7 us  [swap(): lax.ppermute(value, 'ep', [(i, i ^ bit) for i in range(lax.axis_size('ep'...]
  transfers between devices with their start and end apart: 25 -> 24, of which waited for: 12 -> 13; matrix products, arithmetic and copies ran while one was open for 12% -> 0% of each run, Pallas kernels for 2% -> 18%
where the time goes in v3:
time: 123 us
  waiting for transfers between devices  68.7 us (56%)
  starting transfers between devices  28 us (23%)
  Pallas kernels  23.1 us (19%)
  local copies, waits for them, and re-layouts  1.98 us (2%)
    ppermute x14, waiting for transfers between devices, swap(): lax.ppermute(value, 'ep', [(i, i ^ bit) for i in range(lax.axis_size('ep'...  46.7 us
    pallas_call x8, Pallas kernels, call(): pl.pallas_call(kernel, name=name, out_shape=[jax.ShapeDtypeStruct(shape,...  19.1 us
    ppermute x8, starting transfers between devices, to_section(): return lax.ppermute(value, ('pp', 'ep'), pairs)  13.4 us
    ppermute x2, waiting for transfers between devices, to_expert(): lax.ppermute(value, 'ep', [(i, (i + SLICES * shift) % count) for i in ran...  11.5 us
    ppermute x8, waiting for transfers between devices, to_section(): return lax.ppermute(value, ('pp', 'ep'), pairs)  10.5 us
    ppermute x14, starting transfers between devices, swap(): lax.ppermute(value, 'ep', [(i, i ^ bit) for i in range(lax.axis_size('ep'...  9.36 us
    ppermute x2, starting transfers between devices, to_expert(): lax.ppermute(value, 'ep', [(i, (i + SLICES * shift) % count) for i in ran...  5.24 us
    pallas_call x1, Pallas kernels, call_fetching(): pl.pallas_call(fetching, name=name, out_shape=[jax.ShapeDtypeStruct(shape...  2.55 us
  transfers between devices with their start and end apart: 24, of which 13 were waited for; matrix products, arithmetic and copies ran while one was open for 0% of the time, Pallas kernels for 18%

profile of v3, /device:TPU:0, one launch (start us, length us, event | category | flops | bytes accessed | tf_op | source)
XLA Modules:
  0.0 122.8 jit_solution(12738730630367450591)
XLA Ops:
  1.1 2.6 %collective-permute-start = (bf16[256,1792]{1,0:T(8,128)(2,1)}, bf16[256,1792]{1,0:T(8,128)(2,1)}, u32[]{:S(2)}, u32[]{:S(2)}) collective-permute-start(bf16[256,1792]{1,0:T(8,128)(2,1)} %bitcast.17), channel_id=1, source_target_pairs={{0,2},{1,3},{2,0},{3,1},{4,6},{5,7},{6,4},{7,5},{8,10},{9,11},{10,... | collective-permute-start | bytes 2752520 | tf_op jit(solution)/shard_map/ppermute | solution.py:17
  3.9 2.5 %prepare.1 = (bf16[64,3712]{1,0:T(8,128)(2,1)}, bf16[40,3584]{1,0:T(8,128)(2,1)}, bf16[40,3584]{1,0:T(8,128)(2,1)}) custom-call(s32[1,64]{1,0:T(1,128)} %bitcast.27, f32[1,64]{1,0:T(1,128)} %bitcast.28, bf16[64,3584]{1,0:T(8,128)(2,1)} %bitcast.26, f32[1,3584]{1,0:T(1,128)} %refs_5_.1), custom_call_target="tpu_custom_call" | custom-call | flops 199999995904 | tf_op jit(solution)/shard_map/prepare/pallas_call | solution.py:81
  6.5 2.7 %collective-permute-start.4 = (bf16[40,3584]{1,0:T(8,128)(2,1)}, bf16[40,3584]{1,0:T(8,128)(2,1)S(1)}, u32[]{:S(2)}, u32[]{:S(2)}) collective-permute-start(bf16[40,3584]{1,0:T(8,128)(2,1)} %get-tuple-element.48), channel_id=1, source_target_pairs={{0,8},{1,9},{2,10},{3,11},{4,12},{5,13},{6,14},{7,15},{8,0},{9,1},... | collective-permute-start | bytes 860168 | tf_op jit(solution)/shard_map/ppermute | solution.py:22
  9.2 1.6 %collective-permute-start.3 = (bf16[40,3584]{1,0:T(8,128)(2,1)}, bf16[40,3584]{1,0:T(8,128)(2,1)S(1)}, u32[]{:S(2)}, u32[]{:S(2)}) collective-permute-start(bf16[40,3584]{1,0:T(8,128)(2,1)} %get-tuple-element.58.refs_0_), channel_id=1, source_target_pairs={{0,4},{1,5},{2,6},{3,7},{4,0},{5,1},{6,2},{7,3},{8,12},{9,13},{10,... | collective-permute-start | bytes 860168 | tf_op jit(solution)/shard_map/ppermute | solution.py:17
  13.0 10.0 %collective-permute-done.4.refs_0_.refs_1_ = bf16[40,3584]{1,0:T(8,128)(2,1)S(1)} collective-permute-done((bf16[40,3584]{1,0:T(8,128)(2,1)}, bf16[40,3584]{1,0:T(8,128)(2,1)S(1)}, u32[]{:S(2)}, u32[]{:S(2)}) %collective-permute-start.4) | collective-permute-done | bytes 286752 | tf_op jit(solution)/shard_map/ppermute | solution.py:22
  23.2 1.8 %collective-permute-done.refs_2_.refs_14_ = bf16[256,1792]{1,0:T(8,128)(2,1)} collective-permute-done((bf16[256,1792]{1,0:T(8,128)(2,1)}, bf16[256,1792]{1,0:T(8,128)(2,1)}, u32[]{:S(2)}, u32[]{:S(2)}) %collective-permute-start) | collective-permute-done | bytes 917536 | tf_op jit(solution)/shard_map/ppermute | solution.py:17
  25.0 1.8 %collective-permute-start.7 = (bf16[2304,256]{1,0:T(8,128)(2,1)S(1)}, bf16[2304,256]{1,0:T(8,128)(2,1)}, u32[]{:S(2)}, u32[]{:S(2)}) collective-permute-start(bf16[2304,256]{1,0:T(8,128)(2,1)S(1)} %get-tuple-element.52), channel_id=1, source_target_pairs={{0,2},{1,3},{2,0},{3,1},{4,6},{5,7},{6,4},{7,5},{8,10},{9,11},{10,... | collective-permute-start | bytes 3538952 | tf_op jit(solution)/shard_map/ppermute | solution.py:17
  26.8 2.6 %collective-permute-start.8 = (bf16[40,7168]{1,0:T(8,128)(2,1)S(1)}, bf16[40,7168]{1,0:T(8,128)(2,1)S(1)}, u32[]{:S(2)}, u32[]{:S(2)}) collective-permute-start(bf16[40,7168]{1,0:T(8,128)(2,1)S(1)} %get-tuple-element.55), channel_id=1, source_target_pairs={{0,8},{1,9},{2,10},{3,11},{4,12},{5,13},{6,14},{7,15},{8,0},{9,1},... | collective-permute-start | bytes 1720328 | tf_op jit(solution)/shard_map/ppermute | solution.py:22
  31.7 1.6 %collective-permute-start.6 = (bf16[40,7168]{1,0:T(8,128)(2,1)}, bf16[40,7168]{1,0:T(8,128)(2,1)}, u32[]{:S(2)}, u32[]{:S(2)}) collective-permute-start(bf16[40,7168]{1,0:T(8,128)(2,1)} %join.1), channel_id=1, source_target_pairs={{0,4},{1,5},{2,6},{3,7},{4,0},{5,1},{6,2},{7,3},{8,12},{9,13},{10,... | collective-permute-start | bytes 1720328 | tf_op jit(solution)/shard_map/ppermute | solution.py:17
  33.3 19.6 %collective-permute-done.7.refs_0_.refs_12_ = bf16[2304,256]{1,0:T(8,128)(2,1)} collective-permute-done((bf16[2304,256]{1,0:T(8,128)(2,1)S(1)}, bf16[2304,256]{1,0:T(8,128)(2,1)}, u32[]{:S(2)}, u32[]{:S(2)}) %collective-permute-start.7) | collective-permute-done | bytes 1179680 | tf_op jit(solution)/shard_map/ppermute | solution.py:17
  54.4 2.5 %collective-permute-done.6.refs_3_ = bf16[40,7168]{1,0:T(8,128)(2,1)} collective-permute-done((bf16[40,7168]{1,0:T(8,128)(2,1)}, bf16[40,7168]{1,0:T(8,128)(2,1)}, u32[]{:S(2)}, u32[]{:S(2)}) %collective-permute-start.6) | collective-permute-done | bytes 573472 | tf_op jit(solution)/shard_map/ppermute | solution.py:17
  58.6 2.7 %collective-permute-done.10.refs_5_.refs_17_ = bf16[256,1792]{1,0:T(8,128)(2,1)S(1)} collective-permute-done((bf16[256,1792]{1,0:T(8,128)(2,1)}, bf16[256,1792]{1,0:T(8,128)(2,1)S(1)}, u32[]{:S(2)}, u32[]{:S(2)}) %collective-permute-start.10) | collective-permute-done | bytes 917536 | tf_op jit(solution)/shard_map/ppermute | solution.py:17
  63.2 3.4 %forward_near.1 = (bf16[160,3584]{1,0:T(8,128)(2,1)S(1)}, f32[160,3584]{1,0:T(8,128)S(1)}) custom-call(bf16[40,3584]{1,0:T(8,128)(2,1)S(1)} %copy-done.8, bf16[40,3584]{1,0:T(8,128)(2,1)S(1)} %copy-done.3, bf16[40,3584]{1,0:T(8,128)(2,1)S(1)} %copy-done.10, bf16[40,7168]{1,0:T(8,128)(2,1)} %collective-permute-done.6.refs_3_, bf16[1792,256]{1,0:T(8,128)(2,1)S(1)} %bitcast.14, ...), custom_call_target="tpu_custom_call" | custom-call | flops 1000000 | tf_op jit(solution)/shard_map/forward_near/pallas_call | solution.py:53
  66.5 7.5 %collective-permute-done.11.refs_1_.refs_13_ = bf16[1280,256]{1,0:T(8,128)(2,1)S(1)} collective-permute-done((bf16[1280,256]{1,0:T(8,128)(2,1)S(1)}, bf16[1280,256]{1,0:T(8,128)(2,1)S(1)}, u32[]{:S(2)}, u32[]{:S(2)}) %collective-permute-start.11) | collective-permute-done | bytes 655392 | tf_op jit(solution)/shard_map/ppermute | solution.py:17
  74.0 2.1 %collective-permute-done.13.refs_4_.refs_16_ = bf16[1280,256]{1,0:T(8,128)(2,1)S(1)} collective-permute-done((bf16[1280,256]{1,0:T(8,128)(2,1)S(1)}, bf16[1280,256]{1,0:T(8,128)(2,1)S(1)}, u32[]{:S(2)}, u32[]{:S(2)}) %collective-permute-start.13) | collective-permute-done | bytes 655392 | tf_op jit(solution)/shard_map/ppermute | solution.py:17
  76.1 2.8 %forward_side.1 = (bf16[40,3584]{1,0:T(8,128)(2,1)S(1)}, bf16[40,3584]{1,0:T(8,128)(2,1)S(1)}, bf16[40,3584]{1,0:T(8,128)(2,1)S(1)}, f32[40,3584]{1,0:T(8,128)S(1)}) custom-call(bf16[160,3584]{1,0:T(8,128)(2,1)S(1)} %get-tuple-element.62.x_ref, f32[160,3584]{1,0:T(8,128)S(1)} %get-tuple-element.63.part_ref, ...), custom_call_target="tpu_custom_call" | custom-call | flops 1000000 | tf_op jit(solution)/shard_map/forward_side/pallas_call | solution.py:53
  80.9 2.8 %collective-permute-start.17 = (bf16[40,3584]{1,0:T(8,128)(2,1)S(1)}, bf16[40,3584]{1,0:T(8,128)(2,1)S(1)}, u32[]{:S(2)}, u32[]{:S(2)}) collective-permute-start(bf16[40,3584]{1,0:T(8,128)(2,1)S(1)} %get-tuple-element.75), channel_id=1, source_target_pairs={{0,20},{1,21},{2,22},{3,23},{4,16},{5,17},{6,18},{7,19},{8,28},{9,... | collective-permute-start | bytes 860168 | tf_op jit(solution)/shard_map/ppermute | solution.py:32
  83.7 7.5 %backward.1 = (bf16[40,3584]{1,0:T(8,128)(2,1)S(1)}, bf16[40,3584]{1,0:T(8,128)(2,1)S(1)}, bf16[40,3584]{1,0:T(8,128)(2,1)S(1)}, f32[40,3584]{1,0:T(8,128)S(1)}) custom-call(bf16[40,3584]{1,0:T(8,128)(2,1)S(1)} %copy-done.5, bf16[40,3584]{1,0:T(8,128)(2,1)S(1)} %get-tuple-element.53.refs_0_.refs_1_, ...), custom_call_target="tpu_custom_call" | custom-call | flops 1000000 | tf_op jit(solution)/shard_map/backward/pallas_call | solution.py:53
  92.0 3.8 %collective-permute-start.19 = (bf16[40,3584]{1,0:T(8,128)(2,1)S(1)}, bf16[40,3584]{1,0:T(8,128)(2,1)S(1)}, u32[]{:S(2)}, u32[]{:S(2)}) collective-permute-start(bf16[40,3584]{1,0:T(8,128)(2,1)S(1)} %add_convert_fusion.1), channel_id=1, source_target_pairs={{0,24},{1,25},{2,26},{3,27},{4,28},{5,29},{6,30},{7,31},{8,16},{9,... | collective-permute-start | bytes 860168 | tf_op jit(solution)/shard_map/ppermute | solution.py:32
  95.8 10.5 %collective-permute-done.21 = bf16[40,3584]{1,0:T(8,128)(2,1)S(1)} collective-permute-done((bf16[40,3584]{1,0:T(8,128)(2,1)S(1)}, bf16[40,3584]{1,0:T(8,128)(2,1)S(1)}, u32[]{:S(2)}, u32[]{:S(2)}) %collective-permute-start.21) | collective-permute-done | bytes 286752 | tf_op jit(solution)/shard_map/ppermute | solution.py:17
  106.4 3.4 %collective-permute-start.23 = (bf16[40,3584]{1,0:T(8,128)(2,1)S(1)}, bf16[40,3584]{1,0:T(8,128)(2,1)S(1)}, u32[]{:S(2)}, u32[]{:S(2)}) collective-permute-start(bf16[40,3584]{1,0:T(8,128)(2,1)S(1)} %add_convert_fusion), channel_id=1, source_target_pairs={{0,24},{1,25},{2,26},{3,27},{4,28},{5,29},{6,30},{7,31},{8,16},{9,... | collective-permute-start | bytes 860168 | tf_op jit(solution)/shard_map/ppermute | solution.py:32
  109.8 2.3 %finish.1 = bf16[64,3584]{1,0:T(8,128)(2,1)} custom-call(bf16[64,3712]{1,0:T(8,128)(2,1)} %collective-permute-done.5.pack_ref, bf16[40,3584]{1,0:T(8,128)(2,1)S(1)} %collective-permute-done.16.rest_0_, bf16[40,3584]{1,0:T(8,128)(2,1)S(1)} %collective-permute-done.17.rest_1_, bf16[40,3584]{1,0:T(8,128)(2,1)S(1)} %collective-permute-done.19.rest_2_), custom_call_target="tpu_custom_call" | custom-call | flops 1000000 | tf_op jit(solution)/shard_map/finish/pallas_call | solution.py:53
  112.1 6.5 %collective-permute-done.22.rest_1_ = bf16[40,3584]{1,0:T(8,128)(2,1)S(1)} collective-permute-done((bf16[40,3584]{1,0:T(8,128)(2,1)S(1)}, bf16[40,3584]{1,0:T(8,128)(2,1)S(1)}, u32[]{:S(2)}, u32[]{:S(2)}) %collective-permute-start.22) | collective-permute-done | bytes 286752 | tf_op jit(solution)/shard_map/ppermute | solution.py:32
  118.6 2.7 %collective-permute-done.23.rest_2_ = bf16[40,3584]{1,0:T(8,128)(2,1)S(1)} collective-permute-done((bf16[40,3584]{1,0:T(8,128)(2,1)S(1)}, bf16[40,3584]{1,0:T(8,128)(2,1)S(1)}, u32[]{:S(2)}, u32[]{:S(2)}) %collective-permute-start.23) | collective-permute-done | bytes 286752 | tf_op jit(solution)/shard_map/ppermute | solution.py:32
  (66 shorter events, 14.9 us)
Async XLA Ops:
  0.6 22.6 %collective-permute-start.1 = (bf16[256,1792]{1,0:T(8,128)(2,1)}, bf16[256,1792]{1,0:T(8,128)(2,1)}, u32[]{:S(2)}, u32[]{:S(2)}) collective-permute-start(bf16[256,1792]{1,0:T(8,128)(2,1)} %bitcast.16), channel_id=1, source_target_pairs={{0,1},{1,0},{2,3},{3,2},{4,5},{5,4},{6,7},{7,6},{8,9},{9,8},{10,11... | collective-permute-start | bytes 2752520 | tf_op jit(solution)/shard_map/ppermute | solution.py:17
  1.1 23.9 %collective-permute-start = (bf16[256,1792]{1,0:T(8,128)(2,1)}, bf16[256,1792]{1,0:T(8,128)(2,1)}, u32[]{:S(2)}, u32[]{:S(2)}) collective-permute-start(bf16[256,1792]{1,0:T(8,128)(2,1)} %bitcast.17), channel_id=1, source_target_pairs={{0,2},{1,3},{2,0},{3,1},{4,6},{5,7},{6,4},{7,5},{8,10},{9,11},{10,... | collective-permute-start | bytes 2752520 | tf_op jit(solution)/shard_map/ppermute | solution.py:17
  3.7 19.5 %collective-permute-start.2 = (bf16[1792,256]{1,0:T(8,128)(2,1)}, bf16[1792,256]{1,0:T(8,128)(2,1)}, u32[]{:S(2)}, u32[]{:S(2)}) collective-permute-start(bf16[1792,256]{1,0:T(8,128)(2,1)} %bitcast.12), channel_id=1, source_target_pairs={{0,1},{1,0},{2,3},{3,2},{4,5},{5,4},{6,7},{7,6},{8,9},{9,8},{10,11... | collective-permute-start | bytes 2752520 | tf_op jit(solution)/shard_map/ppermute | solution.py:17
  6.5 16.5 %collective-permute-start.4 = (bf16[40,3584]{1,0:T(8,128)(2,1)}, bf16[40,3584]{1,0:T(8,128)(2,1)S(1)}, u32[]{:S(2)}, u32[]{:S(2)}) collective-permute-start(bf16[40,3584]{1,0:T(8,128)(2,1)} %get-tuple-element.48), channel_id=1, source_target_pairs={{0,8},{1,9},{2,10},{3,11},{4,12},{5,13},{6,14},{7,15},{8,0},{9,1},... | collective-permute-start | bytes 860168 | tf_op jit(solution)/shard_map/ppermute | solution.py:22
  9.2 14.0 %collective-permute-start.3 = (bf16[40,3584]{1,0:T(8,128)(2,1)}, bf16[40,3584]{1,0:T(8,128)(2,1)S(1)}, u32[]{:S(2)}, u32[]{:S(2)}) collective-permute-start(bf16[40,3584]{1,0:T(8,128)(2,1)} %get-tuple-element.58.refs_0_), channel_id=1, source_target_pairs={{0,4},{1,5},{2,6},{3,7},{4,0},{5,1},{6,2},{7,3},{8,12},{9,13},{10,... | collective-permute-start | bytes 860168 | tf_op jit(solution)/shard_map/ppermute | solution.py:17
  25.0 27.8 %collective-permute-start.7 = (bf16[2304,256]{1,0:T(8,128)(2,1)S(1)}, bf16[2304,256]{1,0:T(8,128)(2,1)}, u32[]{:S(2)}, u32[]{:S(2)}) collective-permute-start(bf16[2304,256]{1,0:T(8,128)(2,1)S(1)} %get-tuple-element.52), channel_id=1, source_target_pairs={{0,2},{1,3},{2,0},{3,1},{4,6},{5,7},{6,4},{7,5},{8,10},{9,11},{10,... | collective-permute-start | bytes 3538952 | tf_op jit(solution)/shard_map/ppermute | solution.py:17
  26.8 27.5 %collective-permute-start.8 = (bf16[40,7168]{1,0:T(8,128)(2,1)S(1)}, bf16[40,7168]{1,0:T(8,128)(2,1)S(1)}, u32[]{:S(2)}, u32[]{:S(2)}) collective-permute-start(bf16[40,7168]{1,0:T(8,128)(2,1)S(1)} %get-tuple-element.55), channel_id=1, source_target_pairs={{0,8},{1,9},{2,10},{3,11},{4,12},{5,13},{6,14},{7,15},{8,0},{9,1},... | collective-permute-start | bytes 1720328 | tf_op jit(solution)/shard_map/ppermute | solution.py:22
  29.3 25.1 %collective-permute-start.5 = (bf16[64,3712]{1,0:T(8,128)(2,1)}, bf16[64,3712]{1,0:T(8,128)(2,1)}, u32[]{:S(2)}, u32[]{:S(2)}) collective-permute-start(bf16[64,3712]{1,0:T(8,128)(2,1)} %get-tuple-element.49), channel_id=1, source_target_pairs={{0,16},{1,17},{2,18},{3,19},{4,20},{5,21},{6,22},{7,23},{8,24},{9,... | collective-permute-start | bytes 1425416 | tf_op jit(solution)/shard_map/ppermute | solution.py:32
  31.7 25.2 %collective-permute-start.6 = (bf16[40,7168]{1,0:T(8,128)(2,1)}, bf16[40,7168]{1,0:T(8,128)(2,1)}, u32[]{:S(2)}, u32[]{:S(2)}) collective-permute-start(bf16[40,7168]{1,0:T(8,128)(2,1)} %join.1), channel_id=1, source_target_pairs={{0,4},{1,5},{2,6},{3,7},{4,0},{5,1},{6,2},{7,3},{8,12},{9,13},{10,... | collective-permute-start | bytes 1720328 | tf_op jit(solution)/shard_map/ppermute | solution.py:17
  33.3 23.6 %collective-permute-start.9 = (bf16[1792,256]{1,0:T(8,128)(2,1)}, bf16[1792,256]{1,0:T(8,128)(2,1)}, u32[]{:S(2)}, u32[]{:S(2)}) collective-permute-start(bf16[1792,256]{1,0:T(8,128)(2,1)} %bitcast.9.up_ref.refs_5_.refs_7_), channel_id=1, source_target_pairs={{0,1},{1,0},{2,3},{3,2},{4,5},{5,4},{6,7},{7,6},{8,9},{9,8},{10,11... | collective-permute-start | bytes 2752520 | tf_op jit(solution)/shard_map/ppermute | solution.py:17
  56.9 17.2 %collective-permute-start.12 = (bf16[2304,256]{1,0:T(8,128)(2,1)}, bf16[2304,256]{1,0:T(8,128)(2,1)S(1)}, u32[]{:S(2)}, u32[]{:S(2)}) collective-permute-start(bf16[2304,256]{1,0:T(8,128)(2,1)} %collective-permute-done.7.refs_0_.refs_12_), channel_id=1, source_target_pairs={{0,1},{1,0},{2,3},{3,2},{4,5},{5,4},{6,7},{7,6},{8,9},{9,8},{10,11... | collective-permute-start | bytes 3538952 | tf_op jit(solution)/shard_map/ppermute | solution.py:17
  56.9 4.4 %collective-permute-start.10 = (bf16[256,1792]{1,0:T(8,128)(2,1)}, bf16[256,1792]{1,0:T(8,128)(2,1)S(1)}, u32[]{:S(2)}, u32[]{:S(2)}) collective-permute-start(bf16[256,1792]{1,0:T(8,128)(2,1)} %collective-permute-done.refs_2_.refs_14_), channel_id=1, source_target_pairs={{0,1},{1,0},{2,3},{3,2},{4,5},{5,4},{6,7},{7,6},{8,9},{9,8},{10,11... | collective-permute-start | bytes 2752520 | tf_op jit(solution)/shard_map/ppermute | solution.py:17
  57.4 16.6 %collective-permute-start.11 = (bf16[1280,256]{1,0:T(8,128)(2,1)S(1)}, bf16[1280,256]{1,0:T(8,128)(2,1)S(1)}, u32[]{:S(2)}, u32[]{:S(2)}) collective-permute-start(bf16[1280,256]{1,0:T(8,128)(2,1)S(1)} %get-tuple-element.65), channel_id=1, source_target_pairs={{0,2},{1,3},{2,0},{3,1},{4,6},{5,7},{6,4},{7,5},{8,10},{9,11},{10,... | collective-permute-start | bytes 1966088 | tf_op jit(solution)/shard_map/ppermute | solution.py:17
  57.9 22.3 %collective-permute-start.15 = (bf16[64,7296]{1,0:T(8,128)(2,1)S(1)}, bf16[64,7296]{1,0:T(8,128)(2,1)S(1)}, u32[]{:S(2)}, u32[]{:S(2)}) collective-permute-start(bf16[64,7296]{1,0:T(8,128)(2,1)S(1)} %get-tuple-element.73), channel_id=1, source_target_pairs={{0,16},{1,17},{2,18},{3,19},{4,20},{5,21},{6,22},{7,23},{8,24},{9,... | collective-permute-start | bytes 2801672 | tf_op jit(solution)/shard_map/ppermute | solution.py:32
  58.4 20.5 %collective-permute-start.14 = (bf16[40,10752]{1,0:T(8,128)(2,1)S(1)}, bf16[40,10752]{1,0:T(8,128)(2,1)S(1)}, u32[]{:S(2)}, u32[]{:S(2)}) collective-permute-start(bf16[40,10752]{1,0:T(8,128)(2,1)S(1)} %join_back.1), channel_id=1, source_target_pairs={{0,4},{1,5},{2,6},{3,7},{4,0},{5,1},{6,2},{7,3},{8,12},{9,13},{10,... | collective-permute-start | bytes 2580488 | tf_op jit(solution)/shard_map/ppermute | solution.py:17
  74.0 2.1 %collective-permute-start.13 = (bf16[1280,256]{1,0:T(8,128)(2,1)S(1)}, bf16[1280,256]{1,0:T(8,128)(2,1)S(1)}, u32[]{:S(2)}, u32[]{:S(2)}) collective-permute-start(bf16[1280,256]{1,0:T(8,128)(2,1)S(1)} %collective-permute-done.11.refs_1_.refs_13_), channel_id=1, source_target_pairs={{0,1},{1,0},{2,3},{3,2},{4,5},{5,4},{6,7},{7,6},{8,9},{9,8},{10,11... | collective-permute-start | bytes 1966088 | tf_op jit(solution)/shard_map/ppermute | solution.py:17
  80.2 11.1 %collective-permute-start.18 = (bf16[40,3584]{1,0:T(8,128)(2,1)S(1)}, bf16[40,3584]{1,0:T(8,128)(2,1)S(1)}, u32[]{:S(2)}, u32[]{:S(2)}) collective-permute-start(bf16[40,3584]{1,0:T(8,128)(2,1)S(1)} %get-tuple-element.77), channel_id=1, source_target_pairs={{0,4},{1,5},{2,6},{3,7},{4,0},{5,1},{6,2},{7,3},{8,12},{9,13},{10,... | collective-permute-start | bytes 860168 | tf_op jit(solution)/shard_map/ppermute | solution.py:17
  80.2 26.2 %collective-permute-start.16 = (bf16[40,3584]{1,0:T(8,128)(2,1)S(1)}, bf16[40,3584]{1,0:T(8,128)(2,1)S(1)}, u32[]{:S(2)}, u32[]{:S(2)}) collective-permute-start(bf16[40,3584]{1,0:T(8,128)(2,1)S(1)} %get-tuple-element.74), channel_id=1, source_target_pairs={{0,16},{1,17},{2,18},{3,19},{4,20},{5,21},{6,22},{7,23},{8,24},{9,... | collective-permute-start | bytes 860168 | tf_op jit(solution)/shard_map/ppermute | solution.py:32
  80.9 28.9 %collective-permute-start.17 = (bf16[40,3584]{1,0:T(8,128)(2,1)S(1)}, bf16[40,3584]{1,0:T(8,128)(2,1)S(1)}, u32[]{:S(2)}, u32[]{:S(2)}) collective-permute-start(bf16[40,3584]{1,0:T(8,128)(2,1)S(1)} %get-tuple-element.75), channel_id=1, source_target_pairs={{0,20},{1,21},{2,22},{3,23},{4,16},{5,17},{6,18},{7,19},{8,28},{9,... | collective-permute-start | bytes 860168 | tf_op jit(solution)/shard_map/ppermute | solution.py:32
  91.2 15.1 %collective-permute-start.21 = (bf16[40,3584]{1,0:T(8,128)(2,1)S(1)}, bf16[40,3584]{1,0:T(8,128)(2,1)S(1)}, u32[]{:S(2)}, u32[]{:S(2)}) collective-permute-start(bf16[40,3584]{1,0:T(8,128)(2,1)S(1)} %get-tuple-element.83), channel_id=1, source_target_pairs={{0,4},{1,5},{2,6},{3,7},{4,0},{5,1},{6,2},{7,3},{8,12},{9,13},{10,... | collective-permute-start | bytes 860168 | tf_op jit(solution)/shard_map/ppermute | solution.py:17
  91.3 20.8 %collective-permute-start.20 = (bf16[40,3584]{1,0:T(8,128)(2,1)S(1)}, bf16[40,3584]{1,0:T(8,128)(2,1)S(1)}, u32[]{:S(2)}, u32[]{:S(2)}) collective-permute-start(bf16[40,3584]{1,0:T(8,128)(2,1)S(1)} %get-tuple-element.81), channel_id=1, source_target_pairs={{0,16},{1,17},{2,18},{3,19},{4,20},{5,21},{6,22},{7,23},{8,24},{9,... | collective-permute-start | bytes 860168 | tf_op jit(solution)/shard_map/ppermute | solution.py:32
  92.0 17.7 %collective-permute-start.19 = (bf16[40,3584]{1,0:T(8,128)(2,1)S(1)}, bf16[40,3584]{1,0:T(8,128)(2,1)S(1)}, u32[]{:S(2)}, u32[]{:S(2)}) collective-permute-start(bf16[40,3584]{1,0:T(8,128)(2,1)S(1)} %add_convert_fusion.1), channel_id=1, source_target_pairs={{0,24},{1,25},{2,26},{3,27},{4,28},{5,29},{6,30},{7,31},{8,16},{9,... | collective-permute-start | bytes 860168 | tf_op jit(solution)/shard_map/ppermute | solution.py:32
  106.3 12.3 %collective-permute-start.22 = (bf16[40,3584]{1,0:T(8,128)(2,1)S(1)}, bf16[40,3584]{1,0:T(8,128)(2,1)S(1)}, u32[]{:S(2)}, u32[]{:S(2)}) collective-permute-start(bf16[40,3584]{1,0:T(8,128)(2,1)S(1)} %get-tuple-element.84), channel_id=1, source_target_pairs={{0,20},{1,21},{2,22},{3,23},{4,16},{5,17},{6,18},{7,19},{8,28},{9,... | collective-permute-start | bytes 860168 | tf_op jit(solution)/shard_map/ppermute | solution.py:32
  106.4 14.9 %collective-permute-start.23 = (bf16[40,3584]{1,0:T(8,128)(2,1)S(1)}, bf16[40,3584]{1,0:T(8,128)(2,1)S(1)}, u32[]{:S(2)}, u32[]{:S(2)}) collective-permute-start(bf16[40,3584]{1,0:T(8,128)(2,1)S(1)} %add_convert_fusion), channel_id=1, source_target_pairs={{0,24},{1,25},{2,26},{3,27},{4,28},{5,29},{6,30},{7,31},{8,16},{9,... | collective-permute-start | bytes 860168 | tf_op jit(solution)/shard_map/ppermute | solution.py:32
  (15 other events, 170.2 us)

commit v4 on v3

--- a/solution.py
+++ b/solution.py
@@ -111,7 +111,7 @@
 
 def split_weights(gate, up):
     half, units = up.shape
-    cut = -(-half // 512) * 128
+    cut = half * 3 // 7 // 128 * 128
     anywhere = pl.BlockSpec(memory_space=pl.ANY)
     return pl.pallas_call(
         split_kernel,
@@ -405,7 +405,6 @@
     large, small = split_weights(gate, up)
     side_down = swap(down, SIDE)
     near_down = swap(down, NEAR)
-    near_gate = swap(gate, NEAR)
     fwd_pack, *fwd_groups = call_fetching(
         functools.partial(prepare_kernel, experts, capacity),
         "prepare",
@@ -415,6 +414,7 @@
     )
     fwd_far = [to_expert(fwd_groups[r], r) for r in shifts]
     first_pair = swap(fwd_groups[0], FAR)
+    fwd_pack = to_section(fwd_pack, 1)
     bwd_pack, bwd_first, grad_first, *bwd_groups = call(
         functools.partial(prepare_back_kernel, experts, capacity),
         "prepare_back",
@@ -424,8 +424,8 @@
         held=8,
     )
 
-    first = (side_down, near_down, near_gate, first_pair, bwd_first, large, *fwd_far)
-    fwd_pack = to_section(after(fwd_pack, *first), 1)
+    first = (side_down, near_down, fwd_pack, first_pair, bwd_first, large, *fwd_far)
+    bwd_pack = to_section(after(bwd_pack, *first), -1)
     near_up = swap(after(up, *first), NEAR)
     (mixed,) = call(
         join_kernel,
@@ -445,9 +445,9 @@
         LONG,
         (after(grad_first, side_large), *bwd_far),
     )
-    second = (rest, fwd_pack, near_up, own_pair)
+    second = (rest, bwd_pack, near_up, own_pair)
     rest_pair = swap(rest, FAR)
-    bwd_pack = to_section(after(bwd_pack, *second), -1)
+    near_gate = swap(after(gate, *second), NEAR)
     side_small = swap(after(small, *second), SIDE)
     side_near_large = swap(after(side_large, *second), NEAR)
     side_near_down = swap(after(side_down, *second), NEAR)
@@ -475,9 +475,7 @@
         (fwd_x, part, *beside[0], *beside[1]),
         held=6,
     )
-    fwd_own, fwd_near, fwd_cross, fwd_sum, rest_pair, bwd_pack = lax.optimization_barrier(
-        (fwd_own, fwd_near, fwd_cross, fwd_sum, rest_pair, bwd_pack)
-    )
+    rest_pair = after(rest_pair, fwd_own)
     fwd_received = swap(fwd_cross, FAR)
     fwd_near_sums = to_section(fwd_own, 1)
     fwd_second = to_section(fwd_near, 1, lambda i: i ^ FAR)
@@ -489,10 +487,10 @@
         SHORT,
         (bwd_first, grad_first, *bwd_far, own_pair, rest_pair, norm_gain)
         + (*mine[0], *mine[1], *beside[0], *beside[1]),
-        held=10,
+        held=14,
         scratch=(pltpu.VMEM(rows, jnp.bfloat16),) * 2,
     )
-    bwd_received = swap(bwd_cross, FAR)
+    bwd_received = swap(after(bwd_cross, fwd_received, fwd_near_sums), FAR)
     fwd_sums = send_sums(fwd_sum, fwd_received, experts, capacity, 1)
     bwd_near_sums = to_section(after(bwd_own, fwd_received), -1)
     bwd_sums = send_sums(bwd_sum, bwd_received, experts, capacity, -1)
@@ -509,12 +507,19 @@
         (fwd_pack, *fwd_back),
         held=8,
     )
+    (held_pack,) = call(
+        join_kernel,
+        "hold",
+        [(bwd_pack.shape, jnp.bfloat16)],
+        SHORT,
+        (after(bwd_pack, bwd_received),),
+    )
     (bwd_next,) = call(
         functools.partial(finish_back_kernel, experts, capacity),
         "finish_back",
         [((tokens, width), jnp.bfloat16)],
         SHORT,
-        (bwd_pack, *bwd_back),
+        (held_pack, *bwd_back),
         held=8,
     )
     return (fwd_next[None], bwd_next[None])

time: 123 us -> 121 us (0.984)
  the two profiles are of different devices: /device:TPU:0 before, /device:TPU:4 now
where the time goes in v4:
time: 121 us
  waiting for transfers between devices  63 us (52%)
  starting transfers between devices  31.6 us (26%)
  Pallas kernels  23.3 us (19%)
  local copies, waits for them, and re-layouts  1.98 us (2%)
    ppermute x14, waiting for transfers between devices, swap(): lax.ppermute(value, 'ep', [(i, i ^ bit) for i in range(lax.axis_size('ep'...  38.5 us
    pallas_call x9, Pallas kernels, call(): pl.pallas_call(kernel, name=name, out_shape=[jax.ShapeDtypeStruct(shape,...  19.4 us
    ppermute x8, starting transfers between devices, to_section(): return lax.ppermute(value, ('pp', 'ep'), pairs)  18.2 us
    ppermute x8, waiting for transfers between devices, to_section(): return lax.ppermute(value, ('pp', 'ep'), pairs)  15.8 us
    ppermute x2, waiting for transfers between devices, to_expert(): lax.ppermute(value, 'ep', [(i, (i + SLICES * shift) % count) for i in ran...  8.7 us
    ppermute x14, starting transfers between devices, swap(): lax.ppermute(value, 'ep', [(i, i ^ bit) for i in range(lax.axis_size('ep'...  7.95 us
    ppermute x2, starting transfers between devices, to_expert(): lax.ppermute(value, 'ep', [(i, (i + SLICES * shift) % count) for i in ran...  5.42 us
    pallas_call x1, Pallas kernels, call_fetching(): pl.pallas_call(fetching, name=name, out_shape=[jax.ShapeDtypeStruct(shape...  2.55 us
  transfers between devices with their start and end apart: 24, of which 11 were waited for; matrix products, arithmetic and copies ran while one was open for 0% of the time, Pallas kernels for 18%

profile of v4, /device:TPU:4, one launch (start us, length us, event | category | flops | bytes accessed | tf_op | source)
XLA Modules:
  0.0 121.0 jit_solution(16586000450353877926)
XLA Ops:
  0.8 2.6 %prepare.1 = (bf16[64,3712]{1,0:T(8,128)(2,1)}, bf16[40,3584]{1,0:T(8,128)(2,1)}, bf16[40,3584]{1,0:T(8,128)(2,1)}) custom-call(s32[1,64]{1,0:T(1,128)} %bitcast.27, f32[1,64]{1,0:T(1,128)} %bitcast.28, bf16[64,3584]{1,0:T(8,128)(2,1)} %bitcast.26, f32[1,3584]{1,0:T(1,128)} %refs_5_.1), custom_call_target="tpu_custom_call" | custom-call | flops 199999995904 | tf_op jit(solution)/shard_map/prepare/pallas_call | solution.py:81
  3.4 2.0 %collective-permute-start = (bf16[64,3712]{1,0:T(8,128)(2,1)}, bf16[64,3712]{1,0:T(8,128)(2,1)S(1)}, u32[]{:S(2)}, u32[]{:S(2)}) collective-permute-start(bf16[64,3712]{1,0:T(8,128)(2,1)} %get-tuple-element.41), channel_id=1, source_target_pairs={{0,16},{1,17},{2,18},{3,19},{4,20},{5,21},{6,22},{7,23},{8,24},{9,... | collective-permute-start | bytes 1425416 | tf_op jit(solution)/shard_map/ppermute | solution.py:32
  5.5 2.6 %collective-permute-start.1 = (bf16[40,3584]{1,0:T(8,128)(2,1)}, bf16[40,3584]{1,0:T(8,128)(2,1)S(1)}, u32[]{:S(2)}, u32[]{:S(2)}) collective-permute-start(bf16[40,3584]{1,0:T(8,128)(2,1)} %get-tuple-element.43), channel_id=1, source_target_pairs={{0,8},{1,9},{2,10},{3,11},{4,12},{5,13},{6,14},{7,15},{8,0},{9,1},... | collective-permute-start | bytes 860168 | tf_op jit(solution)/shard_map/ppermute | solution.py:22
  8.1 1.6 %collective-permute-start.2 = (bf16[40,3584]{1,0:T(8,128)(2,1)}, bf16[40,3584]{1,0:T(8,128)(2,1)S(1)}, u32[]{:S(2)}, u32[]{:S(2)}) collective-permute-start(bf16[40,3584]{1,0:T(8,128)(2,1)} %get-tuple-element.56.refs_0_), channel_id=1, source_target_pairs={{0,4},{1,5},{2,6},{3,7},{4,0},{5,1},{6,2},{7,3},{8,12},{9,13},{10,... | collective-permute-start | bytes 860168 | tf_op jit(solution)/shard_map/ppermute | solution.py:17
  11.1 1.6 %prepare_back.1 = (bf16[64,7296]{1,0:T(8,128)(2,1)}, bf16[40,3584]{1,0:T(8,128)(2,1)S(1)}, bf16[40,3584]{1,0:T(8,128)(2,1)S(1)}, bf16[40,7168]{1,0:T(8,128)(2,1)S(1)}) custom-call(s32[1,64]{1,0:T(1,128)S(1)} %bitcast.22, f32[1,64]{1,0:T(1,128)S(1)} %bitcast.23, bf16[64,3584]{1,0:T(8,128)(2,1)S(1)} %bitcast.20, bf16[64,3584]{1,0:T(8,128)(2,1)S(1)} %bitcast.21, ...), custom_call_target="tpu_custom_call" | custom-call | flops 1000000 | tf_op jit(solution)/shard_map/prepare_back/pallas_call | solution.py:53
  12.7 8.7 %collective-permute-done.1.refs_0_.refs_1_ = bf16[40,3584]{1,0:T(8,128)(2,1)S(1)} collective-permute-done((bf16[40,3584]{1,0:T(8,128)(2,1)}, bf16[40,3584]{1,0:T(8,128)(2,1)S(1)}, u32[]{:S(2)}, u32[]{:S(2)}) %collective-permute-start.1) | collective-permute-done | bytes 286752 | tf_op jit(solution)/shard_map/ppermute | solution.py:22
  21.6 2.1 %collective-permute-done.3.refs_2_.refs_14_ = bf16[256,1792]{1,0:T(8,128)(2,1)} collective-permute-done((bf16[256,1792]{1,0:T(8,128)(2,1)}, bf16[256,1792]{1,0:T(8,128)(2,1)}, u32[]{:S(2)}, u32[]{:S(2)}) %collective-permute-start.3) | collective-permute-done | bytes 917536 | tf_op jit(solution)/shard_map/ppermute | solution.py:17
  24.1 2.8 %collective-permute-start.7 = (bf16[40,7168]{1,0:T(8,128)(2,1)S(1)}, bf16[40,7168]{1,0:T(8,128)(2,1)S(1)}, u32[]{:S(2)}, u32[]{:S(2)}) collective-permute-start(bf16[40,7168]{1,0:T(8,128)(2,1)S(1)} %get-tuple-element.51), channel_id=1, source_target_pairs={{0,8},{1,9},{2,10},{3,11},{4,12},{5,13},{6,14},{7,15},{8,0},{9,1},... | collective-permute-start | bytes 1720328 | tf_op jit(solution)/shard_map/ppermute | solution.py:22
  30.8 23.4 %collective-permute-done.6.refs_0_.refs_12_ = bf16[2560,256]{1,0:T(8,128)(2,1)} collective-permute-done((bf16[2560,256]{1,0:T(8,128)(2,1)S(1)}, bf16[2560,256]{1,0:T(8,128)(2,1)}, u32[]{:S(2)}, u32[]{:S(2)}) %collective-permute-start.6) | collective-permute-done | bytes 1310752 | tf_op jit(solution)/shard_map/ppermute | solution.py:17
  55.5 1.6 %collective-permute-start.19 = (bf16[40,10752]{1,0:T(8,128)(2,1)S(1)}, bf16[40,10752]{1,0:T(8,128)(2,1)S(1)}, u32[]{:S(2)}, u32[]{:S(2)}) collective-permute-start(bf16[40,10752]{1,0:T(8,128)(2,1)S(1)} %join_back.1), channel_id=1, source_target_pairs={{0,4},{1,5},{2,6},{3,7},{4,0},{5,1},{6,2},{7,3},{8,12},{9,13},{10,... | collective-permute-start | bytes 2580488 | tf_op jit(solution)/shard_map/ppermute | solution.py:17
  57.1 3.2 %collective-permute-done.10.refs_5_.refs_17_ = bf16[256,1792]{1,0:T(8,128)(2,1)S(1)} collective-permute-done((bf16[256,1792]{1,0:T(8,128)(2,1)}, bf16[256,1792]{1,0:T(8,128)(2,1)S(1)}, u32[]{:S(2)}, u32[]{:S(2)}) %collective-permute-start.10) | collective-permute-done | bytes 917536 | tf_op jit(solution)/shard_map/ppermute | solution.py:17
  62.2 3.1 %forward_near.1 = (bf16[160,3584]{1,0:T(8,128)(2,1)S(1)}, f32[160,3584]{1,0:T(8,128)S(1)}) custom-call(bf16[40,3584]{1,0:T(8,128)(2,1)S(1)} %copy-done.10, bf16[40,3584]{1,0:T(8,128)(2,1)S(1)} %copy-done.3, bf16[40,3584]{1,0:T(8,128)(2,1)S(1)} %copy-done.12, bf16[40,7168]{1,0:T(8,128)(2,1)} %collective-permute-done.5.refs_3_, ...), custom_call_target="tpu_custom_call" | custom-call | flops 1000000 | tf_op jit(solution)/shard_map/forward_near/pallas_call | solution.py:53
  65.3 4.0 %collective-permute-done.12.refs_1_.refs_13_ = bf16[1024,256]{1,0:T(8,128)(2,1)S(1)} collective-permute-done((bf16[1024,256]{1,0:T(8,128)(2,1)S(1)}, bf16[1024,256]{1,0:T(8,128)(2,1)S(1)}, u32[]{:S(2)}, u32[]{:S(2)}) %collective-permute-start.12) | collective-permute-done | bytes 524320 | tf_op jit(solution)/shard_map/ppermute | solution.py:17
  69.3 1.9 %collective-permute-done.14.refs_4_.refs_16_ = bf16[1024,256]{1,0:T(8,128)(2,1)S(1)} collective-permute-done((bf16[1024,256]{1,0:T(8,128)(2,1)S(1)}, bf16[1024,256]{1,0:T(8,128)(2,1)S(1)}, u32[]{:S(2)}, u32[]{:S(2)}) %collective-permute-start.14) | collective-permute-done | bytes 524320 | tf_op jit(solution)/shard_map/ppermute | solution.py:17
  71.2 2.8 %forward_side.1 = (bf16[40,3584]{1,0:T(8,128)(2,1)S(1)}, bf16[40,3584]{1,0:T(8,128)(2,1)S(1)}, bf16[40,3584]{1,0:T(8,128)(2,1)S(1)}, f32[40,3584]{1,0:T(8,128)S(1)}) custom-call(bf16[160,3584]{1,0:T(8,128)(2,1)S(1)} %get-tuple-element.61.x_ref, f32[160,3584]{1,0:T(8,128)S(1)} %get-tuple-element.62.part_ref, ...), custom_call_target="tpu_custom_call" | custom-call | flops 1000000 | tf_op jit(solution)/shard_map/forward_side/pallas_call | solution.py:53
  74.0 1.6 %collective-permute-start.17 = (bf16[40,3584]{1,0:T(8,128)(2,1)S(1)}, bf16[40,3584]{1,0:T(8,128)(2,1)S(1)}, u32[]{:S(2)}, u32[]{:S(2)}) collective-permute-start(bf16[40,3584]{1,0:T(8,128)(2,1)S(1)} %get-tuple-element.70), channel_id=1, source_target_pairs={{0,4},{1,5},{2,6},{3,7},{4,0},{5,1},{6,2},{7,3},{8,12},{9,13},{10,... | collective-permute-start | bytes 860168 | tf_op jit(solution)/shard_map/ppermute | solution.py:17
  77.1 2.1 %collective-permute-start.16 = (bf16[40,3584]{1,0:T(8,128)(2,1)S(1)}, bf16[40,3584]{1,0:T(8,128)(2,1)S(1)}, u32[]{:S(2)}, u32[]{:S(2)}) collective-permute-start(bf16[40,3584]{1,0:T(8,128)(2,1)S(1)} %get-tuple-element.68), channel_id=1, source_target_pairs={{0,20},{1,21},{2,22},{3,23},{4,16},{5,17},{6,18},{7,19},{8,28},{9,... | collective-permute-start | bytes 860168 | tf_op jit(solution)/shard_map/ppermute | solution.py:32
  79.2 7.0 %backward.1 = (bf16[40,3584]{1,0:T(8,128)(2,1)S(1)}, bf16[40,3584]{1,0:T(8,128)(2,1)S(1)}, bf16[40,3584]{1,0:T(8,128)(2,1)S(1)}, f32[40,3584]{1,0:T(8,128)S(1)}) custom-call(bf16[40,3584]{1,0:T(8,128)(2,1)S(1)} %copy-done.5, bf16[40,3584]{1,0:T(8,128)(2,1)S(1)} %get-tuple-element.49.refs_0_.refs_1_, ...), custom_call_target="tpu_custom_call" | custom-call | flops 1000000 | tf_op jit(solution)/shard_map/backward/pallas_call | solution.py:53
  86.8 3.8 %collective-permute-done.15.rest_0_ = bf16[40,3584]{1,0:T(8,128)(2,1)S(1)} collective-permute-done((bf16[40,3584]{1,0:T(8,128)(2,1)S(1)}, bf16[40,3584]{1,0:T(8,128)(2,1)S(1)}, u32[]{:S(2)}, u32[]{:S(2)}) %collective-permute-start.15) | collective-permute-done | bytes 286752 | tf_op jit(solution)/shard_map/ppermute | solution.py:32
  90.6 4.5 %collective-permute-start.18 = (bf16[40,3584]{1,0:T(8,128)(2,1)S(1)}, bf16[40,3584]{1,0:T(8,128)(2,1)S(1)}, u32[]{:S(2)}, u32[]{:S(2)}) collective-permute-start(bf16[40,3584]{1,0:T(8,128)(2,1)S(1)} %add_convert_fusion.1), channel_id=1, source_target_pairs={{0,24},{1,25},{2,26},{3,27},{4,28},{5,29},{6,30},{7,31},{8,16},{9,... | collective-permute-start | bytes 860168 | tf_op jit(solution)/shard_map/ppermute | solution.py:32
  95.2 3.7 %collective-permute-done.20 = bf16[40,3584]{1,0:T(8,128)(2,1)S(1)} collective-permute-done((bf16[40,3584]{1,0:T(8,128)(2,1)S(1)}, bf16[40,3584]{1,0:T(8,128)(2,1)S(1)}, u32[]{:S(2)}, u32[]{:S(2)}) %collective-permute-start.20) | collective-permute-done | bytes 286752 | tf_op jit(solution)/shard_map/ppermute | solution.py:17
  98.8 5.9 %collective-permute-start.22 = (bf16[40,3584]{1,0:T(8,128)(2,1)S(1)}, bf16[40,3584]{1,0:T(8,128)(2,1)S(1)}, u32[]{:S(2)}, u32[]{:S(2)}) collective-permute-start(bf16[40,3584]{1,0:T(8,128)(2,1)S(1)} %get-tuple-element.78), channel_id=1, source_target_pairs={{0,20},{1,21},{2,22},{3,23},{4,16},{5,17},{6,18},{7,19},{8,28},{9,... | collective-permute-start | bytes 860168 | tf_op jit(solution)/shard_map/ppermute | solution.py:32
  107.5 9.1 %collective-permute-done.22.rest_1_ = bf16[40,3584]{1,0:T(8,128)(2,1)S(1)} collective-permute-done((bf16[40,3584]{1,0:T(8,128)(2,1)S(1)}, bf16[40,3584]{1,0:T(8,128)(2,1)S(1)}, u32[]{:S(2)}, u32[]{:S(2)}) %collective-permute-start.22) | collective-permute-done | bytes 286752 | tf_op jit(solution)/shard_map/ppermute | solution.py:32
  116.5 2.9 %collective-permute-done.23.rest_2_ = bf16[40,3584]{1,0:T(8,128)(2,1)S(1)} collective-permute-done((bf16[40,3584]{1,0:T(8,128)(2,1)S(1)}, bf16[40,3584]{1,0:T(8,128)(2,1)S(1)}, u32[]{:S(2)}, u32[]{:S(2)}) %collective-permute-start.23) | collective-permute-done | bytes 286752 | tf_op jit(solution)/shard_map/ppermute | solution.py:32
  (71 shorter events, 15.4 us)
Async XLA Ops:
  0.6 21.0 %collective-permute-start.4 = (bf16[256,1792]{1,0:T(8,128)(2,1)}, bf16[256,1792]{1,0:T(8,128)(2,1)}, u32[]{:S(2)}, u32[]{:S(2)}) collective-permute-start(bf16[256,1792]{1,0:T(8,128)(2,1)} %bitcast.16), channel_id=1, source_target_pairs={{0,1},{1,0},{2,3},{3,2},{4,5},{5,4},{6,7},{7,6},{8,9},{9,8},{10,11... | collective-permute-start | bytes 2752520 | tf_op jit(solution)/shard_map/ppermute | solution.py:17
  0.7 23.1 %collective-permute-start.3 = (bf16[256,1792]{1,0:T(8,128)(2,1)}, bf16[256,1792]{1,0:T(8,128)(2,1)}, u32[]{:S(2)}, u32[]{:S(2)}) collective-permute-start(bf16[256,1792]{1,0:T(8,128)(2,1)} %bitcast.17), channel_id=1, source_target_pairs={{0,2},{1,3},{2,0},{3,1},{4,6},{5,7},{6,4},{7,5},{8,10},{9,11},{10,... | collective-permute-start | bytes 2752520 | tf_op jit(solution)/shard_map/ppermute | solution.py:17
  3.4 18.2 %collective-permute-start = (bf16[64,3712]{1,0:T(8,128)(2,1)}, bf16[64,3712]{1,0:T(8,128)(2,1)S(1)}, u32[]{:S(2)}, u32[]{:S(2)}) collective-permute-start(bf16[64,3712]{1,0:T(8,128)(2,1)} %get-tuple-element.41), channel_id=1, source_target_pairs={{0,16},{1,17},{2,18},{3,19},{4,20},{5,21},{6,22},{7,23},{8,24},{9,... | collective-permute-start | bytes 1425416 | tf_op jit(solution)/shard_map/ppermute | solution.py:32
  5.5 16.0 %collective-permute-start.1 = (bf16[40,3584]{1,0:T(8,128)(2,1)}, bf16[40,3584]{1,0:T(8,128)(2,1)S(1)}, u32[]{:S(2)}, u32[]{:S(2)}) collective-permute-start(bf16[40,3584]{1,0:T(8,128)(2,1)} %get-tuple-element.43), channel_id=1, source_target_pairs={{0,8},{1,9},{2,10},{3,11},{4,12},{5,13},{6,14},{7,15},{8,0},{9,1},... | collective-permute-start | bytes 860168 | tf_op jit(solution)/shard_map/ppermute | solution.py:22
  8.1 13.6 %collective-permute-start.2 = (bf16[40,3584]{1,0:T(8,128)(2,1)}, bf16[40,3584]{1,0:T(8,128)(2,1)S(1)}, u32[]{:S(2)}, u32[]{:S(2)}) collective-permute-start(bf16[40,3584]{1,0:T(8,128)(2,1)} %get-tuple-element.56.refs_0_), channel_id=1, source_target_pairs={{0,4},{1,5},{2,6},{3,7},{4,0},{5,1},{6,2},{7,3},{8,12},{9,13},{10,... | collective-permute-start | bytes 860168 | tf_op jit(solution)/shard_map/ppermute | solution.py:17
  23.8 30.4 %collective-permute-start.6 = (bf16[2560,256]{1,0:T(8,128)(2,1)S(1)}, bf16[2560,256]{1,0:T(8,128)(2,1)}, u32[]{:S(2)}, u32[]{:S(2)}) collective-permute-start(bf16[2560,256]{1,0:T(8,128)(2,1)S(1)} %get-tuple-element.48), channel_id=1, source_target_pairs={{0,2},{1,3},{2,0},{3,1},{4,6},{5,7},{6,4},{7,5},{8,10},{9,11},{10,... | collective-permute-start | bytes 3932168 | tf_op jit(solution)/shard_map/ppermute | solution.py:17
  24.1 30.2 %collective-permute-start.7 = (bf16[40,7168]{1,0:T(8,128)(2,1)S(1)}, bf16[40,7168]{1,0:T(8,128)(2,1)S(1)}, u32[]{:S(2)}, u32[]{:S(2)}) collective-permute-start(bf16[40,7168]{1,0:T(8,128)(2,1)S(1)} %get-tuple-element.51), channel_id=1, source_target_pairs={{0,8},{1,9},{2,10},{3,11},{4,12},{5,13},{6,14},{7,15},{8,0},{9,1},... | collective-permute-start | bytes 1720328 | tf_op jit(solution)/shard_map/ppermute | solution.py:22
  27.7 26.6 %collective-permute-start.5 = (bf16[40,7168]{1,0:T(8,128)(2,1)}, bf16[40,7168]{1,0:T(8,128)(2,1)}, u32[]{:S(2)}, u32[]{:S(2)}) collective-permute-start(bf16[40,7168]{1,0:T(8,128)(2,1)} %join.1), channel_id=1, source_target_pairs={{0,4},{1,5},{2,6},{3,7},{4,0},{5,1},{6,2},{7,3},{8,12},{9,13},{10,... | collective-permute-start | bytes 1720328 | tf_op jit(solution)/shard_map/ppermute | solution.py:17
  29.3 25.0 %collective-permute-start.9 = (bf16[1792,256]{1,0:T(8,128)(2,1)}, bf16[1792,256]{1,0:T(8,128)(2,1)}, u32[]{:S(2)}, u32[]{:S(2)}) collective-permute-start(bf16[1792,256]{1,0:T(8,128)(2,1)} %bitcast.9.up_ref.refs_5_.refs_7_), channel_id=1, source_target_pairs={{0,1},{1,0},{2,3},{3,2},{4,5},{5,4},{6,7},{7,6},{8,9},{9,8},{10,11... | collective-permute-start | bytes 2752520 | tf_op jit(solution)/shard_map/ppermute | solution.py:17
  29.3 25.0 %collective-permute-start.8 = (bf16[64,7296]{1,0:T(8,128)(2,1)}, bf16[64,7296]{1,0:T(8,128)(2,1)}, u32[]{:S(2)}, u32[]{:S(2)}) collective-permute-start(bf16[64,7296]{1,0:T(8,128)(2,1)} %get-tuple-element.53), channel_id=1, source_target_pairs={{0,16},{1,17},{2,18},{3,19},{4,20},{5,21},{6,22},{7,23},{8,24},{9,... | collective-permute-start | bytes 2801672 | tf_op jit(solution)/shard_map/ppermute | solution.py:32
  54.4 14.9 %collective-permute-start.13 = (bf16[2560,256]{1,0:T(8,128)(2,1)}, bf16[2560,256]{1,0:T(8,128)(2,1)S(1)}, u32[]{:S(2)}, u32[]{:S(2)}) collective-permute-start(bf16[2560,256]{1,0:T(8,128)(2,1)} %collective-permute-done.6.refs_0_.refs_12_), channel_id=1, source_target_pairs={{0,1},{1,0},{2,3},{3,2},{4,5},{5,4},{6,7},{7,6},{8,9},{9,8},{10,11... | collective-permute-start | bytes 3932168 | tf_op jit(solution)/shard_map/ppermute | solution.py:17
  54.4 5.9 %collective-permute-start.10 = (bf16[256,1792]{1,0:T(8,128)(2,1)}, bf16[256,1792]{1,0:T(8,128)(2,1)S(1)}, u32[]{:S(2)}, u32[]{:S(2)}) collective-permute-start(bf16[256,1792]{1,0:T(8,128)(2,1)} %collective-permute-done.3.refs_2_.refs_14_), channel_id=1, source_target_pairs={{0,1},{1,0},{2,3},{3,2},{4,5},{5,4},{6,7},{7,6},{8,9},{9,8},{10,11... | collective-permute-start | bytes 2752520 | tf_op jit(solution)/shard_map/ppermute | solution.py:17
  54.9 5.4 %collective-permute-start.11 = (bf16[1792,256]{1,0:T(8,128)(2,1)S(1)}, bf16[1792,256]{1,0:T(8,128)(2,1)S(1)}, u32[]{:S(2)}, u32[]{:S(2)}) collective-permute-start(bf16[1792,256]{1,0:T(8,128)(2,1)S(1)} %bitcast.13), channel_id=1, source_target_pairs={{0,1},{1,0},{2,3},{3,2},{4,5},{5,4},{6,7},{7,6},{8,9},{9,8},{10,11... | collective-permute-start | bytes 2752520 | tf_op jit(solution)/shard_map/ppermute | solution.py:17
  55.0 14.3 %collective-permute-start.12 = (bf16[1024,256]{1,0:T(8,128)(2,1)S(1)}, bf16[1024,256]{1,0:T(8,128)(2,1)S(1)}, u32[]{:S(2)}, u32[]{:S(2)}) collective-permute-start(bf16[1024,256]{1,0:T(8,128)(2,1)S(1)} %get-tuple-element.64), channel_id=1, source_target_pairs={{0,2},{1,3},{2,0},{3,1},{4,6},{5,7},{6,4},{7,5},{8,10},{9,11},{10,... | collective-permute-start | bytes 1572872 | tf_op jit(solution)/shard_map/ppermute | solution.py:17
  55.5 21.7 %collective-permute-start.19 = (bf16[40,10752]{1,0:T(8,128)(2,1)S(1)}, bf16[40,10752]{1,0:T(8,128)(2,1)S(1)}, u32[]{:S(2)}, u32[]{:S(2)}) collective-permute-start(bf16[40,10752]{1,0:T(8,128)(2,1)S(1)} %join_back.1), channel_id=1, source_target_pairs={{0,4},{1,5},{2,6},{3,7},{4,0},{5,1},{6,2},{7,3},{8,12},{9,13},{10,... | collective-permute-start | bytes 2580488 | tf_op jit(solution)/shard_map/ppermute | solution.py:17
  69.3 1.9 %collective-permute-start.14 = (bf16[1024,256]{1,0:T(8,128)(2,1)S(1)}, bf16[1024,256]{1,0:T(8,128)(2,1)S(1)}, u32[]{:S(2)}, u32[]{:S(2)}) collective-permute-start(bf16[1024,256]{1,0:T(8,128)(2,1)S(1)} %collective-permute-done.12.refs_1_.refs_13_), channel_id=1, source_target_pairs={{0,1},{1,0},{2,3},{3,2},{4,5},{5,4},{6,7},{7,6},{8,9},{9,8},{10,11... | collective-permute-start | bytes 1572872 | tf_op jit(solution)/shard_map/ppermute | solution.py:17
  74.0 12.2 %collective-permute-start.17 = (bf16[40,3584]{1,0:T(8,128)(2,1)S(1)}, bf16[40,3584]{1,0:T(8,128)(2,1)S(1)}, u32[]{:S(2)}, u32[]{:S(2)}) collective-permute-start(bf16[40,3584]{1,0:T(8,128)(2,1)S(1)} %get-tuple-element.70), channel_id=1, source_target_pairs={{0,4},{1,5},{2,6},{3,7},{4,0},{5,1},{6,2},{7,3},{8,12},{9,13},{10,... | collective-permute-start | bytes 860168 | tf_op jit(solution)/shard_map/ppermute | solution.py:17
  75.7 14.9 %collective-permute-start.15 = (bf16[40,3584]{1,0:T(8,128)(2,1)S(1)}, bf16[40,3584]{1,0:T(8,128)(2,1)S(1)}, u32[]{:S(2)}, u32[]{:S(2)}) collective-permute-start(bf16[40,3584]{1,0:T(8,128)(2,1)S(1)} %get-tuple-element.67), channel_id=1, source_target_pairs={{0,16},{1,17},{2,18},{3,19},{4,20},{5,21},{6,22},{7,23},{8,24},{9,... | collective-permute-start | bytes 860168 | tf_op jit(solution)/shard_map/ppermute | solution.py:32
  77.1 29.0 %collective-permute-start.16 = (bf16[40,3584]{1,0:T(8,128)(2,1)S(1)}, bf16[40,3584]{1,0:T(8,128)(2,1)S(1)}, u32[]{:S(2)}, u32[]{:S(2)}) collective-permute-start(bf16[40,3584]{1,0:T(8,128)(2,1)S(1)} %get-tuple-element.68), channel_id=1, source_target_pairs={{0,20},{1,21},{2,22},{3,23},{4,16},{5,17},{6,18},{7,19},{8,28},{9,... | collective-permute-start | bytes 860168 | tf_op jit(solution)/shard_map/ppermute | solution.py:32
  86.2 21.2 %collective-permute-start.21 = (bf16[40,3584]{1,0:T(8,128)(2,1)S(1)}, bf16[40,3584]{1,0:T(8,128)(2,1)S(1)}, u32[]{:S(2)}, u32[]{:S(2)}) collective-permute-start(bf16[40,3584]{1,0:T(8,128)(2,1)S(1)} %get-tuple-element.76), channel_id=1, source_target_pairs={{0,16},{1,17},{2,18},{3,19},{4,20},{5,21},{6,22},{7,23},{8,24},{9,... | collective-permute-start | bytes 860168 | tf_op jit(solution)/shard_map/ppermute | solution.py:32
  90.6 8.2 %collective-permute-start.20 = (bf16[40,3584]{1,0:T(8,128)(2,1)S(1)}, bf16[40,3584]{1,0:T(8,128)(2,1)S(1)}, u32[]{:S(2)}, u32[]{:S(2)}) collective-permute-start(bf16[40,3584]{1,0:T(8,128)(2,1)S(1)} %get-tuple-element.73), channel_id=1, source_target_pairs={{0,4},{1,5},{2,6},{3,7},{4,0},{5,1},{6,2},{7,3},{8,12},{9,13},{10,... | collective-permute-start | bytes 860168 | tf_op jit(solution)/shard_map/ppermute | solution.py:17
  90.6 15.5 %collective-permute-start.18 = (bf16[40,3584]{1,0:T(8,128)(2,1)S(1)}, bf16[40,3584]{1,0:T(8,128)(2,1)S(1)}, u32[]{:S(2)}, u32[]{:S(2)}) collective-permute-start(bf16[40,3584]{1,0:T(8,128)(2,1)S(1)} %add_convert_fusion.1), channel_id=1, source_target_pairs={{0,24},{1,25},{2,26},{3,27},{4,28},{5,29},{6,30},{7,31},{8,16},{9,... | collective-permute-start | bytes 860168 | tf_op jit(solution)/shard_map/ppermute | solution.py:32
  98.8 17.7 %collective-permute-start.22 = (bf16[40,3584]{1,0:T(8,128)(2,1)S(1)}, bf16[40,3584]{1,0:T(8,128)(2,1)S(1)}, u32[]{:S(2)}, u32[]{:S(2)}) collective-permute-start(bf16[40,3584]{1,0:T(8,128)(2,1)S(1)} %get-tuple-element.78), channel_id=1, source_target_pairs={{0,20},{1,21},{2,22},{3,23},{4,16},{5,17},{6,18},{7,19},{8,28},{9,... | collective-permute-start | bytes 860168 | tf_op jit(solution)/shard_map/ppermute | solution.py:32
  104.8 14.7 %collective-permute-start.23 = (bf16[40,3584]{1,0:T(8,128)(2,1)S(1)}, bf16[40,3584]{1,0:T(8,128)(2,1)S(1)}, u32[]{:S(2)}, u32[]{:S(2)}) collective-permute-start(bf16[40,3584]{1,0:T(8,128)(2,1)S(1)} %add_convert_fusion), channel_id=1, source_target_pairs={{0,24},{1,25},{2,26},{3,27},{4,28},{5,29},{6,30},{7,31},{8,16},{9,... | collective-permute-start | bytes 860168 | tf_op jit(solution)/shard_map/ppermute | solution.py:32
  (17 other events, 218.6 us)

commit v5 on v4

--- a/solution.py
+++ b/solution.py
@@ -404,7 +404,6 @@
 
     large, small = split_weights(gate, up)
     side_down = swap(down, SIDE)
-    near_down = swap(down, NEAR)
     fwd_pack, *fwd_groups = call_fetching(
         functools.partial(prepare_kernel, experts, capacity),
         "prepare",
@@ -414,6 +413,7 @@
     )
     fwd_far = [to_expert(fwd_groups[r], r) for r in shifts]
     first_pair = swap(fwd_groups[0], FAR)
+    near_down = swap(after(down, fwd_groups[0]), NEAR)
     fwd_pack = to_section(fwd_pack, 1)
     bwd_pack, bwd_first, grad_first, *bwd_groups = call(
         functools.partial(prepare_back_kernel, experts, capacity),
@@ -477,8 +477,8 @@
     )
     rest_pair = after(rest_pair, fwd_own)
     fwd_received = swap(fwd_cross, FAR)
+    fwd_second = to_section(fwd_near, 1, lambda i: i ^ FAR)
     fwd_near_sums = to_section(fwd_own, 1)
-    fwd_second = to_section(fwd_near, 1, lambda i: i ^ FAR)
 
     bwd_own, bwd_near, bwd_cross, bwd_sum = call(
         functools.partial(backward_kernel, experts, capacity),
@@ -490,7 +490,7 @@
         held=14,
         scratch=(pltpu.VMEM(rows, jnp.bfloat16),) * 2,
     )
-    bwd_received = swap(after(bwd_cross, fwd_received, fwd_near_sums), FAR)
+    bwd_received = swap(after(bwd_cross, fwd_received), FAR)
     fwd_sums = send_sums(fwd_sum, fwd_received, experts, capacity, 1)
     bwd_near_sums = to_section(after(bwd_own, fwd_received), -1)
     bwd_sums = send_sums(bwd_sum, bwd_received, experts, capacity, -1)

time: 121 us -> 120 us (level)
  the two profiles are of different devices: /device:TPU:4 before, /device:TPU:0 now
where the time goes in v5:
time: 120 us; the launch traced here: 119 us
  waiting for transfers between devices  59.7 us (50%)
  starting transfers between devices  33.8 us (28%)
  Pallas kernels  22.9 us (19%)
  local copies, waits for them, and re-layouts  1.25 us (1%)
    ppermute x14, waiting for transfers between devices, swap(): lax.ppermute(value, 'ep', [(i, i ^ bit) for i in range(lax.axis_size('ep'...  42.4 us
    pallas_call x9, Pallas kernels, call(): pl.pallas_call(kernel, name=name, out_shape=[jax.ShapeDtypeStruct(shape,...  18.9 us
    ppermute x8, starting transfers between devices, to_section(): return lax.ppermute(value, ('pp', 'ep'), pairs)  14.8 us
    ppermute x14, starting transfers between devices, swap(): lax.ppermute(value, 'ep', [(i, i ^ bit) for i in range(lax.axis_size('ep'...  13.9 us
    ppermute x2, waiting for transfers between devices, to_expert(): lax.ppermute(value, 'ep', [(i, (i + SLICES * shift) % count) for i in ran...  9 us
    ppermute x8, waiting for transfers between devices, to_section(): return lax.ppermute(value, ('pp', 'ep'), pairs)  8.36 us
    ppermute x2, starting transfers between devices, to_expert(): lax.ppermute(value, 'ep', [(i, (i + SLICES * shift) % count) for i in ran...  5.18 us
    pallas_call x1, Pallas kernels, call_fetching(): pl.pallas_call(fetching, name=name, out_shape=[jax.ShapeDtypeStruct(shape...  2.6 us
  transfers between devices with their start and end apart: 24, of which 9 were waited for; matrix products, arithmetic and copies ran while one was open for 0% of the time, Pallas kernels for 18%

profile of v5, /device:TPU:0, one launch (start us, length us, event | category | flops | bytes accessed | tf_op | source)
XLA Modules:
  0.0 118.7 jit_solution(13841156708824978939)
XLA Ops:
  0.6 3.0 %collective-permute-start.3 = (bf16[256,1792]{1,0:T(8,128)(2,1)}, bf16[256,1792]{1,0:T(8,128)(2,1)}, u32[]{:S(2)}, u32[]{:S(2)}) collective-permute-start(bf16[256,1792]{1,0:T(8,128)(2,1)} %bitcast.16), channel_id=1, source_target_pairs={{0,2},{1,3},{2,0},{3,1},{4,6},{5,7},{6,4},{7,5},{8,10},{9,11},{10,... | collective-permute-start | bytes 2752520 | tf_op jit(solution)/shard_map/ppermute | solution.py:17
  3.7 2.6 %prepare.1 = (bf16[64,3712]{1,0:T(8,128)(2,1)}, bf16[40,3584]{1,0:T(8,128)(2,1)}, bf16[40,3584]{1,0:T(8,128)(2,1)}) custom-call(s32[1,64]{1,0:T(1,128)} %bitcast.27, f32[1,64]{1,0:T(1,128)} %bitcast.28, bf16[64,3584]{1,0:T(8,128)(2,1)} %bitcast.26, f32[1,3584]{1,0:T(1,128)} %refs_5_.1), custom_call_target="tpu_custom_call" | custom-call | flops 199999995904 | tf_op jit(solution)/shard_map/prepare/pallas_call | solution.py:81
  6.4 1.6 %collective-permute-start = (bf16[64,3712]{1,0:T(8,128)(2,1)}, bf16[64,3712]{1,0:T(8,128)(2,1)S(1)}, u32[]{:S(2)}, u32[]{:S(2)}) collective-permute-start(bf16[64,3712]{1,0:T(8,128)(2,1)} %get-tuple-element.42), channel_id=1, source_target_pairs={{0,16},{1,17},{2,18},{3,19},{4,20},{5,21},{6,22},{7,23},{8,24},{9,... | collective-permute-start | bytes 1425416 | tf_op jit(solution)/shard_map/ppermute | solution.py:32
  8.0 2.6 %collective-permute-start.1 = (bf16[40,3584]{1,0:T(8,128)(2,1)}, bf16[40,3584]{1,0:T(8,128)(2,1)S(1)}, u32[]{:S(2)}, u32[]{:S(2)}) collective-permute-start(bf16[40,3584]{1,0:T(8,128)(2,1)} %get-tuple-element.44), channel_id=1, source_target_pairs={{0,8},{1,9},{2,10},{3,11},{4,12},{5,13},{6,14},{7,15},{8,0},{9,1},... | collective-permute-start | bytes 860168 | tf_op jit(solution)/shard_map/ppermute | solution.py:22
  10.6 1.6 %collective-permute-start.2 = (bf16[40,3584]{1,0:T(8,128)(2,1)}, bf16[40,3584]{1,0:T(8,128)(2,1)S(1)}, u32[]{:S(2)}, u32[]{:S(2)}) collective-permute-start(bf16[40,3584]{1,0:T(8,128)(2,1)} %get-tuple-element.58.refs_0_), channel_id=1, source_target_pairs={{0,4},{1,5},{2,6},{3,7},{4,0},{5,1},{6,2},{7,3},{8,12},{9,13},{10,... | collective-permute-start | bytes 860168 | tf_op jit(solution)/shard_map/ppermute | solution.py:17
  13.6 1.6 %prepare_back.1 = (bf16[64,7296]{1,0:T(8,128)(2,1)}, bf16[40,3584]{1,0:T(8,128)(2,1)S(1)}, bf16[40,3584]{1,0:T(8,128)(2,1)S(1)}, bf16[40,7168]{1,0:T(8,128)(2,1)S(1)}) custom-call(s32[1,64]{1,0:T(1,128)S(1)} %bitcast.22, f32[1,64]{1,0:T(1,128)S(1)} %bitcast.23, bf16[64,3584]{1,0:T(8,128)(2,1)S(1)} %bitcast.20, bf16[64,3584]{1,0:T(8,128)(2,1)S(1)} %bitcast.21, ...), custom_call_target="tpu_custom_call" | custom-call | flops 1000000 | tf_op jit(solution)/shard_map/prepare_back/pallas_call | solution.py:53
  15.3 9.0 %collective-permute-done.1.refs_0_.refs_1_ = bf16[40,3584]{1,0:T(8,128)(2,1)S(1)} collective-permute-done((bf16[40,3584]{1,0:T(8,128)(2,1)}, bf16[40,3584]{1,0:T(8,128)(2,1)S(1)}, u32[]{:S(2)}, u32[]{:S(2)}) %collective-permute-start.1) | collective-permute-done | bytes 286752 | tf_op jit(solution)/shard_map/ppermute | solution.py:22
  24.5 1.6 %collective-permute-start.6 = (bf16[2560,256]{1,0:T(8,128)(2,1)S(1)}, bf16[2560,256]{1,0:T(8,128)(2,1)}, u32[]{:S(2)}, u32[]{:S(2)}) collective-permute-start(bf16[2560,256]{1,0:T(8,128)(2,1)S(1)} %get-tuple-element.50), channel_id=1, source_target_pairs={{0,2},{1,3},{2,0},{3,1},{4,6},{5,7},{6,4},{7,5},{8,10},{9,11},{10,... | collective-permute-start | bytes 3932168 | tf_op jit(solution)/shard_map/ppermute | solution.py:17
  26.1 2.6 %collective-permute-start.7 = (bf16[40,7168]{1,0:T(8,128)(2,1)S(1)}, bf16[40,7168]{1,0:T(8,128)(2,1)S(1)}, u32[]{:S(2)}, u32[]{:S(2)}) collective-permute-start(bf16[40,7168]{1,0:T(8,128)(2,1)S(1)} %get-tuple-element.53), channel_id=1, source_target_pairs={{0,8},{1,9},{2,10},{3,11},{4,12},{5,13},{6,14},{7,15},{8,0},{9,1},... | collective-permute-start | bytes 1720328 | tf_op jit(solution)/shard_map/ppermute | solution.py:22
  29.5 1.6 %collective-permute-start.5 = (bf16[40,7168]{1,0:T(8,128)(2,1)}, bf16[40,7168]{1,0:T(8,128)(2,1)}, u32[]{:S(2)}, u32[]{:S(2)}) collective-permute-start(bf16[40,7168]{1,0:T(8,128)(2,1)} %join.1), channel_id=1, source_target_pairs={{0,4},{1,5},{2,6},{3,7},{4,0},{5,1},{6,2},{7,3},{8,12},{9,13},{10,... | collective-permute-start | bytes 1720328 | tf_op jit(solution)/shard_map/ppermute | solution.py:17
  32.6 21.8 %collective-permute-done.6.refs_0_.refs_12_ = bf16[2560,256]{1,0:T(8,128)(2,1)} collective-permute-done((bf16[2560,256]{1,0:T(8,128)(2,1)S(1)}, bf16[2560,256]{1,0:T(8,128)(2,1)}, u32[]{:S(2)}, u32[]{:S(2)}) %collective-permute-start.6) | collective-permute-done | bytes 1310752 | tf_op jit(solution)/shard_map/ppermute | solution.py:17
  56.6 1.6 %collective-permute-start.19 = (bf16[40,10752]{1,0:T(8,128)(2,1)S(1)}, bf16[40,10752]{1,0:T(8,128)(2,1)S(1)}, u32[]{:S(2)}, u32[]{:S(2)}) collective-permute-start(bf16[40,10752]{1,0:T(8,128)(2,1)S(1)} %join_back.1), channel_id=1, source_target_pairs={{0,4},{1,5},{2,6},{3,7},{4,0},{5,1},{6,2},{7,3},{8,12},{9,13},{10,... | collective-permute-start | bytes 2580488 | tf_op jit(solution)/shard_map/ppermute | solution.py:17
  58.2 2.3 %collective-permute-done.10.refs_5_.refs_17_ = bf16[256,1792]{1,0:T(8,128)(2,1)S(1)} collective-permute-done((bf16[256,1792]{1,0:T(8,128)(2,1)}, bf16[256,1792]{1,0:T(8,128)(2,1)S(1)}, u32[]{:S(2)}, u32[]{:S(2)}) %collective-permute-start.10) | collective-permute-done | bytes 917536 | tf_op jit(solution)/shard_map/ppermute | solution.py:17
  61.7 2.8 %forward_near.1 = (bf16[160,3584]{1,0:T(8,128)(2,1)S(1)}, f32[160,3584]{1,0:T(8,128)S(1)}) custom-call(bf16[40,3584]{1,0:T(8,128)(2,1)S(1)} %copy-done.11, bf16[40,3584]{1,0:T(8,128)(2,1)S(1)} %collective-permute-done.1.refs_0_.refs_1_, bf16[40,3584]{1,0:T(8,128)(2,1)S(1)} %collective-permute-done.2.refs_2_, ...), custom_call_target="tpu_custom_call" | custom-call | flops 1000000 | tf_op jit(solution)/shard_map/forward_near/pallas_call | solution.py:53
  64.5 5.0 %collective-permute-done.12.refs_1_.refs_13_ = bf16[1024,256]{1,0:T(8,128)(2,1)S(1)} collective-permute-done((bf16[1024,256]{1,0:T(8,128)(2,1)S(1)}, bf16[1024,256]{1,0:T(8,128)(2,1)S(1)}, u32[]{:S(2)}, u32[]{:S(2)}) %collective-permute-start.12) | collective-permute-done | bytes 524320 | tf_op jit(solution)/shard_map/ppermute | solution.py:17
  69.5 1.9 %collective-permute-done.14.refs_4_.refs_16_ = bf16[1024,256]{1,0:T(8,128)(2,1)S(1)} collective-permute-done((bf16[1024,256]{1,0:T(8,128)(2,1)S(1)}, bf16[1024,256]{1,0:T(8,128)(2,1)S(1)}, u32[]{:S(2)}, u32[]{:S(2)}) %collective-permute-start.14) | collective-permute-done | bytes 524320 | tf_op jit(solution)/shard_map/ppermute | solution.py:17
  71.4 2.8 %forward_side.1 = (bf16[40,3584]{1,0:T(8,128)(2,1)S(1)}, bf16[40,3584]{1,0:T(8,128)(2,1)S(1)}, bf16[40,3584]{1,0:T(8,128)(2,1)S(1)}, f32[40,3584]{1,0:T(8,128)S(1)}) custom-call(bf16[160,3584]{1,0:T(8,128)(2,1)S(1)} %get-tuple-element.63.x_ref, f32[160,3584]{1,0:T(8,128)S(1)} %get-tuple-element.64.part_ref, ...), custom_call_target="tpu_custom_call" | custom-call | flops 1000000 | tf_op jit(solution)/shard_map/forward_side/pallas_call | solution.py:53
  74.2 1.9 %collective-permute-start.17 = (bf16[40,3584]{1,0:T(8,128)(2,1)S(1)}, bf16[40,3584]{1,0:T(8,128)(2,1)S(1)}, u32[]{:S(2)}, u32[]{:S(2)}) collective-permute-start(bf16[40,3584]{1,0:T(8,128)(2,1)S(1)} %get-tuple-element.72), channel_id=1, source_target_pairs={{0,4},{1,5},{2,6},{3,7},{4,0},{5,1},{6,2},{7,3},{8,12},{9,13},{10,... | collective-permute-start | bytes 860168 | tf_op jit(solution)/shard_map/ppermute | solution.py:17
  78.5 2.6 %collective-permute-start.16 = (bf16[40,3584]{1,0:T(8,128)(2,1)S(1)}, bf16[40,3584]{1,0:T(8,128)(2,1)S(1)}, u32[]{:S(2)}, u32[]{:S(2)}) collective-permute-start(bf16[40,3584]{1,0:T(8,128)(2,1)S(1)} %get-tuple-element.70), channel_id=1, source_target_pairs={{0,20},{1,21},{2,22},{3,23},{4,16},{5,17},{6,18},{7,19},{8,28},{9,... | collective-permute-start | bytes 860168 | tf_op jit(solution)/shard_map/ppermute | solution.py:32
  81.1 6.7 %backward.1 = (bf16[40,3584]{1,0:T(8,128)(2,1)S(1)}, bf16[40,3584]{1,0:T(8,128)(2,1)S(1)}, bf16[40,3584]{1,0:T(8,128)(2,1)S(1)}, f32[40,3584]{1,0:T(8,128)S(1)}) custom-call(bf16[40,3584]{1,0:T(8,128)(2,1)S(1)} %copy-done.6, bf16[40,3584]{1,0:T(8,128)(2,1)S(1)} %get-tuple-element.51.refs_0_.refs_1_, ...), custom_call_target="tpu_custom_call" | custom-call | flops 1000000 | tf_op jit(solution)/shard_map/backward/pallas_call | solution.py:53
  88.8 3.7 %collective-permute-start.18 = (bf16[40,3584]{1,0:T(8,128)(2,1)S(1)}, bf16[40,3584]{1,0:T(8,128)(2,1)S(1)}, u32[]{:S(2)}, u32[]{:S(2)}) collective-permute-start(bf16[40,3584]{1,0:T(8,128)(2,1)S(1)} %add_convert_fusion.1), channel_id=1, source_target_pairs={{0,24},{1,25},{2,26},{3,27},{4,28},{5,29},{6,30},{7,31},{8,16},{9,... | collective-permute-start | bytes 860168 | tf_op jit(solution)/shard_map/ppermute | solution.py:32
  92.5 9.9 %collective-permute-done.20 = bf16[40,3584]{1,0:T(8,128)(2,1)S(1)} collective-permute-done((bf16[40,3584]{1,0:T(8,128)(2,1)S(1)}, bf16[40,3584]{1,0:T(8,128)(2,1)S(1)}, u32[]{:S(2)}, u32[]{:S(2)}) %collective-permute-start.20) | collective-permute-done | bytes 286752 | tf_op jit(solution)/shard_map/ppermute | solution.py:17
  102.9 3.4 %collective-permute-start.23 = (bf16[40,3584]{1,0:T(8,128)(2,1)S(1)}, bf16[40,3584]{1,0:T(8,128)(2,1)S(1)}, u32[]{:S(2)}, u32[]{:S(2)}) collective-permute-start(bf16[40,3584]{1,0:T(8,128)(2,1)S(1)} %add_convert_fusion), channel_id=1, source_target_pairs={{0,24},{1,25},{2,26},{3,27},{4,28},{5,29},{6,30},{7,31},{8,16},{9,... | collective-permute-start | bytes 860168 | tf_op jit(solution)/shard_map/ppermute | solution.py:32
  108.8 8.3 %collective-permute-done.22.rest_1_ = bf16[40,3584]{1,0:T(8,128)(2,1)S(1)} collective-permute-done((bf16[40,3584]{1,0:T(8,128)(2,1)S(1)}, bf16[40,3584]{1,0:T(8,128)(2,1)S(1)}, u32[]{:S(2)}, u32[]{:S(2)}) %collective-permute-start.22) | collective-permute-done | bytes 286752 | tf_op jit(solution)/shard_map/ppermute | solution.py:32
  (69 shorter events, 15.2 us)
Async XLA Ops:
  0.6 23.8 %collective-permute-start.3 = (bf16[256,1792]{1,0:T(8,128)(2,1)}, bf16[256,1792]{1,0:T(8,128)(2,1)}, u32[]{:S(2)}, u32[]{:S(2)}) collective-permute-start(bf16[256,1792]{1,0:T(8,128)(2,1)} %bitcast.16), channel_id=1, source_target_pairs={{0,2},{1,3},{2,0},{3,1},{4,6},{5,7},{6,4},{7,5},{8,10},{9,11},{10,... | collective-permute-start | bytes 2752520 | tf_op jit(solution)/shard_map/ppermute | solution.py:17
  6.3 18.1 %collective-permute-start.4 = (bf16[256,1792]{1,0:T(8,128)(2,1)S(1)}, bf16[256,1792]{1,0:T(8,128)(2,1)S(1)}, u32[]{:S(2)}, u32[]{:S(2)}) collective-permute-start(bf16[256,1792]{1,0:T(8,128)(2,1)S(1)} %bitcast.17), channel_id=1, source_target_pairs={{0,1},{1,0},{2,3},{3,2},{4,5},{5,4},{6,7},{7,6},{8,9},{9,8},{10,11... | collective-permute-start | bytes 2752520 | tf_op jit(solution)/shard_map/ppermute | solution.py:17
  6.4 18.0 %collective-permute-start = (bf16[64,3712]{1,0:T(8,128)(2,1)}, bf16[64,3712]{1,0:T(8,128)(2,1)S(1)}, u32[]{:S(2)}, u32[]{:S(2)}) collective-permute-start(bf16[64,3712]{1,0:T(8,128)(2,1)} %get-tuple-element.42), channel_id=1, source_target_pairs={{0,16},{1,17},{2,18},{3,19},{4,20},{5,21},{6,22},{7,23},{8,24},{9,... | collective-permute-start | bytes 1425416 | tf_op jit(solution)/shard_map/ppermute | solution.py:32
  8.0 16.3 %collective-permute-start.1 = (bf16[40,3584]{1,0:T(8,128)(2,1)}, bf16[40,3584]{1,0:T(8,128)(2,1)S(1)}, u32[]{:S(2)}, u32[]{:S(2)}) collective-permute-start(bf16[40,3584]{1,0:T(8,128)(2,1)} %get-tuple-element.44), channel_id=1, source_target_pairs={{0,8},{1,9},{2,10},{3,11},{4,12},{5,13},{6,14},{7,15},{8,0},{9,1},... | collective-permute-start | bytes 860168 | tf_op jit(solution)/shard_map/ppermute | solution.py:22
  10.6 13.9 %collective-permute-start.2 = (bf16[40,3584]{1,0:T(8,128)(2,1)}, bf16[40,3584]{1,0:T(8,128)(2,1)S(1)}, u32[]{:S(2)}, u32[]{:S(2)}) collective-permute-start(bf16[40,3584]{1,0:T(8,128)(2,1)} %get-tuple-element.58.refs_0_), channel_id=1, source_target_pairs={{0,4},{1,5},{2,6},{3,7},{4,0},{5,1},{6,2},{7,3},{8,12},{9,13},{10,... | collective-permute-start | bytes 860168 | tf_op jit(solution)/shard_map/ppermute | solution.py:17
  24.5 29.9 %collective-permute-start.6 = (bf16[2560,256]{1,0:T(8,128)(2,1)S(1)}, bf16[2560,256]{1,0:T(8,128)(2,1)}, u32[]{:S(2)}, u32[]{:S(2)}) collective-permute-start(bf16[2560,256]{1,0:T(8,128)(2,1)S(1)} %get-tuple-element.50), channel_id=1, source_target_pairs={{0,2},{1,3},{2,0},{3,1},{4,6},{5,7},{6,4},{7,5},{8,10},{9,11},{10,... | collective-permute-start | bytes 3932168 | tf_op jit(solution)/shard_map/ppermute | solution.py:17
  26.1 28.3 %collective-permute-start.7 = (bf16[40,7168]{1,0:T(8,128)(2,1)S(1)}, bf16[40,7168]{1,0:T(8,128)(2,1)S(1)}, u32[]{:S(2)}, u32[]{:S(2)}) collective-permute-start(bf16[40,7168]{1,0:T(8,128)(2,1)S(1)} %get-tuple-element.53), channel_id=1, source_target_pairs={{0,8},{1,9},{2,10},{3,11},{4,12},{5,13},{6,14},{7,15},{8,0},{9,1},... | collective-permute-start | bytes 1720328 | tf_op jit(solution)/shard_map/ppermute | solution.py:22
  29.5 25.0 %collective-permute-start.5 = (bf16[40,7168]{1,0:T(8,128)(2,1)}, bf16[40,7168]{1,0:T(8,128)(2,1)}, u32[]{:S(2)}, u32[]{:S(2)}) collective-permute-start(bf16[40,7168]{1,0:T(8,128)(2,1)} %join.1), channel_id=1, source_target_pairs={{0,4},{1,5},{2,6},{3,7},{4,0},{5,1},{6,2},{7,3},{8,12},{9,13},{10,... | collective-permute-start | bytes 1720328 | tf_op jit(solution)/shard_map/ppermute | solution.py:17
  31.1 23.4 %collective-permute-start.9 = (bf16[1792,256]{1,0:T(8,128)(2,1)}, bf16[1792,256]{1,0:T(8,128)(2,1)}, u32[]{:S(2)}, u32[]{:S(2)}) collective-permute-start(bf16[1792,256]{1,0:T(8,128)(2,1)} %bitcast.9.up_ref.refs_5_.refs_7_), channel_id=1, source_target_pairs={{0,1},{1,0},{2,3},{3,2},{4,5},{5,4},{6,7},{7,6},{8,9},{9,8},{10,11... | collective-permute-start | bytes 2752520 | tf_op jit(solution)/shard_map/ppermute | solution.py:17
  31.1 23.4 %collective-permute-start.8 = (bf16[64,7296]{1,0:T(8,128)(2,1)}, bf16[64,7296]{1,0:T(8,128)(2,1)}, u32[]{:S(2)}, u32[]{:S(2)}) collective-permute-start(bf16[64,7296]{1,0:T(8,128)(2,1)} %get-tuple-element.55), channel_id=1, source_target_pairs={{0,16},{1,17},{2,18},{3,19},{4,20},{5,21},{6,22},{7,23},{8,24},{9,... | collective-permute-start | bytes 2801672 | tf_op jit(solution)/shard_map/ppermute | solution.py:32
  54.5 14.9 %collective-permute-start.13 = (bf16[2560,256]{1,0:T(8,128)(2,1)}, bf16[2560,256]{1,0:T(8,128)(2,1)S(1)}, u32[]{:S(2)}, u32[]{:S(2)}) collective-permute-start(bf16[2560,256]{1,0:T(8,128)(2,1)} %collective-permute-done.6.refs_0_.refs_12_), channel_id=1, source_target_pairs={{0,1},{1,0},{2,3},{3,2},{4,5},{5,4},{6,7},{7,6},{8,9},{9,8},{10,11... | collective-permute-start | bytes 3932168 | tf_op jit(solution)/shard_map/ppermute | solution.py:17
  54.6 5.9 %collective-permute-start.10 = (bf16[256,1792]{1,0:T(8,128)(2,1)}, bf16[256,1792]{1,0:T(8,128)(2,1)S(1)}, u32[]{:S(2)}, u32[]{:S(2)}) collective-permute-start(bf16[256,1792]{1,0:T(8,128)(2,1)} %collective-permute-done.3.refs_2_.refs_14_), channel_id=1, source_target_pairs={{0,1},{1,0},{2,3},{3,2},{4,5},{5,4},{6,7},{7,6},{8,9},{9,8},{10,11... | collective-permute-start | bytes 2752520 | tf_op jit(solution)/shard_map/ppermute | solution.py:17
  55.1 5.4 %collective-permute-start.11 = (bf16[1792,256]{1,0:T(8,128)(2,1)S(1)}, bf16[1792,256]{1,0:T(8,128)(2,1)S(1)}, u32[]{:S(2)}, u32[]{:S(2)}) collective-permute-start(bf16[1792,256]{1,0:T(8,128)(2,1)S(1)} %bitcast.13), channel_id=1, source_target_pairs={{0,1},{1,0},{2,3},{3,2},{4,5},{5,4},{6,7},{7,6},{8,9},{9,8},{10,11... | collective-permute-start | bytes 2752520 | tf_op jit(solution)/shard_map/ppermute | solution.py:17
  55.2 14.3 %collective-permute-start.12 = (bf16[1024,256]{1,0:T(8,128)(2,1)S(1)}, bf16[1024,256]{1,0:T(8,128)(2,1)S(1)}, u32[]{:S(2)}, u32[]{:S(2)}) collective-permute-start(bf16[1024,256]{1,0:T(8,128)(2,1)S(1)} %get-tuple-element.66), channel_id=1, source_target_pairs={{0,2},{1,3},{2,0},{3,1},{4,6},{5,7},{6,4},{7,5},{8,10},{9,11},{10,... | collective-permute-start | bytes 1572872 | tf_op jit(solution)/shard_map/ppermute | solution.py:17
  56.6 21.8 %collective-permute-start.19 = (bf16[40,10752]{1,0:T(8,128)(2,1)S(1)}, bf16[40,10752]{1,0:T(8,128)(2,1)S(1)}, u32[]{:S(2)}, u32[]{:S(2)}) collective-permute-start(bf16[40,10752]{1,0:T(8,128)(2,1)S(1)} %join_back.1), channel_id=1, source_target_pairs={{0,4},{1,5},{2,6},{3,7},{4,0},{5,1},{6,2},{7,3},{8,12},{9,13},{10,... | collective-permute-start | bytes 2580488 | tf_op jit(solution)/shard_map/ppermute | solution.py:17
  69.5 1.9 %collective-permute-start.14 = (bf16[1024,256]{1,0:T(8,128)(2,1)S(1)}, bf16[1024,256]{1,0:T(8,128)(2,1)S(1)}, u32[]{:S(2)}, u32[]{:S(2)}) collective-permute-start(bf16[1024,256]{1,0:T(8,128)(2,1)S(1)} %collective-permute-done.12.refs_1_.refs_13_), channel_id=1, source_target_pairs={{0,1},{1,0},{2,3},{3,2},{4,5},{5,4},{6,7},{7,6},{8,9},{9,8},{10,11... | collective-permute-start | bytes 1572872 | tf_op jit(solution)/shard_map/ppermute | solution.py:17
  74.2 13.5 %collective-permute-start.17 = (bf16[40,3584]{1,0:T(8,128)(2,1)S(1)}, bf16[40,3584]{1,0:T(8,128)(2,1)S(1)}, u32[]{:S(2)}, u32[]{:S(2)}) collective-permute-start(bf16[40,3584]{1,0:T(8,128)(2,1)S(1)} %get-tuple-element.72), channel_id=1, source_target_pairs={{0,4},{1,5},{2,6},{3,7},{4,0},{5,1},{6,2},{7,3},{8,12},{9,13},{10,... | collective-permute-start | bytes 860168 | tf_op jit(solution)/shard_map/ppermute | solution.py:17
  76.1 31.4 %collective-permute-start.15 = (bf16[40,3584]{1,0:T(8,128)(2,1)S(1)}, bf16[40,3584]{1,0:T(8,128)(2,1)S(1)}, u32[]{:S(2)}, u32[]{:S(2)}) collective-permute-start(bf16[40,3584]{1,0:T(8,128)(2,1)S(1)} %get-tuple-element.69), channel_id=1, source_target_pairs={{0,16},{1,17},{2,18},{3,19},{4,20},{5,21},{6,22},{7,23},{8,24},{9,... | collective-permute-start | bytes 860168 | tf_op jit(solution)/shard_map/ppermute | solution.py:32
  78.5 24.5 %collective-permute-start.16 = (bf16[40,3584]{1,0:T(8,128)(2,1)S(1)}, bf16[40,3584]{1,0:T(8,128)(2,1)S(1)}, u32[]{:S(2)}, u32[]{:S(2)}) collective-permute-start(bf16[40,3584]{1,0:T(8,128)(2,1)S(1)} %get-tuple-element.70), channel_id=1, source_target_pairs={{0,20},{1,21},{2,22},{3,23},{4,16},{5,17},{6,18},{7,19},{8,28},{9,... | collective-permute-start | bytes 860168 | tf_op jit(solution)/shard_map/ppermute | solution.py:32
  87.8 14.6 %collective-permute-start.20 = (bf16[40,3584]{1,0:T(8,128)(2,1)S(1)}, bf16[40,3584]{1,0:T(8,128)(2,1)S(1)}, u32[]{:S(2)}, u32[]{:S(2)}) collective-permute-start(bf16[40,3584]{1,0:T(8,128)(2,1)S(1)} %get-tuple-element.75), channel_id=1, source_target_pairs={{0,4},{1,5},{2,6},{3,7},{4,0},{5,1},{6,2},{7,3},{8,12},{9,13},{10,... | collective-permute-start | bytes 860168 | tf_op jit(solution)/shard_map/ppermute | solution.py:17
  88.3 20.5 %collective-permute-start.21 = (bf16[40,3584]{1,0:T(8,128)(2,1)S(1)}, bf16[40,3584]{1,0:T(8,128)(2,1)S(1)}, u32[]{:S(2)}, u32[]{:S(2)}) collective-permute-start(bf16[40,3584]{1,0:T(8,128)(2,1)S(1)} %get-tuple-element.78), channel_id=1, source_target_pairs={{0,16},{1,17},{2,18},{3,19},{4,20},{5,21},{6,22},{7,23},{8,24},{9,... | collective-permute-start | bytes 860168 | tf_op jit(solution)/shard_map/ppermute | solution.py:32
  88.8 18.8 %collective-permute-start.18 = (bf16[40,3584]{1,0:T(8,128)(2,1)S(1)}, bf16[40,3584]{1,0:T(8,128)(2,1)S(1)}, u32[]{:S(2)}, u32[]{:S(2)}) collective-permute-start(bf16[40,3584]{1,0:T(8,128)(2,1)S(1)} %add_convert_fusion.1), channel_id=1, source_target_pairs={{0,24},{1,25},{2,26},{3,27},{4,28},{5,29},{6,30},{7,31},{8,16},{9,... | collective-permute-start | bytes 860168 | tf_op jit(solution)/shard_map/ppermute | solution.py:32
  102.4 14.8 %collective-permute-start.22 = (bf16[40,3584]{1,0:T(8,128)(2,1)S(1)}, bf16[40,3584]{1,0:T(8,128)(2,1)S(1)}, u32[]{:S(2)}, u32[]{:S(2)}) collective-permute-start(bf16[40,3584]{1,0:T(8,128)(2,1)S(1)} %get-tuple-element.80), channel_id=1, source_target_pairs={{0,20},{1,21},{2,22},{3,23},{4,16},{5,17},{6,18},{7,19},{8,28},{9,... | collective-permute-start | bytes 860168 | tf_op jit(solution)/shard_map/ppermute | solution.py:32
  102.9 14.3 %collective-permute-start.23 = (bf16[40,3584]{1,0:T(8,128)(2,1)S(1)}, bf16[40,3584]{1,0:T(8,128)(2,1)S(1)}, u32[]{:S(2)}, u32[]{:S(2)}) collective-permute-start(bf16[40,3584]{1,0:T(8,128)(2,1)S(1)} %add_convert_fusion), channel_id=1, source_target_pairs={{0,24},{1,25},{2,26},{3,27},{4,28},{5,29},{6,30},{7,31},{8,16},{9,... | collective-permute-start | bytes 860168 | tf_op jit(solution)/shard_map/ppermute | solution.py:32
  (16 other events, 188.0 us)

commit v6 on v5

--- a/solution.py
+++ b/solution.py
@@ -48,7 +48,7 @@
     return lax.dot_general(a, b, (((0,), (0,)), ((), ())), preferred_element_type=jnp.float32)
 
 
-def call(kernel, name, outs, cost, args, held=4, scratch=()):
+def call(kernel, name, outs, cost, args, held=1, scratch=()):
     space = pl.BlockSpec(memory_space=pltpu.VMEM)
     return pl.pallas_call(
         kernel,

time: 120 us -> 120 us (level)
  no operation moved by 1% of the time
where the time goes in v6:
time: 120 us; the launch traced here: 119 us
  waiting for transfers between devices  59.7 us (50%)
  starting transfers between devices  33.8 us (28%)
  Pallas kernels  22.9 us (19%)
  local copies, waits for them, and re-layouts  1.25 us (1%)
    ppermute x14, waiting for transfers between devices, swap(): lax.ppermute(value, 'ep', [(i, i ^ bit) for i in range(lax.axis_size('ep'...  42.4 us
    pallas_call x9, Pallas kernels, call(): pl.pallas_call(kernel, name=name, out_shape=[jax.ShapeDtypeStruct(shape,...  18.9 us
    ppermute x8, starting transfers between devices, to_section(): return lax.ppermute(value, ('pp', 'ep'), pairs)  14.8 us
    ppermute x14, starting transfers between devices, swap(): lax.ppermute(value, 'ep', [(i, i ^ bit) for i in range(lax.axis_size('ep'...  13.9 us
    ppermute x2, waiting for transfers between devices, to_expert(): lax.ppermute(value, 'ep', [(i, (i + SLICES * shift) % count) for i in ran...  9 us
    ppermute x8, waiting for transfers between devices, to_section(): return lax.ppermute(value, ('pp', 'ep'), pairs)  8.36 us
    ppermute x2, starting transfers between devices, to_expert(): lax.ppermute(value, 'ep', [(i, (i + SLICES * shift) % count) for i in ran...  5.18 us
    pallas_call x1, Pallas kernels, call_fetching(): pl.pallas_call(fetching, name=name, out_shape=[jax.ShapeDtypeStruct(shape...  2.6 us
  transfers between devices with their start and end apart: 24, of which 9 were waited for; matrix products, arithmetic and copies ran while one was open for 0% of the time, Pallas kernels for 18%

profile of v6, /device:TPU:0, one launch (start us, length us, event | category | flops | bytes accessed | tf_op | source)
XLA Modules:
  0.0 118.7 jit_solution(13841156708824978939)
XLA Ops:
  0.6 3.0 %collective-permute-start.3 = (bf16[256,1792]{1,0:T(8,128)(2,1)}, bf16[256,1792]{1,0:T(8,128)(2,1)}, u32[]{:S(2)}, u32[]{:S(2)}) collective-permute-start(bf16[256,1792]{1,0:T(8,128)(2,1)} %bitcast.16), channel_id=1, source_target_pairs={{0,2},{1,3},{2,0},{3,1},{4,6},{5,7},{6,4},{7,5},{8,10},{9,11},{10,... | collective-permute-start | bytes 2752520 | tf_op jit(solution)/shard_map/ppermute | solution.py:17
  3.7 2.6 %prepare.1 = (bf16[64,3712]{1,0:T(8,128)(2,1)}, bf16[40,3584]{1,0:T(8,128)(2,1)}, bf16[40,3584]{1,0:T(8,128)(2,1)}) custom-call(s32[1,64]{1,0:T(1,128)} %bitcast.27, f32[1,64]{1,0:T(1,128)} %bitcast.28, bf16[64,3584]{1,0:T(8,128)(2,1)} %bitcast.26, f32[1,3584]{1,0:T(1,128)} %refs_5_.1), custom_call_target="tpu_custom_call" | custom-call | flops 199999995904 | tf_op jit(solution)/shard_map/prepare/pallas_call | solution.py:81
  6.4 1.6 %collective-permute-start = (bf16[64,3712]{1,0:T(8,128)(2,1)}, bf16[64,3712]{1,0:T(8,128)(2,1)S(1)}, u32[]{:S(2)}, u32[]{:S(2)}) collective-permute-start(bf16[64,3712]{1,0:T(8,128)(2,1)} %get-tuple-element.42), channel_id=1, source_target_pairs={{0,16},{1,17},{2,18},{3,19},{4,20},{5,21},{6,22},{7,23},{8,24},{9,... | collective-permute-start | bytes 1425416 | tf_op jit(solution)/shard_map/ppermute | solution.py:32
  8.0 2.6 %collective-permute-start.1 = (bf16[40,3584]{1,0:T(8,128)(2,1)}, bf16[40,3584]{1,0:T(8,128)(2,1)S(1)}, u32[]{:S(2)}, u32[]{:S(2)}) collective-permute-start(bf16[40,3584]{1,0:T(8,128)(2,1)} %get-tuple-element.44), channel_id=1, source_target_pairs={{0,8},{1,9},{2,10},{3,11},{4,12},{5,13},{6,14},{7,15},{8,0},{9,1},... | collective-permute-start | bytes 860168 | tf_op jit(solution)/shard_map/ppermute | solution.py:22
  10.6 1.6 %collective-permute-start.2 = (bf16[40,3584]{1,0:T(8,128)(2,1)}, bf16[40,3584]{1,0:T(8,128)(2,1)S(1)}, u32[]{:S(2)}, u32[]{:S(2)}) collective-permute-start(bf16[40,3584]{1,0:T(8,128)(2,1)} %get-tuple-element.58.refs_0_), channel_id=1, source_target_pairs={{0,4},{1,5},{2,6},{3,7},{4,0},{5,1},{6,2},{7,3},{8,12},{9,13},{10,... | collective-permute-start | bytes 860168 | tf_op jit(solution)/shard_map/ppermute | solution.py:17
  13.6 1.6 %prepare_back.1 = (bf16[64,7296]{1,0:T(8,128)(2,1)}, bf16[40,3584]{1,0:T(8,128)(2,1)S(1)}, bf16[40,3584]{1,0:T(8,128)(2,1)S(1)}, bf16[40,7168]{1,0:T(8,128)(2,1)S(1)}) custom-call(s32[1,64]{1,0:T(1,128)S(1)} %bitcast.22, f32[1,64]{1,0:T(1,128)S(1)} %bitcast.23, bf16[64,3584]{1,0:T(8,128)(2,1)S(1)} %bitcast.20, bf16[64,3584]{1,0:T(8,128)(2,1)S(1)} %bitcast.21, ...), custom_call_target="tpu_custom_call" | custom-call | flops 1000000 | tf_op jit(solution)/shard_map/prepare_back/pallas_call | solution.py:53
  15.3 9.0 %collective-permute-done.1.refs_0_.refs_1_ = bf16[40,3584]{1,0:T(8,128)(2,1)S(1)} collective-permute-done((bf16[40,3584]{1,0:T(8,128)(2,1)}, bf16[40,3584]{1,0:T(8,128)(2,1)S(1)}, u32[]{:S(2)}, u32[]{:S(2)}) %collective-permute-start.1) | collective-permute-done | bytes 286752 | tf_op jit(solution)/shard_map/ppermute | solution.py:22
  24.5 1.6 %collective-permute-start.6 = (bf16[2560,256]{1,0:T(8,128)(2,1)S(1)}, bf16[2560,256]{1,0:T(8,128)(2,1)}, u32[]{:S(2)}, u32[]{:S(2)}) collective-permute-start(bf16[2560,256]{1,0:T(8,128)(2,1)S(1)} %get-tuple-element.50), channel_id=1, source_target_pairs={{0,2},{1,3},{2,0},{3,1},{4,6},{5,7},{6,4},{7,5},{8,10},{9,11},{10,... | collective-permute-start | bytes 3932168 | tf_op jit(solution)/shard_map/ppermute | solution.py:17
  26.1 2.6 %collective-permute-start.7 = (bf16[40,7168]{1,0:T(8,128)(2,1)S(1)}, bf16[40,7168]{1,0:T(8,128)(2,1)S(1)}, u32[]{:S(2)}, u32[]{:S(2)}) collective-permute-start(bf16[40,7168]{1,0:T(8,128)(2,1)S(1)} %get-tuple-element.53), channel_id=1, source_target_pairs={{0,8},{1,9},{2,10},{3,11},{4,12},{5,13},{6,14},{7,15},{8,0},{9,1},... | collective-permute-start | bytes 1720328 | tf_op jit(solution)/shard_map/ppermute | solution.py:22
  29.5 1.6 %collective-permute-start.5 = (bf16[40,7168]{1,0:T(8,128)(2,1)}, bf16[40,7168]{1,0:T(8,128)(2,1)}, u32[]{:S(2)}, u32[]{:S(2)}) collective-permute-start(bf16[40,7168]{1,0:T(8,128)(2,1)} %join.1), channel_id=1, source_target_pairs={{0,4},{1,5},{2,6},{3,7},{4,0},{5,1},{6,2},{7,3},{8,12},{9,13},{10,... | collective-permute-start | bytes 1720328 | tf_op jit(solution)/shard_map/ppermute | solution.py:17
  32.6 21.8 %collective-permute-done.6.refs_0_.refs_12_ = bf16[2560,256]{1,0:T(8,128)(2,1)} collective-permute-done((bf16[2560,256]{1,0:T(8,128)(2,1)S(1)}, bf16[2560,256]{1,0:T(8,128)(2,1)}, u32[]{:S(2)}, u32[]{:S(2)}) %collective-permute-start.6) | collective-permute-done | bytes 1310752 | tf_op jit(solution)/shard_map/ppermute | solution.py:17
  56.6 1.6 %collective-permute-start.19 = (bf16[40,10752]{1,0:T(8,128)(2,1)S(1)}, bf16[40,10752]{1,0:T(8,128)(2,1)S(1)}, u32[]{:S(2)}, u32[]{:S(2)}) collective-permute-start(bf16[40,10752]{1,0:T(8,128)(2,1)S(1)} %join_back.1), channel_id=1, source_target_pairs={{0,4},{1,5},{2,6},{3,7},{4,0},{5,1},{6,2},{7,3},{8,12},{9,13},{10,... | collective-permute-start | bytes 2580488 | tf_op jit(solution)/shard_map/ppermute | solution.py:17
  58.2 2.3 %collective-permute-done.10.refs_5_.refs_17_ = bf16[256,1792]{1,0:T(8,128)(2,1)S(1)} collective-permute-done((bf16[256,1792]{1,0:T(8,128)(2,1)}, bf16[256,1792]{1,0:T(8,128)(2,1)S(1)}, u32[]{:S(2)}, u32[]{:S(2)}) %collective-permute-start.10) | collective-permute-done | bytes 917536 | tf_op jit(solution)/shard_map/ppermute | solution.py:17
  61.7 2.8 %forward_near.1 = (bf16[160,3584]{1,0:T(8,128)(2,1)S(1)}, f32[160,3584]{1,0:T(8,128)S(1)}) custom-call(bf16[40,3584]{1,0:T(8,128)(2,1)S(1)} %copy-done.11, bf16[40,3584]{1,0:T(8,128)(2,1)S(1)} %collective-permute-done.1.refs_0_.refs_1_, bf16[40,3584]{1,0:T(8,128)(2,1)S(1)} %collective-permute-done.2.refs_2_, ...), custom_call_target="tpu_custom_call" | custom-call | flops 1000000 | tf_op jit(solution)/shard_map/forward_near/pallas_call | solution.py:53
  64.5 5.0 %collective-permute-done.12.refs_1_.refs_13_ = bf16[1024,256]{1,0:T(8,128)(2,1)S(1)} collective-permute-done((bf16[1024,256]{1,0:T(8,128)(2,1)S(1)}, bf16[1024,256]{1,0:T(8,128)(2,1)S(1)}, u32[]{:S(2)}, u32[]{:S(2)}) %collective-permute-start.12) | collective-permute-done | bytes 524320 | tf_op jit(solution)/shard_map/ppermute | solution.py:17
  69.5 1.9 %collective-permute-done.14.refs_4_.refs_16_ = bf16[1024,256]{1,0:T(8,128)(2,1)S(1)} collective-permute-done((bf16[1024,256]{1,0:T(8,128)(2,1)S(1)}, bf16[1024,256]{1,0:T(8,128)(2,1)S(1)}, u32[]{:S(2)}, u32[]{:S(2)}) %collective-permute-start.14) | collective-permute-done | bytes 524320 | tf_op jit(solution)/shard_map/ppermute | solution.py:17
  71.4 2.8 %forward_side.1 = (bf16[40,3584]{1,0:T(8,128)(2,1)S(1)}, bf16[40,3584]{1,0:T(8,128)(2,1)S(1)}, bf16[40,3584]{1,0:T(8,128)(2,1)S(1)}, f32[40,3584]{1,0:T(8,128)S(1)}) custom-call(bf16[160,3584]{1,0:T(8,128)(2,1)S(1)} %get-tuple-element.63.x_ref, f32[160,3584]{1,0:T(8,128)S(1)} %get-tuple-element.64.part_ref, ...), custom_call_target="tpu_custom_call" | custom-call | flops 1000000 | tf_op jit(solution)/shard_map/forward_side/pallas_call | solution.py:53
  74.2 1.9 %collective-permute-start.17 = (bf16[40,3584]{1,0:T(8,128)(2,1)S(1)}, bf16[40,3584]{1,0:T(8,128)(2,1)S(1)}, u32[]{:S(2)}, u32[]{:S(2)}) collective-permute-start(bf16[40,3584]{1,0:T(8,128)(2,1)S(1)} %get-tuple-element.72), channel_id=1, source_target_pairs={{0,4},{1,5},{2,6},{3,7},{4,0},{5,1},{6,2},{7,3},{8,12},{9,13},{10,... | collective-permute-start | bytes 860168 | tf_op jit(solution)/shard_map/ppermute | solution.py:17
  78.5 2.6 %collective-permute-start.16 = (bf16[40,3584]{1,0:T(8,128)(2,1)S(1)}, bf16[40,3584]{1,0:T(8,128)(2,1)S(1)}, u32[]{:S(2)}, u32[]{:S(2)}) collective-permute-start(bf16[40,3584]{1,0:T(8,128)(2,1)S(1)} %get-tuple-element.70), channel_id=1, source_target_pairs={{0,20},{1,21},{2,22},{3,23},{4,16},{5,17},{6,18},{7,19},{8,28},{9,... | collective-permute-start | bytes 860168 | tf_op jit(solution)/shard_map/ppermute | solution.py:32
  81.1 6.7 %backward.1 = (bf16[40,3584]{1,0:T(8,128)(2,1)S(1)}, bf16[40,3584]{1,0:T(8,128)(2,1)S(1)}, bf16[40,3584]{1,0:T(8,128)(2,1)S(1)}, f32[40,3584]{1,0:T(8,128)S(1)}) custom-call(bf16[40,3584]{1,0:T(8,128)(2,1)S(1)} %copy-done.6, bf16[40,3584]{1,0:T(8,128)(2,1)S(1)} %get-tuple-element.51.refs_0_.refs_1_, ...), custom_call_target="tpu_custom_call" | custom-call | flops 1000000 | tf_op jit(solution)/shard_map/backward/pallas_call | solution.py:53
  88.8 3.7 %collective-permute-start.18 = (bf16[40,3584]{1,0:T(8,128)(2,1)S(1)}, bf16[40,3584]{1,0:T(8,128)(2,1)S(1)}, u32[]{:S(2)}, u32[]{:S(2)}) collective-permute-start(bf16[40,3584]{1,0:T(8,128)(2,1)S(1)} %add_convert_fusion.1), channel_id=1, source_target_pairs={{0,24},{1,25},{2,26},{3,27},{4,28},{5,29},{6,30},{7,31},{8,16},{9,... | collective-permute-start | bytes 860168 | tf_op jit(solution)/shard_map/ppermute | solution.py:32
  92.5 9.9 %collective-permute-done.20 = bf16[40,3584]{1,0:T(8,128)(2,1)S(1)} collective-permute-done((bf16[40,3584]{1,0:T(8,128)(2,1)S(1)}, bf16[40,3584]{1,0:T(8,128)(2,1)S(1)}, u32[]{:S(2)}, u32[]{:S(2)}) %collective-permute-start.20) | collective-permute-done | bytes 286752 | tf_op jit(solution)/shard_map/ppermute | solution.py:17
  102.9 3.4 %collective-permute-start.23 = (bf16[40,3584]{1,0:T(8,128)(2,1)S(1)}, bf16[40,3584]{1,0:T(8,128)(2,1)S(1)}, u32[]{:S(2)}, u32[]{:S(2)}) collective-permute-start(bf16[40,3584]{1,0:T(8,128)(2,1)S(1)} %add_convert_fusion), channel_id=1, source_target_pairs={{0,24},{1,25},{2,26},{3,27},{4,28},{5,29},{6,30},{7,31},{8,16},{9,... | collective-permute-start | bytes 860168 | tf_op jit(solution)/shard_map/ppermute | solution.py:32
  108.8 8.3 %collective-permute-done.22.rest_1_ = bf16[40,3584]{1,0:T(8,128)(2,1)S(1)} collective-permute-done((bf16[40,3584]{1,0:T(8,128)(2,1)S(1)}, bf16[40,3584]{1,0:T(8,128)(2,1)S(1)}, u32[]{:S(2)}, u32[]{:S(2)}) %collective-permute-start.22) | collective-permute-done | bytes 286752 | tf_op jit(solution)/shard_map/ppermute | solution.py:32
  (69 shorter events, 15.2 us)
Async XLA Ops:
  0.6 23.8 %collective-permute-start.3 = (bf16[256,1792]{1,0:T(8,128)(2,1)}, bf16[256,1792]{1,0:T(8,128)(2,1)}, u32[]{:S(2)}, u32[]{:S(2)}) collective-permute-start(bf16[256,1792]{1,0:T(8,128)(2,1)} %bitcast.16), channel_id=1, source_target_pairs={{0,2},{1,3},{2,0},{3,1},{4,6},{5,7},{6,4},{7,5},{8,10},{9,11},{10,... | collective-permute-start | bytes 2752520 | tf_op jit(solution)/shard_map/ppermute | solution.py:17
  6.3 18.1 %collective-permute-start.4 = (bf16[256,1792]{1,0:T(8,128)(2,1)S(1)}, bf16[256,1792]{1,0:T(8,128)(2,1)S(1)}, u32[]{:S(2)}, u32[]{:S(2)}) collective-permute-start(bf16[256,1792]{1,0:T(8,128)(2,1)S(1)} %bitcast.17), channel_id=1, source_target_pairs={{0,1},{1,0},{2,3},{3,2},{4,5},{5,4},{6,7},{7,6},{8,9},{9,8},{10,11... | collective-permute-start | bytes 2752520 | tf_op jit(solution)/shard_map/ppermute | solution.py:17
  6.4 18.0 %collective-permute-start = (bf16[64,3712]{1,0:T(8,128)(2,1)}, bf16[64,3712]{1,0:T(8,128)(2,1)S(1)}, u32[]{:S(2)}, u32[]{:S(2)}) collective-permute-start(bf16[64,3712]{1,0:T(8,128)(2,1)} %get-tuple-element.42), channel_id=1, source_target_pairs={{0,16},{1,17},{2,18},{3,19},{4,20},{5,21},{6,22},{7,23},{8,24},{9,... | collective-permute-start | bytes 1425416 | tf_op jit(solution)/shard_map/ppermute | solution.py:32
  8.0 16.3 %collective-permute-start.1 = (bf16[40,3584]{1,0:T(8,128)(2,1)}, bf16[40,3584]{1,0:T(8,128)(2,1)S(1)}, u32[]{:S(2)}, u32[]{:S(2)}) collective-permute-start(bf16[40,3584]{1,0:T(8,128)(2,1)} %get-tuple-element.44), channel_id=1, source_target_pairs={{0,8},{1,9},{2,10},{3,11},{4,12},{5,13},{6,14},{7,15},{8,0},{9,1},... | collective-permute-start | bytes 860168 | tf_op jit(solution)/shard_map/ppermute | solution.py:22
  10.6 13.9 %collective-permute-start.2 = (bf16[40,3584]{1,0:T(8,128)(2,1)}, bf16[40,3584]{1,0:T(8,128)(2,1)S(1)}, u32[]{:S(2)}, u32[]{:S(2)}) collective-permute-start(bf16[40,3584]{1,0:T(8,128)(2,1)} %get-tuple-element.58.refs_0_), channel_id=1, source_target_pairs={{0,4},{1,5},{2,6},{3,7},{4,0},{5,1},{6,2},{7,3},{8,12},{9,13},{10,... | collective-permute-start | bytes 860168 | tf_op jit(solution)/shard_map/ppermute | solution.py:17
  24.5 29.9 %collective-permute-start.6 = (bf16[2560,256]{1,0:T(8,128)(2,1)S(1)}, bf16[2560,256]{1,0:T(8,128)(2,1)}, u32[]{:S(2)}, u32[]{:S(2)}) collective-permute-start(bf16[2560,256]{1,0:T(8,128)(2,1)S(1)} %get-tuple-element.50), channel_id=1, source_target_pairs={{0,2},{1,3},{2,0},{3,1},{4,6},{5,7},{6,4},{7,5},{8,10},{9,11},{10,... | collective-permute-start | bytes 3932168 | tf_op jit(solution)/shard_map/ppermute | solution.py:17
  26.1 28.3 %collective-permute-start.7 = (bf16[40,7168]{1,0:T(8,128)(2,1)S(1)}, bf16[40,7168]{1,0:T(8,128)(2,1)S(1)}, u32[]{:S(2)}, u32[]{:S(2)}) collective-permute-start(bf16[40,7168]{1,0:T(8,128)(2,1)S(1)} %get-tuple-element.53), channel_id=1, source_target_pairs={{0,8},{1,9},{2,10},{3,11},{4,12},{5,13},{6,14},{7,15},{8,0},{9,1},... | collective-permute-start | bytes 1720328 | tf_op jit(solution)/shard_map/ppermute | solution.py:22
  29.5 25.0 %collective-permute-start.5 = (bf16[40,7168]{1,0:T(8,128)(2,1)}, bf16[40,7168]{1,0:T(8,128)(2,1)}, u32[]{:S(2)}, u32[]{:S(2)}) collective-permute-start(bf16[40,7168]{1,0:T(8,128)(2,1)} %join.1), channel_id=1, source_target_pairs={{0,4},{1,5},{2,6},{3,7},{4,0},{5,1},{6,2},{7,3},{8,12},{9,13},{10,... | collective-permute-start | bytes 1720328 | tf_op jit(solution)/shard_map/ppermute | solution.py:17
  31.1 23.4 %collective-permute-start.9 = (bf16[1792,256]{1,0:T(8,128)(2,1)}, bf16[1792,256]{1,0:T(8,128)(2,1)}, u32[]{:S(2)}, u32[]{:S(2)}) collective-permute-start(bf16[1792,256]{1,0:T(8,128)(2,1)} %bitcast.9.up_ref.refs_5_.refs_7_), channel_id=1, source_target_pairs={{0,1},{1,0},{2,3},{3,2},{4,5},{5,4},{6,7},{7,6},{8,9},{9,8},{10,11... | collective-permute-start | bytes 2752520 | tf_op jit(solution)/shard_map/ppermute | solution.py:17
  31.1 23.4 %collective-permute-start.8 = (bf16[64,7296]{1,0:T(8,128)(2,1)}, bf16[64,7296]{1,0:T(8,128)(2,1)}, u32[]{:S(2)}, u32[]{:S(2)}) collective-permute-start(bf16[64,7296]{1,0:T(8,128)(2,1)} %get-tuple-element.55), channel_id=1, source_target_pairs={{0,16},{1,17},{2,18},{3,19},{4,20},{5,21},{6,22},{7,23},{8,24},{9,... | collective-permute-start | bytes 2801672 | tf_op jit(solution)/shard_map/ppermute | solution.py:32
  54.5 14.9 %collective-permute-start.13 = (bf16[2560,256]{1,0:T(8,128)(2,1)}, bf16[2560,256]{1,0:T(8,128)(2,1)S(1)}, u32[]{:S(2)}, u32[]{:S(2)}) collective-permute-start(bf16[2560,256]{1,0:T(8,128)(2,1)} %collective-permute-done.6.refs_0_.refs_12_), channel_id=1, source_target_pairs={{0,1},{1,0},{2,3},{3,2},{4,5},{5,4},{6,7},{7,6},{8,9},{9,8},{10,11... | collective-permute-start | bytes 3932168 | tf_op jit(solution)/shard_map/ppermute | solution.py:17
  54.6 5.9 %collective-permute-start.10 = (bf16[256,1792]{1,0:T(8,128)(2,1)}, bf16[256,1792]{1,0:T(8,128)(2,1)S(1)}, u32[]{:S(2)}, u32[]{:S(2)}) collective-permute-start(bf16[256,1792]{1,0:T(8,128)(2,1)} %collective-permute-done.3.refs_2_.refs_14_), channel_id=1, source_target_pairs={{0,1},{1,0},{2,3},{3,2},{4,5},{5,4},{6,7},{7,6},{8,9},{9,8},{10,11... | collective-permute-start | bytes 2752520 | tf_op jit(solution)/shard_map/ppermute | solution.py:17
  55.1 5.4 %collective-permute-start.11 = (bf16[1792,256]{1,0:T(8,128)(2,1)S(1)}, bf16[1792,256]{1,0:T(8,128)(2,1)S(1)}, u32[]{:S(2)}, u32[]{:S(2)}) collective-permute-start(bf16[1792,256]{1,0:T(8,128)(2,1)S(1)} %bitcast.13), channel_id=1, source_target_pairs={{0,1},{1,0},{2,3},{3,2},{4,5},{5,4},{6,7},{7,6},{8,9},{9,8},{10,11... | collective-permute-start | bytes 2752520 | tf_op jit(solution)/shard_map/ppermute | solution.py:17
  55.2 14.3 %collective-permute-start.12 = (bf16[1024,256]{1,0:T(8,128)(2,1)S(1)}, bf16[1024,256]{1,0:T(8,128)(2,1)S(1)}, u32[]{:S(2)}, u32[]{:S(2)}) collective-permute-start(bf16[1024,256]{1,0:T(8,128)(2,1)S(1)} %get-tuple-element.66), channel_id=1, source_target_pairs={{0,2},{1,3},{2,0},{3,1},{4,6},{5,7},{6,4},{7,5},{8,10},{9,11},{10,... | collective-permute-start | bytes 1572872 | tf_op jit(solution)/shard_map/ppermute | solution.py:17
  56.6 21.8 %collective-permute-start.19 = (bf16[40,10752]{1,0:T(8,128)(2,1)S(1)}, bf16[40,10752]{1,0:T(8,128)(2,1)S(1)}, u32[]{:S(2)}, u32[]{:S(2)}) collective-permute-start(bf16[40,10752]{1,0:T(8,128)(2,1)S(1)} %join_back.1), channel_id=1, source_target_pairs={{0,4},{1,5},{2,6},{3,7},{4,0},{5,1},{6,2},{7,3},{8,12},{9,13},{10,... | collective-permute-start | bytes 2580488 | tf_op jit(solution)/shard_map/ppermute | solution.py:17
  69.5 1.9 %collective-permute-start.14 = (bf16[1024,256]{1,0:T(8,128)(2,1)S(1)}, bf16[1024,256]{1,0:T(8,128)(2,1)S(1)}, u32[]{:S(2)}, u32[]{:S(2)}) collective-permute-start(bf16[1024,256]{1,0:T(8,128)(2,1)S(1)} %collective-permute-done.12.refs_1_.refs_13_), channel_id=1, source_target_pairs={{0,1},{1,0},{2,3},{3,2},{4,5},{5,4},{6,7},{7,6},{8,9},{9,8},{10,11... | collective-permute-start | bytes 1572872 | tf_op jit(solution)/shard_map/ppermute | solution.py:17
  74.2 13.5 %collective-permute-start.17 = (bf16[40,3584]{1,0:T(8,128)(2,1)S(1)}, bf16[40,3584]{1,0:T(8,128)(2,1)S(1)}, u32[]{:S(2)}, u32[]{:S(2)}) collective-permute-start(bf16[40,3584]{1,0:T(8,128)(2,1)S(1)} %get-tuple-element.72), channel_id=1, source_target_pairs={{0,4},{1,5},{2,6},{3,7},{4,0},{5,1},{6,2},{7,3},{8,12},{9,13},{10,... | collective-permute-start | bytes 860168 | tf_op jit(solution)/shard_map/ppermute | solution.py:17
  76.1 31.4 %collective-permute-start.15 = (bf16[40,3584]{1,0:T(8,128)(2,1)S(1)}, bf16[40,3584]{1,0:T(8,128)(2,1)S(1)}, u32[]{:S(2)}, u32[]{:S(2)}) collective-permute-start(bf16[40,3584]{1,0:T(8,128)(2,1)S(1)} %get-tuple-element.69), channel_id=1, source_target_pairs={{0,16},{1,17},{2,18},{3,19},{4,20},{5,21},{6,22},{7,23},{8,24},{9,... | collective-permute-start | bytes 860168 | tf_op jit(solution)/shard_map/ppermute | solution.py:32
  78.5 24.5 %collective-permute-start.16 = (bf16[40,3584]{1,0:T(8,128)(2,1)S(1)}, bf16[40,3584]{1,0:T(8,128)(2,1)S(1)}, u32[]{:S(2)}, u32[]{:S(2)}) collective-permute-start(bf16[40,3584]{1,0:T(8,128)(2,1)S(1)} %get-tuple-element.70), channel_id=1, source_target_pairs={{0,20},{1,21},{2,22},{3,23},{4,16},{5,17},{6,18},{7,19},{8,28},{9,... | collective-permute-start | bytes 860168 | tf_op jit(solution)/shard_map/ppermute | solution.py:32
  87.8 14.6 %collective-permute-start.20 = (bf16[40,3584]{1,0:T(8,128)(2,1)S(1)}, bf16[40,3584]{1,0:T(8,128)(2,1)S(1)}, u32[]{:S(2)}, u32[]{:S(2)}) collective-permute-start(bf16[40,3584]{1,0:T(8,128)(2,1)S(1)} %get-tuple-element.75), channel_id=1, source_target_pairs={{0,4},{1,5},{2,6},{3,7},{4,0},{5,1},{6,2},{7,3},{8,12},{9,13},{10,... | collective-permute-start | bytes 860168 | tf_op jit(solution)/shard_map/ppermute | solution.py:17
  88.3 20.5 %collective-permute-start.21 = (bf16[40,3584]{1,0:T(8,128)(2,1)S(1)}, bf16[40,3584]{1,0:T(8,128)(2,1)S(1)}, u32[]{:S(2)}, u32[]{:S(2)}) collective-permute-start(bf16[40,3584]{1,0:T(8,128)(2,1)S(1)} %get-tuple-element.78), channel_id=1, source_target_pairs={{0,16},{1,17},{2,18},{3,19},{4,20},{5,21},{6,22},{7,23},{8,24},{9,... | collective-permute-start | bytes 860168 | tf_op jit(solution)/shard_map/ppermute | solution.py:32
  88.8 18.8 %collective-permute-start.18 = (bf16[40,3584]{1,0:T(8,128)(2,1)S(1)}, bf16[40,3584]{1,0:T(8,128)(2,1)S(1)}, u32[]{:S(2)}, u32[]{:S(2)}) collective-permute-start(bf16[40,3584]{1,0:T(8,128)(2,1)S(1)} %add_convert_fusion.1), channel_id=1, source_target_pairs={{0,24},{1,25},{2,26},{3,27},{4,28},{5,29},{6,30},{7,31},{8,16},{9,... | collective-permute-start | bytes 860168 | tf_op jit(solution)/shard_map/ppermute | solution.py:32
  102.4 14.8 %collective-permute-start.22 = (bf16[40,3584]{1,0:T(8,128)(2,1)S(1)}, bf16[40,3584]{1,0:T(8,128)(2,1)S(1)}, u32[]{:S(2)}, u32[]{:S(2)}) collective-permute-start(bf16[40,3584]{1,0:T(8,128)(2,1)S(1)} %get-tuple-element.80), channel_id=1, source_target_pairs={{0,20},{1,21},{2,22},{3,23},{4,16},{5,17},{6,18},{7,19},{8,28},{9,... | collective-permute-start | bytes 860168 | tf_op jit(solution)/shard_map/ppermute | solution.py:32
  102.9 14.3 %collective-permute-start.23 = (bf16[40,3584]{1,0:T(8,128)(2,1)S(1)}, bf16[40,3584]{1,0:T(8,128)(2,1)S(1)}, u32[]{:S(2)}, u32[]{:S(2)}) collective-permute-start(bf16[40,3584]{1,0:T(8,128)(2,1)S(1)} %add_convert_fusion), channel_id=1, source_target_pairs={{0,24},{1,25},{2,26},{3,27},{4,28},{5,29},{6,30},{7,31},{8,16},{9,... | collective-permute-start | bytes 860168 | tf_op jit(solution)/shard_map/ppermute | solution.py:32
  (16 other events, 188.0 us)

commit v7 on v6

--- a/solution.py
+++ b/solution.py
@@ -370,13 +370,17 @@
             put_rows(capacity, gain * total, k * half + begin, *outs)
 
 
-def send_sums(far, received, experts, capacity, step):
-    sums = []
-    for r in range(1, experts):
-        rows = slice((r - 1) * capacity, r * capacity)
-        summed = (far[rows] + received[rows].astype(jnp.float32)).astype(jnp.bfloat16)
-        sums.append(to_section(summed, step, lambda i, r=r: i - SLICES * r))
-    return sums
+def add_rows(kept, received, count, capacity):
+    return [
+        (kept[rows] + received[rows].astype(jnp.float32)).astype(jnp.bfloat16)
+        for rows in (slice(i * capacity, (i + 1) * capacity) for i in range(count))
+    ]
+
+
+def send_sums(sums, step):
+    return [
+        to_section(part, step, lambda i, r=r: i - SLICES * r) for r, part in enumerate(sums, 1)
+    ]
 
 
 def body(
@@ -491,11 +495,12 @@
         scratch=(pltpu.VMEM(rows, jnp.bfloat16),) * 2,
     )
     bwd_received = swap(after(bwd_cross, fwd_received), FAR)
-    fwd_sums = send_sums(fwd_sum, fwd_received, experts, capacity, 1)
+    fwd_sums = send_sums(add_rows(fwd_sum, fwd_received, experts - 1, capacity), 1)
     bwd_near_sums = to_section(after(bwd_own, fwd_received), -1)
-    bwd_sums = send_sums(bwd_sum, bwd_received, experts, capacity, -1)
+    bwd_totals = add_rows(bwd_sum, bwd_received, experts - 1, capacity)
+    bwd_sums = send_sums(bwd_totals, -1)
     both = (fwd_received, bwd_received)
-    bwd_second = to_section(after(bwd_near, *both), -1, lambda i: i ^ FAR)
+    bwd_second = to_section(after(bwd_near, *both, *bwd_totals), -1, lambda i: i ^ FAR)
     fwd_back = (fwd_near_sums, fwd_second, *fwd_sums)
     bwd_back = (bwd_near_sums, bwd_second, *bwd_sums)
 

time: 120 us -> 120 us (level)
  no operation moved by 1% of the time
where the time goes in v7:
time: 120 us; the launch traced here: 119 us
  waiting for transfers between devices  59.8 us (50%)
  starting transfers between devices  33.8 us (28%)
  Pallas kernels  22.9 us (19%)
  local copies, waits for them, and re-layouts  1.25 us (1%)
    ppermute x14, waiting for transfers between devices, swap(): lax.ppermute(value, 'ep', [(i, i ^ bit) for i in range(lax.axis_size('ep'...  42.4 us
    pallas_call x9, Pallas kernels, call(): pl.pallas_call(kernel, name=name, out_shape=[jax.ShapeDtypeStruct(shape,...  18.9 us
    ppermute x8, starting transfers between devices, to_section(): return lax.ppermute(value, ('pp', 'ep'), pairs)  14.7 us
    ppermute x14, starting transfers between devices, swap(): lax.ppermute(value, 'ep', [(i, i ^ bit) for i in range(lax.axis_size('ep'...  13.9 us
    ppermute x2, waiting for transfers between devices, to_expert(): lax.ppermute(value, 'ep', [(i, (i + SLICES * shift) % count) for i in ran...  9 us
    ppermute x8, waiting for transfers between devices, to_section(): return lax.ppermute(value, ('pp', 'ep'), pairs)  8.48 us
    ppermute x2, starting transfers between devices, to_expert(): lax.ppermute(value, 'ep', [(i, (i + SLICES * shift) % count) for i in ran...  5.18 us
    pallas_call x1, Pallas kernels, call_fetching(): pl.pallas_call(fetching, name=name, out_shape=[jax.ShapeDtypeStruct(shape...  2.6 us
  transfers between devices with their start and end apart: 24, of which 9 were waited for; matrix products, arithmetic and copies ran while one was open for 0% of the time, Pallas kernels for 18%

profile of v7, /device:TPU:0, one launch (start us, length us, event | category | flops | bytes accessed | tf_op | source)
XLA Modules:
  0.0 118.8 jit_solution(1217081440737003095)
XLA Ops:
  0.6 3.0 %collective-permute-start.3 = (bf16[256,1792]{1,0:T(8,128)(2,1)}, bf16[256,1792]{1,0:T(8,128)(2,1)}, u32[]{:S(2)}, u32[]{:S(2)}) collective-permute-start(bf16[256,1792]{1,0:T(8,128)(2,1)} %bitcast.16), channel_id=1, source_target_pairs={{0,2},{1,3},{2,0},{3,1},{4,6},{5,7},{6,4},{7,5},{8,10},{9,11},{10,... | collective-permute-start | bytes 2752520 | tf_op jit(solution)/shard_map/ppermute | solution.py:17
  3.7 2.6 %prepare.1 = (bf16[64,3712]{1,0:T(8,128)(2,1)}, bf16[40,3584]{1,0:T(8,128)(2,1)}, bf16[40,3584]{1,0:T(8,128)(2,1)}) custom-call(s32[1,64]{1,0:T(1,128)} %bitcast.27, f32[1,64]{1,0:T(1,128)} %bitcast.28, bf16[64,3584]{1,0:T(8,128)(2,1)} %bitcast.26, f32[1,3584]{1,0:T(1,128)} %refs_5_.1), custom_call_target="tpu_custom_call" | custom-call | flops 199999995904 | tf_op jit(solution)/shard_map/prepare/pallas_call | solution.py:81
  6.4 1.6 %collective-permute-start = (bf16[64,3712]{1,0:T(8,128)(2,1)}, bf16[64,3712]{1,0:T(8,128)(2,1)S(1)}, u32[]{:S(2)}, u32[]{:S(2)}) collective-permute-start(bf16[64,3712]{1,0:T(8,128)(2,1)} %get-tuple-element.42), channel_id=1, source_target_pairs={{0,16},{1,17},{2,18},{3,19},{4,20},{5,21},{6,22},{7,23},{8,24},{9,... | collective-permute-start | bytes 1425416 | tf_op jit(solution)/shard_map/ppermute | solution.py:32
  8.0 2.6 %collective-permute-start.1 = (bf16[40,3584]{1,0:T(8,128)(2,1)}, bf16[40,3584]{1,0:T(8,128)(2,1)S(1)}, u32[]{:S(2)}, u32[]{:S(2)}) collective-permute-start(bf16[40,3584]{1,0:T(8,128)(2,1)} %get-tuple-element.44), channel_id=1, source_target_pairs={{0,8},{1,9},{2,10},{3,11},{4,12},{5,13},{6,14},{7,15},{8,0},{9,1},... | collective-permute-start | bytes 860168 | tf_op jit(solution)/shard_map/ppermute | solution.py:22
  10.6 1.6 %collective-permute-start.2 = (bf16[40,3584]{1,0:T(8,128)(2,1)}, bf16[40,3584]{1,0:T(8,128)(2,1)S(1)}, u32[]{:S(2)}, u32[]{:S(2)}) collective-permute-start(bf16[40,3584]{1,0:T(8,128)(2,1)} %get-tuple-element.58.refs_0_), channel_id=1, source_target_pairs={{0,4},{1,5},{2,6},{3,7},{4,0},{5,1},{6,2},{7,3},{8,12},{9,13},{10,... | collective-permute-start | bytes 860168 | tf_op jit(solution)/shard_map/ppermute | solution.py:17
  13.6 1.6 %prepare_back.1 = (bf16[64,7296]{1,0:T(8,128)(2,1)}, bf16[40,3584]{1,0:T(8,128)(2,1)S(1)}, bf16[40,3584]{1,0:T(8,128)(2,1)S(1)}, bf16[40,7168]{1,0:T(8,128)(2,1)S(1)}) custom-call(s32[1,64]{1,0:T(1,128)S(1)} %bitcast.22, f32[1,64]{1,0:T(1,128)S(1)} %bitcast.23, bf16[64,3584]{1,0:T(8,128)(2,1)S(1)} %bitcast.20, bf16[64,3584]{1,0:T(8,128)(2,1)S(1)} %bitcast.21, ...), custom_call_target="tpu_custom_call" | custom-call | flops 1000000 | tf_op jit(solution)/shard_map/prepare_back/pallas_call | solution.py:53
  15.3 9.0 %collective-permute-done.1.refs_0_.refs_1_ = bf16[40,3584]{1,0:T(8,128)(2,1)S(1)} collective-permute-done((bf16[40,3584]{1,0:T(8,128)(2,1)}, bf16[40,3584]{1,0:T(8,128)(2,1)S(1)}, u32[]{:S(2)}, u32[]{:S(2)}) %collective-permute-start.1) | collective-permute-done | bytes 286752 | tf_op jit(solution)/shard_map/ppermute | solution.py:22
  24.5 1.6 %collective-permute-start.6 = (bf16[2560,256]{1,0:T(8,128)(2,1)S(1)}, bf16[2560,256]{1,0:T(8,128)(2,1)}, u32[]{:S(2)}, u32[]{:S(2)}) collective-permute-start(bf16[2560,256]{1,0:T(8,128)(2,1)S(1)} %get-tuple-element.50), channel_id=1, source_target_pairs={{0,2},{1,3},{2,0},{3,1},{4,6},{5,7},{6,4},{7,5},{8,10},{9,11},{10,... | collective-permute-start | bytes 3932168 | tf_op jit(solution)/shard_map/ppermute | solution.py:17
  26.1 2.6 %collective-permute-start.7 = (bf16[40,7168]{1,0:T(8,128)(2,1)S(1)}, bf16[40,7168]{1,0:T(8,128)(2,1)S(1)}, u32[]{:S(2)}, u32[]{:S(2)}) collective-permute-start(bf16[40,7168]{1,0:T(8,128)(2,1)S(1)} %get-tuple-element.53), channel_id=1, source_target_pairs={{0,8},{1,9},{2,10},{3,11},{4,12},{5,13},{6,14},{7,15},{8,0},{9,1},... | collective-permute-start | bytes 1720328 | tf_op jit(solution)/shard_map/ppermute | solution.py:22
  29.5 1.6 %collective-permute-start.5 = (bf16[40,7168]{1,0:T(8,128)(2,1)}, bf16[40,7168]{1,0:T(8,128)(2,1)}, u32[]{:S(2)}, u32[]{:S(2)}) collective-permute-start(bf16[40,7168]{1,0:T(8,128)(2,1)} %join.1), channel_id=1, source_target_pairs={{0,4},{1,5},{2,6},{3,7},{4,0},{5,1},{6,2},{7,3},{8,12},{9,13},{10,... | collective-permute-start | bytes 1720328 | tf_op jit(solution)/shard_map/ppermute | solution.py:17
  32.6 21.8 %collective-permute-done.6.refs_0_.refs_12_ = bf16[2560,256]{1,0:T(8,128)(2,1)} collective-permute-done((bf16[2560,256]{1,0:T(8,128)(2,1)S(1)}, bf16[2560,256]{1,0:T(8,128)(2,1)}, u32[]{:S(2)}, u32[]{:S(2)}) %collective-permute-start.6) | collective-permute-done | bytes 1310752 | tf_op jit(solution)/shard_map/ppermute | solution.py:17
  56.6 1.6 %collective-permute-start.19 = (bf16[40,10752]{1,0:T(8,128)(2,1)S(1)}, bf16[40,10752]{1,0:T(8,128)(2,1)S(1)}, u32[]{:S(2)}, u32[]{:S(2)}) collective-permute-start(bf16[40,10752]{1,0:T(8,128)(2,1)S(1)} %join_back.1), channel_id=1, source_target_pairs={{0,4},{1,5},{2,6},{3,7},{4,0},{5,1},{6,2},{7,3},{8,12},{9,13},{10,... | collective-permute-start | bytes 2580488 | tf_op jit(solution)/shard_map/ppermute | solution.py:17
  58.2 2.3 %collective-permute-done.10.refs_5_.refs_17_ = bf16[256,1792]{1,0:T(8,128)(2,1)S(1)} collective-permute-done((bf16[256,1792]{1,0:T(8,128)(2,1)}, bf16[256,1792]{1,0:T(8,128)(2,1)S(1)}, u32[]{:S(2)}, u32[]{:S(2)}) %collective-permute-start.10) | collective-permute-done | bytes 917536 | tf_op jit(solution)/shard_map/ppermute | solution.py:17
  61.7 2.8 %forward_near.1 = (bf16[160,3584]{1,0:T(8,128)(2,1)S(1)}, f32[160,3584]{1,0:T(8,128)S(1)}) custom-call(bf16[40,3584]{1,0:T(8,128)(2,1)S(1)} %copy-done.11, bf16[40,3584]{1,0:T(8,128)(2,1)S(1)} %collective-permute-done.1.refs_0_.refs_1_, bf16[40,3584]{1,0:T(8,128)(2,1)S(1)} %collective-permute-done.2.refs_2_, ...), custom_call_target="tpu_custom_call" | custom-call | flops 1000000 | tf_op jit(solution)/shard_map/forward_near/pallas_call | solution.py:53
  64.5 5.0 %collective-permute-done.12.refs_1_.refs_13_ = bf16[1024,256]{1,0:T(8,128)(2,1)S(1)} collective-permute-done((bf16[1024,256]{1,0:T(8,128)(2,1)S(1)}, bf16[1024,256]{1,0:T(8,128)(2,1)S(1)}, u32[]{:S(2)}, u32[]{:S(2)}) %collective-permute-start.12) | collective-permute-done | bytes 524320 | tf_op jit(solution)/shard_map/ppermute | solution.py:17
  69.5 1.9 %collective-permute-done.14.refs_4_.refs_16_ = bf16[1024,256]{1,0:T(8,128)(2,1)S(1)} collective-permute-done((bf16[1024,256]{1,0:T(8,128)(2,1)S(1)}, bf16[1024,256]{1,0:T(8,128)(2,1)S(1)}, u32[]{:S(2)}, u32[]{:S(2)}) %collective-permute-start.14) | collective-permute-done | bytes 524320 | tf_op jit(solution)/shard_map/ppermute | solution.py:17
  71.4 2.8 %forward_side.1 = (bf16[40,3584]{1,0:T(8,128)(2,1)S(1)}, bf16[40,3584]{1,0:T(8,128)(2,1)S(1)}, bf16[40,3584]{1,0:T(8,128)(2,1)S(1)}, f32[40,3584]{1,0:T(8,128)S(1)}) custom-call(bf16[160,3584]{1,0:T(8,128)(2,1)S(1)} %get-tuple-element.63.x_ref, f32[160,3584]{1,0:T(8,128)S(1)} %get-tuple-element.64.part_ref, ...), custom_call_target="tpu_custom_call" | custom-call | flops 1000000 | tf_op jit(solution)/shard_map/forward_side/pallas_call | solution.py:53
  74.2 1.9 %collective-permute-start.17 = (bf16[40,3584]{1,0:T(8,128)(2,1)S(1)}, bf16[40,3584]{1,0:T(8,128)(2,1)S(1)}, u32[]{:S(2)}, u32[]{:S(2)}) collective-permute-start(bf16[40,3584]{1,0:T(8,128)(2,1)S(1)} %get-tuple-element.72), channel_id=1, source_target_pairs={{0,4},{1,5},{2,6},{3,7},{4,0},{5,1},{6,2},{7,3},{8,12},{9,13},{10,... | collective-permute-start | bytes 860168 | tf_op jit(solution)/shard_map/ppermute | solution.py:17
  78.5 2.6 %collective-permute-start.16 = (bf16[40,3584]{1,0:T(8,128)(2,1)S(1)}, bf16[40,3584]{1,0:T(8,128)(2,1)S(1)}, u32[]{:S(2)}, u32[]{:S(2)}) collective-permute-start(bf16[40,3584]{1,0:T(8,128)(2,1)S(1)} %get-tuple-element.70), channel_id=1, source_target_pairs={{0,20},{1,21},{2,22},{3,23},{4,16},{5,17},{6,18},{7,19},{8,28},{9,... | collective-permute-start | bytes 860168 | tf_op jit(solution)/shard_map/ppermute | solution.py:32
  81.1 6.7 %backward.1 = (bf16[40,3584]{1,0:T(8,128)(2,1)S(1)}, bf16[40,3584]{1,0:T(8,128)(2,1)S(1)}, bf16[40,3584]{1,0:T(8,128)(2,1)S(1)}, f32[40,3584]{1,0:T(8,128)S(1)}) custom-call(bf16[40,3584]{1,0:T(8,128)(2,1)S(1)} %copy-done.6, bf16[40,3584]{1,0:T(8,128)(2,1)S(1)} %get-tuple-element.51.refs_0_.refs_1_, ...), custom_call_target="tpu_custom_call" | custom-call | flops 1000000 | tf_op jit(solution)/shard_map/backward/pallas_call | solution.py:53
  88.8 3.7 %collective-permute-start.18 = (bf16[40,3584]{1,0:T(8,128)(2,1)S(1)}, bf16[40,3584]{1,0:T(8,128)(2,1)S(1)}, u32[]{:S(2)}, u32[]{:S(2)}) collective-permute-start(bf16[40,3584]{1,0:T(8,128)(2,1)S(1)} %add_convert_fusion.1), channel_id=1, source_target_pairs={{0,24},{1,25},{2,26},{3,27},{4,28},{5,29},{6,30},{7,31},{8,16},{9,... | collective-permute-start | bytes 860168 | tf_op jit(solution)/shard_map/ppermute | solution.py:32
  92.5 9.9 %collective-permute-done.20 = bf16[40,3584]{1,0:T(8,128)(2,1)S(1)} collective-permute-done((bf16[40,3584]{1,0:T(8,128)(2,1)S(1)}, bf16[40,3584]{1,0:T(8,128)(2,1)S(1)}, u32[]{:S(2)}, u32[]{:S(2)}) %collective-permute-start.20) | collective-permute-done | bytes 286752 | tf_op jit(solution)/shard_map/ppermute | solution.py:17
  103.0 3.3 %collective-permute-start.23 = (bf16[40,3584]{1,0:T(8,128)(2,1)S(1)}, bf16[40,3584]{1,0:T(8,128)(2,1)S(1)}, u32[]{:S(2)}, u32[]{:S(2)}) collective-permute-start(bf16[40,3584]{1,0:T(8,128)(2,1)S(1)} %add_convert_fusion), channel_id=1, source_target_pairs={{0,24},{1,25},{2,26},{3,27},{4,28},{5,29},{6,30},{7,31},{8,16},{9,... | collective-permute-start | bytes 860168 | tf_op jit(solution)/shard_map/ppermute | solution.py:32
  108.8 8.5 %collective-permute-done.22.rest_1_ = bf16[40,3584]{1,0:T(8,128)(2,1)S(1)} collective-permute-done((bf16[40,3584]{1,0:T(8,128)(2,1)S(1)}, bf16[40,3584]{1,0:T(8,128)(2,1)S(1)}, u32[]{:S(2)}, u32[]{:S(2)}) %collective-permute-start.22) | collective-permute-done | bytes 286752 | tf_op jit(solution)/shard_map/ppermute | solution.py:32
  (69 shorter events, 15.3 us)
Async XLA Ops:
  0.6 23.8 %collective-permute-start.3 = (bf16[256,1792]{1,0:T(8,128)(2,1)}, bf16[256,1792]{1,0:T(8,128)(2,1)}, u32[]{:S(2)}, u32[]{:S(2)}) collective-permute-start(bf16[256,1792]{1,0:T(8,128)(2,1)} %bitcast.16), channel_id=1, source_target_pairs={{0,2},{1,3},{2,0},{3,1},{4,6},{5,7},{6,4},{7,5},{8,10},{9,11},{10,... | collective-permute-start | bytes 2752520 | tf_op jit(solution)/shard_map/ppermute | solution.py:17
  6.3 18.1 %collective-permute-start.4 = (bf16[256,1792]{1,0:T(8,128)(2,1)S(1)}, bf16[256,1792]{1,0:T(8,128)(2,1)S(1)}, u32[]{:S(2)}, u32[]{:S(2)}) collective-permute-start(bf16[256,1792]{1,0:T(8,128)(2,1)S(1)} %bitcast.17), channel_id=1, source_target_pairs={{0,1},{1,0},{2,3},{3,2},{4,5},{5,4},{6,7},{7,6},{8,9},{9,8},{10,11... | collective-permute-start | bytes 2752520 | tf_op jit(solution)/shard_map/ppermute | solution.py:17
  6.4 18.0 %collective-permute-start = (bf16[64,3712]{1,0:T(8,128)(2,1)}, bf16[64,3712]{1,0:T(8,128)(2,1)S(1)}, u32[]{:S(2)}, u32[]{:S(2)}) collective-permute-start(bf16[64,3712]{1,0:T(8,128)(2,1)} %get-tuple-element.42), channel_id=1, source_target_pairs={{0,16},{1,17},{2,18},{3,19},{4,20},{5,21},{6,22},{7,23},{8,24},{9,... | collective-permute-start | bytes 1425416 | tf_op jit(solution)/shard_map/ppermute | solution.py:32
  8.0 16.3 %collective-permute-start.1 = (bf16[40,3584]{1,0:T(8,128)(2,1)}, bf16[40,3584]{1,0:T(8,128)(2,1)S(1)}, u32[]{:S(2)}, u32[]{:S(2)}) collective-permute-start(bf16[40,3584]{1,0:T(8,128)(2,1)} %get-tuple-element.44), channel_id=1, source_target_pairs={{0,8},{1,9},{2,10},{3,11},{4,12},{5,13},{6,14},{7,15},{8,0},{9,1},... | collective-permute-start | bytes 860168 | tf_op jit(solution)/shard_map/ppermute | solution.py:22
  10.6 13.9 %collective-permute-start.2 = (bf16[40,3584]{1,0:T(8,128)(2,1)}, bf16[40,3584]{1,0:T(8,128)(2,1)S(1)}, u32[]{:S(2)}, u32[]{:S(2)}) collective-permute-start(bf16[40,3584]{1,0:T(8,128)(2,1)} %get-tuple-element.58.refs_0_), channel_id=1, source_target_pairs={{0,4},{1,5},{2,6},{3,7},{4,0},{5,1},{6,2},{7,3},{8,12},{9,13},{10,... | collective-permute-start | bytes 860168 | tf_op jit(solution)/shard_map/ppermute | solution.py:17
  24.5 29.9 %collective-permute-start.6 = (bf16[2560,256]{1,0:T(8,128)(2,1)S(1)}, bf16[2560,256]{1,0:T(8,128)(2,1)}, u32[]{:S(2)}, u32[]{:S(2)}) collective-permute-start(bf16[2560,256]{1,0:T(8,128)(2,1)S(1)} %get-tuple-element.50), channel_id=1, source_target_pairs={{0,2},{1,3},{2,0},{3,1},{4,6},{5,7},{6,4},{7,5},{8,10},{9,11},{10,... | collective-permute-start | bytes 3932168 | tf_op jit(solution)/shard_map/ppermute | solution.py:17
  26.1 28.3 %collective-permute-start.7 = (bf16[40,7168]{1,0:T(8,128)(2,1)S(1)}, bf16[40,7168]{1,0:T(8,128)(2,1)S(1)}, u32[]{:S(2)}, u32[]{:S(2)}) collective-permute-start(bf16[40,7168]{1,0:T(8,128)(2,1)S(1)} %get-tuple-element.53), channel_id=1, source_target_pairs={{0,8},{1,9},{2,10},{3,11},{4,12},{5,13},{6,14},{7,15},{8,0},{9,1},... | collective-permute-start | bytes 1720328 | tf_op jit(solution)/shard_map/ppermute | solution.py:22
  29.5 25.0 %collective-permute-start.5 = (bf16[40,7168]{1,0:T(8,128)(2,1)}, bf16[40,7168]{1,0:T(8,128)(2,1)}, u32[]{:S(2)}, u32[]{:S(2)}) collective-permute-start(bf16[40,7168]{1,0:T(8,128)(2,1)} %join.1), channel_id=1, source_target_pairs={{0,4},{1,5},{2,6},{3,7},{4,0},{5,1},{6,2},{7,3},{8,12},{9,13},{10,... | collective-permute-start | bytes 1720328 | tf_op jit(solution)/shard_map/ppermute | solution.py:17
  31.1 23.4 %collective-permute-start.9 = (bf16[1792,256]{1,0:T(8,128)(2,1)}, bf16[1792,256]{1,0:T(8,128)(2,1)}, u32[]{:S(2)}, u32[]{:S(2)}) collective-permute-start(bf16[1792,256]{1,0:T(8,128)(2,1)} %bitcast.9.up_ref.refs_5_.refs_7_), channel_id=1, source_target_pairs={{0,1},{1,0},{2,3},{3,2},{4,5},{5,4},{6,7},{7,6},{8,9},{9,8},{10,11... | collective-permute-start | bytes 2752520 | tf_op jit(solution)/shard_map/ppermute | solution.py:17
  31.1 23.4 %collective-permute-start.8 = (bf16[64,7296]{1,0:T(8,128)(2,1)}, bf16[64,7296]{1,0:T(8,128)(2,1)}, u32[]{:S(2)}, u32[]{:S(2)}) collective-permute-start(bf16[64,7296]{1,0:T(8,128)(2,1)} %get-tuple-element.55), channel_id=1, source_target_pairs={{0,16},{1,17},{2,18},{3,19},{4,20},{5,21},{6,22},{7,23},{8,24},{9,... | collective-permute-start | bytes 2801672 | tf_op jit(solution)/shard_map/ppermute | solution.py:32
  54.5 14.9 %collective-permute-start.13 = (bf16[2560,256]{1,0:T(8,128)(2,1)}, bf16[2560,256]{1,0:T(8,128)(2,1)S(1)}, u32[]{:S(2)}, u32[]{:S(2)}) collective-permute-start(bf16[2560,256]{1,0:T(8,128)(2,1)} %collective-permute-done.6.refs_0_.refs_12_), channel_id=1, source_target_pairs={{0,1},{1,0},{2,3},{3,2},{4,5},{5,4},{6,7},{7,6},{8,9},{9,8},{10,11... | collective-permute-start | bytes 3932168 | tf_op jit(solution)/shard_map/ppermute | solution.py:17
  54.6 5.9 %collective-permute-start.10 = (bf16[256,1792]{1,0:T(8,128)(2,1)}, bf16[256,1792]{1,0:T(8,128)(2,1)S(1)}, u32[]{:S(2)}, u32[]{:S(2)}) collective-permute-start(bf16[256,1792]{1,0:T(8,128)(2,1)} %collective-permute-done.3.refs_2_.refs_14_), channel_id=1, source_target_pairs={{0,1},{1,0},{2,3},{3,2},{4,5},{5,4},{6,7},{7,6},{8,9},{9,8},{10,11... | collective-permute-start | bytes 2752520 | tf_op jit(solution)/shard_map/ppermute | solution.py:17
  55.1 5.4 %collective-permute-start.11 = (bf16[1792,256]{1,0:T(8,128)(2,1)S(1)}, bf16[1792,256]{1,0:T(8,128)(2,1)S(1)}, u32[]{:S(2)}, u32[]{:S(2)}) collective-permute-start(bf16[1792,256]{1,0:T(8,128)(2,1)S(1)} %bitcast.13), channel_id=1, source_target_pairs={{0,1},{1,0},{2,3},{3,2},{4,5},{5,4},{6,7},{7,6},{8,9},{9,8},{10,11... | collective-permute-start | bytes 2752520 | tf_op jit(solution)/shard_map/ppermute | solution.py:17
  55.2 14.3 %collective-permute-start.12 = (bf16[1024,256]{1,0:T(8,128)(2,1)S(1)}, bf16[1024,256]{1,0:T(8,128)(2,1)S(1)}, u32[]{:S(2)}, u32[]{:S(2)}) collective-permute-start(bf16[1024,256]{1,0:T(8,128)(2,1)S(1)} %get-tuple-element.66), channel_id=1, source_target_pairs={{0,2},{1,3},{2,0},{3,1},{4,6},{5,7},{6,4},{7,5},{8,10},{9,11},{10,... | collective-permute-start | bytes 1572872 | tf_op jit(solution)/shard_map/ppermute | solution.py:17
  56.6 21.8 %collective-permute-start.19 = (bf16[40,10752]{1,0:T(8,128)(2,1)S(1)}, bf16[40,10752]{1,0:T(8,128)(2,1)S(1)}, u32[]{:S(2)}, u32[]{:S(2)}) collective-permute-start(bf16[40,10752]{1,0:T(8,128)(2,1)S(1)} %join_back.1), channel_id=1, source_target_pairs={{0,4},{1,5},{2,6},{3,7},{4,0},{5,1},{6,2},{7,3},{8,12},{9,13},{10,... | collective-permute-start | bytes 2580488 | tf_op jit(solution)/shard_map/ppermute | solution.py:17
  69.5 1.9 %collective-permute-start.14 = (bf16[1024,256]{1,0:T(8,128)(2,1)S(1)}, bf16[1024,256]{1,0:T(8,128)(2,1)S(1)}, u32[]{:S(2)}, u32[]{:S(2)}) collective-permute-start(bf16[1024,256]{1,0:T(8,128)(2,1)S(1)} %collective-permute-done.12.refs_1_.refs_13_), channel_id=1, source_target_pairs={{0,1},{1,0},{2,3},{3,2},{4,5},{5,4},{6,7},{7,6},{8,9},{9,8},{10,11... | collective-permute-start | bytes 1572872 | tf_op jit(solution)/shard_map/ppermute | solution.py:17
  74.2 13.5 %collective-permute-start.17 = (bf16[40,3584]{1,0:T(8,128)(2,1)S(1)}, bf16[40,3584]{1,0:T(8,128)(2,1)S(1)}, u32[]{:S(2)}, u32[]{:S(2)}) collective-permute-start(bf16[40,3584]{1,0:T(8,128)(2,1)S(1)} %get-tuple-element.72), channel_id=1, source_target_pairs={{0,4},{1,5},{2,6},{3,7},{4,0},{5,1},{6,2},{7,3},{8,12},{9,13},{10,... | collective-permute-start | bytes 860168 | tf_op jit(solution)/shard_map/ppermute | solution.py:17
  76.1 31.4 %collective-permute-start.15 = (bf16[40,3584]{1,0:T(8,128)(2,1)S(1)}, bf16[40,3584]{1,0:T(8,128)(2,1)S(1)}, u32[]{:S(2)}, u32[]{:S(2)}) collective-permute-start(bf16[40,3584]{1,0:T(8,128)(2,1)S(1)} %get-tuple-element.69), channel_id=1, source_target_pairs={{0,16},{1,17},{2,18},{3,19},{4,20},{5,21},{6,22},{7,23},{8,24},{9,... | collective-permute-start | bytes 860168 | tf_op jit(solution)/shard_map/ppermute | solution.py:32
  78.5 24.5 %collective-permute-start.16 = (bf16[40,3584]{1,0:T(8,128)(2,1)S(1)}, bf16[40,3584]{1,0:T(8,128)(2,1)S(1)}, u32[]{:S(2)}, u32[]{:S(2)}) collective-permute-start(bf16[40,3584]{1,0:T(8,128)(2,1)S(1)} %get-tuple-element.70), channel_id=1, source_target_pairs={{0,20},{1,21},{2,22},{3,23},{4,16},{5,17},{6,18},{7,19},{8,28},{9,... | collective-permute-start | bytes 860168 | tf_op jit(solution)/shard_map/ppermute | solution.py:32
  87.8 14.6 %collective-permute-start.20 = (bf16[40,3584]{1,0:T(8,128)(2,1)S(1)}, bf16[40,3584]{1,0:T(8,128)(2,1)S(1)}, u32[]{:S(2)}, u32[]{:S(2)}) collective-permute-start(bf16[40,3584]{1,0:T(8,128)(2,1)S(1)} %get-tuple-element.75), channel_id=1, source_target_pairs={{0,4},{1,5},{2,6},{3,7},{4,0},{5,1},{6,2},{7,3},{8,12},{9,13},{10,... | collective-permute-start | bytes 860168 | tf_op jit(solution)/shard_map/ppermute | solution.py:17
  88.3 20.5 %collective-permute-start.21 = (bf16[40,3584]{1,0:T(8,128)(2,1)S(1)}, bf16[40,3584]{1,0:T(8,128)(2,1)S(1)}, u32[]{:S(2)}, u32[]{:S(2)}) collective-permute-start(bf16[40,3584]{1,0:T(8,128)(2,1)S(1)} %get-tuple-element.78), channel_id=1, source_target_pairs={{0,16},{1,17},{2,18},{3,19},{4,20},{5,21},{6,22},{7,23},{8,24},{9,... | collective-permute-start | bytes 860168 | tf_op jit(solution)/shard_map/ppermute | solution.py:32
  88.8 18.7 %collective-permute-start.18 = (bf16[40,3584]{1,0:T(8,128)(2,1)S(1)}, bf16[40,3584]{1,0:T(8,128)(2,1)S(1)}, u32[]{:S(2)}, u32[]{:S(2)}) collective-permute-start(bf16[40,3584]{1,0:T(8,128)(2,1)S(1)} %add_convert_fusion.1), channel_id=1, source_target_pairs={{0,24},{1,25},{2,26},{3,27},{4,28},{5,29},{6,30},{7,31},{8,16},{9,... | collective-permute-start | bytes 860168 | tf_op jit(solution)/shard_map/ppermute | solution.py:32
  102.5 14.8 %collective-permute-start.22 = (bf16[40,3584]{1,0:T(8,128)(2,1)S(1)}, bf16[40,3584]{1,0:T(8,128)(2,1)S(1)}, u32[]{:S(2)}, u32[]{:S(2)}) collective-permute-start(bf16[40,3584]{1,0:T(8,128)(2,1)S(1)} %get-tuple-element.81), channel_id=1, source_target_pairs={{0,20},{1,21},{2,22},{3,23},{4,16},{5,17},{6,18},{7,19},{8,28},{9,... | collective-permute-start | bytes 860168 | tf_op jit(solution)/shard_map/ppermute | solution.py:32
  103.0 14.3 %collective-permute-start.23 = (bf16[40,3584]{1,0:T(8,128)(2,1)S(1)}, bf16[40,3584]{1,0:T(8,128)(2,1)S(1)}, u32[]{:S(2)}, u32[]{:S(2)}) collective-permute-start(bf16[40,3584]{1,0:T(8,128)(2,1)S(1)} %add_convert_fusion), channel_id=1, source_target_pairs={{0,24},{1,25},{2,26},{3,27},{4,28},{5,29},{6,30},{7,31},{8,16},{9,... | collective-permute-start | bytes 860168 | tf_op jit(solution)/shard_map/ppermute | solution.py:32
  (16 other events, 188.4 us)
